TPU v7x, 32 devices: a whole 2x2x4 slice. The times are simulated.
32 devices in a mesh: dp: 8 (over z, x), expert: 4 (over y, core).
Axes of the slice: x: 2, y: 2, z: 4, core: 2. Of those that a mesh axis runs over, the one named last changes fastest.
Arguments:
- tokens: bfloat16 [31520, 512], P(('dp', 'expert')), may hold values from -6 to 6
- cotangent: bfloat16 [31520, 512], P(('dp', 'expert')), may hold values from -6 to 6
- routes: int32 [31520, 2], P(('dp', 'expert')), may hold values from 0 to 15, all different within a row; in each aligned block of 985 rows (0 to 984, 985 to 1969, ...) at most 246 rows name the same one
- combine: float32 [31520, 2], P(('dp', 'expert')), may hold values from 0.25 to 0.75
- attn_master: float32 [512, 2048], P('dp')
- attn_first: float32 [512, 2048], P('dp')
- attn_second: float32 [512, 2048], P('dp')
- vector_master: float32 [5, 512], P(None, 'dp')
- vector_first: float32 [5, 512], P(None, 'dp')
- vector_second: float32 [5, 512], P(None, 'dp')
- expert_master: float32 [512, 2, 16, 2048], P('dp', None, 'expert'), may hold values from -0.25 to 0.25
- expert_first: float32 [512, 2, 16, 2048], P('dp', None, 'expert')
- expert_second: float32 [512, 2, 16, 2048], P('dp', None, 'expert')
Outputs:
- mixed: bfloat16 [31520, 512], P(('dp', 'expert'))
- grad_tokens: bfloat16 [31520, 512], P(('dp', 'expert'))
- attn_master_new: float32 [512, 2048], P('dp')
- attn_first_new: float32 [512, 2048], P('dp')
- attn_second_new: float32 [512, 2048], P('dp')
- vector_master_new: float32 [5, 512], P(None, 'dp')
- vector_first_new: float32 [5, 512], P(None, 'dp')
- vector_second_new: float32 [5, 512], P(None, 'dp')
- expert_master_new: float32 [512, 2, 16, 2048], P('dp', None, 'expert')
- expert_first_new: float32 [512, 2, 16, 2048], P('dp', None, 'expert')
- expert_second_new: float32 [512, 2, 16, 2048], P('dp', None, 'expert')
Inputs may be any that keep to these rules, and one draw needn't show every extreme that they name: `routes`: within the 985 rows of one device (aligned blocks) no expert is named in more than 246 slots, some expert in exactly 246; a row names 2 different experts.
All inputs are finite; a program needn't handle non-finite values.
Results may differ from a plain program's by a relative error of at most 0.015.
The roundings to bfloat16 on the way count: a program that leaves them out, or rounds other values in their place, can miss the bound.
Values may be sent and summed in bfloat16 or wider, within the bound.
A program may use at most 256 MiB of HBM per device.

v0:
```python
import jax
import jax.numpy as jnp
from jax import lax
from jax.sharding import PartitionSpec as P

D = 512
HEADS = 8
HEAD_DIM = 64
SEQ = 197
TOP = 2
STEP = 10


LN_EPS = 1e-06
BETA_ONE = 0.9
BETA_TWO = 0.999
ADAM_EPS = 1e-08


def normalize(values):
    centered = values - jnp.mean(values, axis=-1, keepdims=True)
    inverse = lax.rsqrt(jnp.mean(centered * centered, axis=-1, keepdims=True) + LN_EPS)
    return (centered * inverse, inverse)


def norm_back(grad_normed, normed, inverse):
    first_mean = jnp.mean(grad_normed, axis=-1, keepdims=True)
    second_mean = jnp.mean(grad_normed * normed, axis=-1, keepdims=True)
    return inverse * (grad_normed - first_mean - normed * second_mean)


def gelu_slope(preact):
    return (
        0.5 * (1.0 + lax.erf(preact * 0.7071067811865476))
        + preact * jnp.exp(-0.5 * preact * preact) * 0.3989422804014327
    )


def slot_places(routes, experts):
    flat_routes = routes.reshape(-1)
    onehot = (flat_routes[:, None] == jnp.arange(experts, dtype=jnp.int32)[None, :]).astype(
        jnp.int32
    )
    before = jnp.cumsum(onehot, axis=0) - onehot
    return jnp.sum(before * onehot, axis=1)


def contract_rows(left, right):
    return lax.dot_general(
        left, right, (((0,), (0,)), ((), ())), preferred_element_type=jnp.float32
    )


def contract_last(left, right):
    return lax.dot_general(
        left, right, (((1,), (1,)), ((), ())), preferred_element_type=jnp.float32
    )


def adam_update(master, first, second, gradient, step_rate, decay_rate):
    first = BETA_ONE * first + (1.0 - BETA_ONE) * gradient
    second = BETA_TWO * second + (1.0 - BETA_TWO) * gradient * gradient
    first_hat = first / (1.0 - BETA_ONE**STEP)
    second_hat = second / (1.0 - BETA_TWO**STEP)
    master = master - step_rate * (
        first_hat / (jnp.sqrt(second_hat) + ADAM_EPS) + decay_rate * master
    )
    return (master, first, second)


def body(
    tokens,
    cotangent,
    routes,
    combine,
    attn_master,
    attn_first,
    attn_second,
    vector_master,
    vector_first,
    vector_second,
    expert_master,
    expert_first,
    expert_second,
):
    group_size = lax.axis_size("expert")
    local_experts = expert_master.shape[2]
    experts = local_experts * group_size
    token_count = tokens.shape[0]
    capacity = max(2, 4 * token_count // experts)
    images = token_count // SEQ
    score_scale = HEAD_DIM ** (-0.5)
    attn_weight, vector_weight, expert_weight = (
        lax.all_gather(attn_master.astype(jnp.bfloat16), "dp", axis=0, tiled=True),
        lax.all_gather(vector_master.astype(jnp.bfloat16), "dp", axis=1, tiled=True),
        lax.all_gather(expert_master.astype(jnp.bfloat16), "dp", axis=0, tiled=True),
    )
    vectors = vector_weight.astype(jnp.float32)
    w_packed = attn_weight[:, : 3 * D]
    w_project = attn_weight[:, 3 * D :]
    inputs = tokens.astype(jnp.float32)
    normed_one, inverse_one = normalize(inputs)
    lowered_one = (normed_one * vectors[0] + vectors[1]).astype(jnp.bfloat16)
    packed = jnp.dot(lowered_one, w_packed, preferred_element_type=jnp.float32).astype(jnp.bfloat16)
    packed = packed.reshape(images, SEQ, 3, HEADS, HEAD_DIM)
    queries = packed[:, :, 0]
    keys_all = packed[:, :, 1]
    values_all = packed[:, :, 2]
    scores = (
        jnp.einsum("bqhc,bkhc->bhqk", queries, keys_all, preferred_element_type=jnp.float32)
        * score_scale
    )
    softmax_out = jax.nn.softmax(scores, axis=-1)
    softmax_low = softmax_out.astype(jnp.bfloat16)
    attended = jnp.einsum(
        "bhqk,bkhc->bqhc", softmax_low, values_all, preferred_element_type=jnp.float32
    )
    attended = attended.reshape(token_count, D).astype(jnp.bfloat16)
    middle = inputs + jnp.dot(attended, w_project, preferred_element_type=jnp.float32) + vectors[4]
    normed_two, inverse_two = normalize(middle)
    mixed_in = (normed_two * vectors[2] + vectors[3]).astype(jnp.bfloat16)
    slot_index = routes.reshape(-1) * capacity + slot_places(routes, experts)

    def dispatch(slot_rows):
        filled = jnp.zeros((experts * capacity, D), jnp.bfloat16).at[slot_index].set(slot_rows)
        return filled.reshape(group_size, local_experts, capacity, D)

    def collect(returned):
        picked = returned.reshape(experts * capacity, D)[slot_index]
        return picked.reshape(token_count, TOP, D).astype(jnp.float32)

    received = lax.all_to_all(
        dispatch(jnp.repeat(mixed_in, TOP, axis=0)),
        "expert",
        split_axis=0,
        concat_axis=0,
        tiled=True,
    )
    produced = []
    for expert_item in range(local_experts):
        arrived = received[:, expert_item].reshape(group_size * capacity, D)
        preact = jnp.dot(
            arrived, expert_weight[:, 0, expert_item], preferred_element_type=jnp.float32
        )
        hidden = jax.nn.gelu(preact, approximate=False).astype(jnp.bfloat16)
        output_rows = contract_last(hidden, expert_weight[:, 1, expert_item]).astype(jnp.bfloat16)
        produced.append(output_rows.reshape(group_size, capacity, D))
    returned = lax.all_to_all(
        jnp.stack(produced, 1), "expert", split_axis=0, concat_axis=0, tiled=True
    )
    mixed = middle + jnp.sum(combine[:, :, None] * collect(returned), axis=1)
    grad_out = cotangent.astype(jnp.float32)
    slot_grads = (
        (combine[:, :, None] * grad_out[:, None, :])
        .reshape(token_count * TOP, D)
        .astype(jnp.bfloat16)
    )
    grads_in = lax.all_to_all(
        dispatch(slot_grads), "expert", split_axis=0, concat_axis=0, tiled=True
    )
    sent_back = []
    shards = []
    for expert_item in range(local_experts):
        arrived = received[:, expert_item].reshape(group_size * capacity, D)
        arrived_grad = grads_in[:, expert_item].reshape(group_size * capacity, D)
        w_in = expert_weight[:, 0, expert_item]
        w_out = expert_weight[:, 1, expert_item]
        preact = jnp.dot(arrived, w_in, preferred_element_type=jnp.float32)
        hidden = jax.nn.gelu(preact, approximate=False).astype(jnp.bfloat16)
        grad_hidden = jnp.dot(arrived_grad, w_out, preferred_element_type=jnp.float32)
        grad_pre = (grad_hidden * gelu_slope(preact)).astype(jnp.bfloat16)
        sent_back.append(
            contract_last(grad_pre, w_in).astype(jnp.bfloat16).reshape(group_size, capacity, D)
        )
        full_grad = jnp.stack(
            [contract_rows(arrived, grad_pre), contract_rows(arrived_grad, hidden)], 1
        )
        shards.append(lax.psum_scatter(full_grad, "dp", scatter_dimension=0, tiled=True))
    expert_grad = jnp.stack(shards, 2)
    returned_grads = lax.all_to_all(
        jnp.stack(sent_back, 1), "expert", split_axis=0, concat_axis=0, tiled=True
    )
    grad_mixed = jnp.sum(collect(returned_grads), axis=1)
    grad_gain_two = jnp.sum(grad_mixed * normed_two, axis=0)
    grad_shift_two = jnp.sum(grad_mixed, axis=0)
    grad_middle = grad_out + norm_back(grad_mixed * vectors[2], normed_two, inverse_two)
    middle_low = grad_middle.astype(jnp.bfloat16)
    grad_project = contract_rows(attended, middle_low)
    grad_attended = (
        contract_last(middle_low, w_project)
        .astype(jnp.bfloat16)
        .reshape(images, SEQ, HEADS, HEAD_DIM)
    )
    grad_soft = jnp.einsum(
        "bqhc,bkhc->bhqk", grad_attended, values_all, preferred_element_type=jnp.float32
    )
    grad_scores = (
        softmax_out * (grad_soft - jnp.sum(softmax_out * grad_soft, axis=-1, keepdims=True))
    ).astype(jnp.bfloat16)
    grad_queries = (
        jnp.einsum("bhqk,bkhc->bqhc", grad_scores, keys_all, preferred_element_type=jnp.float32)
        * score_scale
    )
    grad_keys = (
        jnp.einsum("bhqk,bqhc->bkhc", grad_scores, queries, preferred_element_type=jnp.float32)
        * score_scale
    )
    grad_values = jnp.einsum(
        "bhqk,bqhc->bkhc", softmax_low, grad_attended, preferred_element_type=jnp.float32
    )
    grad_packed = (
        jnp.stack([grad_queries, grad_keys, grad_values], 2)
        .reshape(token_count, 3 * D)
        .astype(jnp.bfloat16)
    )
    grad_weight_packed = contract_rows(lowered_one, grad_packed)
    grad_lowered = contract_last(grad_packed, w_packed)
    grad_gain_one = jnp.sum(grad_lowered * normed_one, axis=0)
    grad_shift_one = jnp.sum(grad_lowered, axis=0)
    grad_tokens = grad_middle + norm_back(grad_lowered * vectors[0], normed_one, inverse_one)
    attn_grad = jnp.concatenate([grad_weight_packed, grad_project], axis=1)
    vector_grad = jnp.stack(
        [
            grad_gain_one,
            grad_shift_one,
            grad_gain_two,
            grad_shift_two,
            jnp.sum(grad_middle, axis=0),
        ],
        0,
    )
    attn_whole, vector_whole = lax.psum((attn_grad, vector_grad), "expert")
    attn_part, vector_part = (
        lax.psum_scatter(attn_whole, "dp", scatter_dimension=0, tiled=True),
        lax.psum_scatter(vector_whole, "dp", scatter_dimension=1, tiled=True),
    )
    attn_new = adam_update(attn_master, attn_first, attn_second, attn_part, 0.03, 0.1)
    vector_new = adam_update(vector_master, vector_first, vector_second, vector_part, 0.2, 0.0)
    expert_new = adam_update(expert_master, expert_first, expert_second, expert_grad, 0.02, 0.1)
    return (
        mixed.astype(jnp.bfloat16),
        grad_tokens.astype(jnp.bfloat16),
        attn_new[0],
        attn_new[1],
        attn_new[2],
        vector_new[0],
        vector_new[1],
        vector_new[2],
        expert_new[0],
        expert_new[1],
        expert_new[2],
    )


def solution(mesh):
    return jax.shard_map(
        body,
        mesh=mesh,
        in_specs=(
            P(("dp", "expert"), None),
            P(("dp", "expert"), None),
            P(("dp", "expert"), None),
            P(("dp", "expert"), None),
            P("dp", None),
            P("dp", None),
            P("dp", None),
            P(None, "dp"),
            P(None, "dp"),
            P(None, "dp"),
            P("dp", None, "expert", None),
            P("dp", None, "expert", None),
            P("dp", None, "expert", None),
        ),
        out_specs=(
            P(("dp", "expert"), None),
            P(("dp", "expert"), None),
            P("dp", None),
            P("dp", None),
            P("dp", None),
            P(None, "dp"),
            P(None, "dp"),
            P(None, "dp"),
            P("dp", None, "expert", None),
            P("dp", None, "expert", None),
            P("dp", None, "expert", None),
        ),
        check_vma=False,
    )
```

profile of v0, /device:TPU:0, one launch (start us, length us, event | category | flops | bytes accessed | tf_op | source)
XLA Modules:
  0.0 1493.0 jit_solution(9094180110123981603)
XLA Ops:
  30.8 19.0 %scatter_custom_fusion.1 = bf16[3936,512]{1,0:T(8,128)(2,1)} fusion(s32[1970]{0:T(1024)S(1)} %bitcast.206, f32[1970,512]{1,0:T(8,128)} %mul.435, f32[1970]{0:T(1024)S(1)} %mul.432, bf16[]{:T(256)} %constant.56.clone.1), kind=kCustom, calls=%fused_computation.182 | custom fusion | flops 2017280 | bytes 8073218 | tf_op jit(solution)/shard_map/scatter | solution.py:125
  66.0 28.3 %all-gather = bf16[8,64,5]{1,2,0:T(8,128)(2,1)S(1)} all-gather(bf16[1,64,5]{1,2,0:T(8,128)(2,1)S(1)} %convert_bitcast_fusion.1), channel_id=1, replica_groups=mesh['dp'=8,'expert'=4] {'dp'}, dimensions={0}, use_global_device_ids=true | all-gather | bytes 5760 | tf_op jit(solution)/shard_map/all_gather | solution.py:95
  152.3 22.0 %scatter_custom_fusion = bf16[3936,512]{1,0:T(8,128)(2,1)} fusion(s32[1970]{0:T(1024)S(1)} %bitcast.207, bf16[1970,512]{1,0:T(8,128)(2,1)} %reshape.174, bf16[]{:T(256)} %constant.56.clone.1), kind=kCustom, calls=%fused_computation.193 | custom fusion | bytes 4030976 | tf_op jit(solution)/shard_map/scatter | solution.py:125
  190.4 23.1 %slice_reduce_fusion.3 = (bf16[4,246,512]{2,1,0:T(8,128)(2,1)}, bf16[4,246,512]{2,1,0:T(8,128)(2,1)S(1)}, bf16[4,246,512]{2,1,0:T(8,128)(2,1)S(1)}, bf16[4,246,512]{2,1,0:T(8,128)(2,1)S(1)}) fusion(bf16[4,4,246,512]{3,1,2,0:T(4,128)(2,1)} %all-to-all-done.2), kind=kLoop, calls=%fused_computation.187 | loop fusion | bytes 8060928 | tf_op jit(solution)/shard_map/slice | solution.py:165
  219.7 17.2 %all-to-all-done = bf16[4,4,246,512]{3,1,2,0:T(4,128)(2,1)} async-done(((bf16[4,4,246,512]{3,1,2,0:T(4,128)(2,1)}), bf16[4,4,246,512]{3,1,2,0:T(4,128)(2,1)}, u32[]{:S(2)}, u32[]{:S(2)}) %all-to-all-start) | async-done | bytes 4030496 | tf_op jit(solution)/shard_map/all_to_all | solution.py:132
  236.9 23.8 %slice_reduce_fusion.7 = (bf16[4,246,512]{2,1,0:T(8,128)(2,1)S(1)}, bf16[4,246,512]{2,1,0:T(8,128)(2,1)}, bf16[4,246,512]{2,1,0:T(8,128)(2,1)S(1)}, bf16[4,246,512]{2,1,0:T(8,128)(2,1)}) fusion(bf16[4,4,246,512]{3,1,2,0:T(4,128)(2,1)} %all-to-all-done), kind=kLoop, calls=%fused_computation.191 | loop fusion | bytes 8060928 | tf_op jit(solution)/shard_map/slice | solution.py:141
  265.6 25.7 %all-gather.6.cloned.1.call-done = bf16[512,2,4,2048]{3,0,2,1:T(8,128)(2,1)} async-done(((bf16[64,2,4,2048]{3,0,2,1:T(8,128)(2,1)}), bf16[512,2,4,2048]{3,0,2,1:T(8,128)(2,1)}) %all-gather.6.cloned.1.call-update) | async-done | bytes 16777232 | tf_op jit(solution)/shard_map/all_gather | solution.py:96
  291.3 21.4 %fusion.6 = (bf16[984,2048]{1,0:T(8,128)(2,1)S(1)}, f32[984,2048]{1,0:T(8,128)}) fusion(bf16[984,512]{1,0:T(8,128)(2,1)S(1)} %reshape_squeeze.29, bf16[512,2,4,2048]{3,0,2,1:T(8,128)(2,1)} %all-gather.6.cloned.1.call-done), kind=kOutput, calls=%fused_computation.25 | convolution fusion | flops 2194587648 | bytes 15196160 | tf_op jit(solution)/shard_map/dot_general | solution.py:142
  319.9 21.0 %fusion.9 = (bf16[984,2048]{1,0:T(8,128)(2,1)S(1)}, f32[984,2048]{1,0:T(8,128)}) fusion(bf16[984,512]{1,0:T(8,128)(2,1)S(1)} %reshape_squeeze.30, bf16[512,2,4,2048]{3,0,2,1:T(8,128)(2,1)} %all-gather.6.cloned.1.call-done), kind=kOutput, calls=%fused_computation.28 | convolution fusion | flops 2194587648 | bytes 15196160 | tf_op jit(solution)/shard_map/dot_general | solution.py:142
  347.1 21.2 %fusion.12 = (bf16[984,2048]{1,0:T(8,128)(2,1)S(1)}, f32[984,2048]{1,0:T(8,128)}) fusion(bf16[984,512]{1,0:T(8,128)(2,1)S(1)} %reshape_squeeze.31, bf16[512,2,4,2048]{3,0,2,1:T(8,128)(2,1)} %all-gather.6.cloned.1.call-done), kind=kOutput, calls=%fused_computation.31 | convolution fusion | flops 2194587648 | bytes 15196160 | tf_op jit(solution)/shard_map/dot_general | solution.py:142
  376.7 21.4 %fusion.3 = (bf16[984,2048]{1,0:T(8,128)(2,1)S(1)}, f32[984,2048]{1,0:T(8,128)}) fusion(bf16[984,512]{1,0:T(8,128)(2,1)S(1)} %copy-done.24, bf16[512,2,4,2048]{3,0,2,1:T(8,128)(2,1)} %all-gather.6.cloned.1.call-done), kind=kOutput, calls=%fused_computation.22 | convolution fusion | flops 2194587648 | bytes 15196160 | tf_op jit(solution)/shard_map/dot_general | solution.py:142
  496.7 36.3 %all-to-all-done.3 = bf16[4,4,246,512]{3,1,2,0:T(4,128)(2,1)} async-done(((bf16[4,4,246,512]{3,1,2,0:T(4,128)(2,1)}), bf16[4,4,246,512]{3,1,2,0:T(4,128)(2,1)}, u32[]{:S(2)}, u32[]{:S(2)}) %all-to-all-start.3) | async-done | bytes 4030496 | tf_op jit(solution)/shard_map/all_to_all | solution.py:180
  542.9 11.9 gather_fusion
  554.8 11.9 gather_fusion.1
  589.5 22.4 %multiply_reduce_fusion.2 = f32[985,512]{1,0:T(8,128)S(1)} fusion(f32[985,2,512]{2,1,0:T(2,128)} %reshape.152, f32[985,2]{1,0:T(8,128)S(1)} %copy-done.38), kind=kLoop, calls=%fused_computation.132 | loop fusion | flops 1512960 | bytes 6059720 | tf_op jit(solution)/shard_map/reduce_sum | solution.py:151
  640.0 9.2 copy.124
  683.0 66.8 %reduce-scatter.17.cloned.1.call-done = f32[64,2048]{1,0:T(8,128)} async-done(((f32[512,2048]{1,0:T(8,128)}), f32[64,2048]{1,0:T(8,128)}) %reduce-scatter.17.cloned.1.call-update) | async-done | bytes 524304 | tf_op jit(solution)/shard_map/reduce_scatter | solution.py:234
  799.1 15.8 %reduce-scatter.19.cloned.1.call-done = f32[64,5]{1,0:T(8,128)} async-done(((f32[512,5]{1,0:T(8,128)}), f32[64,5]{1,0:T(8,128)}) %reduce-scatter.19.cloned.1.call-update) | async-done | bytes 1296
  822.5 27.0 %all-reduce.3.cloned.1.call-done = f32[64,2048]{1,0:T(8,128)} async-done(((f32[64,2048]{1,0:T(8,128)}), f32[64,2048]{1,0:T(8,128)}) %all-reduce.3.cloned.1.call-update) | async-done | bytes 524304 | tf_op jit(solution)/shard_map/psum | solution.py:232
  852.3 150.1 %reduce-scatter.11.cloned.1.call-done = f32[64,2,2048]{2,0,1:T(8,128)} async-done(((f32[512,2,2048]{2,0,1:T(8,128)}), f32[64,2,2048]{2,0,1:T(8,128)}) %reduce-scatter.11.cloned.1.call-update) | async-done | bytes 1048592 | tf_op jit(solution)/shard_map/reduce_scatter | solution.py:178
  1002.4 151.7 %reduce-scatter.13.cloned.1.call-done = f32[64,2,2048]{2,0,1:T(8,128)} async-done(((f32[512,2,2048]{2,0,1:T(8,128)}), f32[64,2,2048]{2,0,1:T(8,128)}) %reduce-scatter.13.cloned.1.call-update) | async-done | bytes 1048592 | tf_op jit(solution)/shard_map/reduce_scatter | solution.py:178
  1154.1 152.1 %reduce-scatter.15.cloned.1.call-done = f32[64,2,2048]{2,0,1:T(8,128)} async-done(((f32[512,2,2048]{2,0,1:T(8,128)}), f32[64,2,2048]{2,0,1:T(8,128)}) %reduce-scatter.15.cloned.1.call-update) | async-done | bytes 1048592 | tf_op jit(solution)/shard_map/reduce_scatter | solution.py:178
  1306.2 151.7 %reduce-scatter.9.cloned.1.call-done = f32[64,2,2048]{2,0,1:T(8,128)} async-done(((f32[512,2,2048]{2,0,1:T(8,128)}), f32[64,2,2048]{2,0,1:T(8,128)}) %reduce-scatter.9.cloned.1.call-update) | async-done | bytes 1048592 | tf_op jit(solution)/shard_map/reduce_scatter | solution.py:178
  1457.9 14.2 multiply_subtract_fusion
  (310 shorter events, 412.5 us)
Async XLA Ops:
  7.2 88.0 %all-gather.4.cloned.1.call-start = ((), (), s32[]{:S(2)}) async-start(), calls=%async_computation.10 | async-start | bytes 2359296 | tf_op jit(solution)/shard_map/all_gather | solution.py:94
  9.1 282.2 %all-gather.6.cloned.1.call-start = ((), (), s32[]{:S(2)}) async-start(), calls=%async_computation.11 | async-start | bytes 18874368 | tf_op jit(solution)/shard_map/all_gather | solution.py:96
  15.9 33.9 %copy-start.37 = (f32[985,2]{1,0:T(8,128)}, f32[985,2]{1,0:T(8,128)S(1)}, u32[]{:S(2)}) copy-start(f32[985,2]{1,0:T(8,128)S(1)} %copy.108) | copy-start | bytes 23644
  30.8 121.5 %copy-start.62 = (s32[1970,1]{0,1:T(1,128)}, s32[1970,1]{0,1:T(1,128)S(1)}, u32[]{:S(2)}) copy-start(s32[1970,1]{0,1:T(1,128)S(1)} %compare_select_fusion) | copy-start | bytes 23644
  54.8 39.5 %copy-start.8 = (bf16[985,512]{1,0:T(8,128)(2,1)S(1)}, bf16[985,512]{1,0:T(8,128)(2,1)}, u32[]{:S(2)}) copy-start(bf16[985,512]{1,0:T(8,128)(2,1)} %param.13) | copy-start | bytes 3025924
  61.1 124.4 %all-to-all-start.2 = ((bf16[4,4,246,512]{3,1,2,0:T(4,128)(2,1)}), bf16[4,4,246,512]{3,1,2,0:T(4,128)(2,1)}, u32[]{:S(2)}, u32[]{:S(2)}) async-start(bf16[4,4,246,512]{3,1,2,0:T(4,128)(2,1)} %copy.116), calls=%async_computation.2 | async-start | bytes 8060928 | tf_op jit(solution)/shard_map/all_to_all | solution.py:158
  95.2 52.7 %copy-start.60 = (f32[1,512]{1,0:T(1,128)}, f32[1,512]{1,0:T(1,128)S(1)}, u32[]{:S(2)}) copy-start(f32[1,512]{1,0:T(1,128)S(1)} %get-tuple-element.85) | copy-start | bytes 6148
  185.5 51.4 %all-to-all-start = ((bf16[4,4,246,512]{3,1,2,0:T(4,128)(2,1)}), bf16[4,4,246,512]{3,1,2,0:T(4,128)(2,1)}, u32[]{:S(2)}, u32[]{:S(2)}) async-start(bf16[4,4,246,512]{3,1,2,0:T(4,128)(2,1)} %copy.111), calls=%async_computation | async-start | bytes 8060928 | tf_op jit(solution)/shard_map/all_to_all | solution.py:132
  263.4 83.7 %copy-start.30 = (bf16[984,512]{1,0:T(8,128)(2,1)}, bf16[984,512]{1,0:T(8,128)(2,1)S(1)}, u32[]{:S(2)}) copy-start(bf16[984,512]{1,0:T(8,128)(2,1)S(1)} %reshape_squeeze.31) | copy-start | bytes 3022852
  263.7 56.2 %copy-start.32 = (bf16[984,512]{1,0:T(8,128)(2,1)}, bf16[984,512]{1,0:T(8,128)(2,1)S(1)}, u32[]{:S(2)}) copy-start(bf16[984,512]{1,0:T(8,128)(2,1)S(1)} %reshape_squeeze.30) | copy-start | bytes 3022852
  265.6 47.1 %copy-start.36 = (bf16[984,512]{1,0:T(8,128)(2,1)}, bf16[984,512]{1,0:T(8,128)(2,1)S(1)}, u32[]{:S(2)}) copy-start(bf16[984,512]{1,0:T(8,128)(2,1)S(1)} %reshape_squeeze.29) | copy-start | bytes 3022852
  414.2 67.6 %all-to-all-start.1 = ((bf16[4,4,246,512]{3,1,2,0:T(4,128)(2,1)}), bf16[4,4,246,512]{3,1,2,0:T(4,128)(2,1)}, u32[]{:S(2)}, u32[]{:S(2)}) async-start(bf16[4,4,246,512]{3,1,2,0:T(4,128)(2,1)} %copy.113), calls=%async_computation.1 | async-start | bytes 8060928 | tf_op jit(solution)/shard_map/all_to_all | solution.py:148
  481.7 51.3 %all-to-all-start.3 = ((bf16[4,4,246,512]{3,1,2,0:T(4,128)(2,1)}), bf16[4,4,246,512]{3,1,2,0:T(4,128)(2,1)}, u32[]{:S(2)}, u32[]{:S(2)}) async-start(bf16[4,4,246,512]{3,1,2,0:T(4,128)(2,1)} %copy.117), calls=%async_computation.3 | async-start | bytes 8060928 | tf_op jit(solution)/shard_map/all_to_all | solution.py:180
  486.5 263.3 %reduce-scatter.17.cloned.1.call-start = ((), (), s32[]{:S(2)}) async-start(), calls=%async_computation.16 | async-start | bytes 4718592 | tf_op jit(solution)/shard_map/reduce_scatter | solution.py:234
  580.5 32.1 %copy-start.41 = (bf16[985,512]{1,0:T(8,128)(2,1)S(1)}, bf16[985,512]{1,0:T(8,128)(2,1)}, u32[]{:S(2)}) copy-start(bf16[985,512]{1,0:T(8,128)(2,1)} %param.14) | copy-start | bytes 3025924
  664.5 150.4 %reduce-scatter.19.cloned.1.call-start = ((), (), s32[]{:S(2)}) async-start(), calls=%async_computation.18 | async-start | bytes 294912
  676.2 173.2 %all-reduce.3.cloned.1.call-start = ((), (), s32[]{:S(2)}) async-start(), calls=%async_computation.17 | async-start | bytes 1048576 | tf_op jit(solution)/shard_map/psum | solution.py:232
  749.9 252.5 %reduce-scatter.11.cloned.1.call-start = ((), (), s32[]{:S(2)}) async-start(), calls=%async_computation.13 | async-start | bytes 9437184 | tf_op jit(solution)/shard_map/reduce_scatter | solution.py:178
  757.7 396.3 %reduce-scatter.13.cloned.1.call-start = ((), (), s32[]{:S(2)}) async-start(), calls=%async_computation.14 | async-start | bytes 9437184 | tf_op jit(solution)/shard_map/reduce_scatter | solution.py:178
  770.1 536.1 %reduce-scatter.15.cloned.1.call-start = ((), (), s32[]{:S(2)}) async-start(), calls=%async_computation.15 | async-start | bytes 9437184 | tf_op jit(solution)/shard_map/reduce_scatter | solution.py:178
  782.4 675.5 %reduce-scatter.9.cloned.1.call-start = ((), (), s32[]{:S(2)}) async-start(), calls=%async_computation.12 | async-start | bytes 9437184 | tf_op jit(solution)/shard_map/reduce_scatter | solution.py:178
  794.7 27.2 %copy-start.65 = (f32[5,64]{1,0:T(8,128)S(1)}, f32[5,64]{1,0:T(8,128)}, u32[]{:S(2)}) copy-start(f32[5,64]{1,0:T(8,128)} %param.20) | copy-start | bytes 3844
  794.7 27.2 %copy-start.69 = (f32[5,64]{1,0:T(8,128)S(1)}, f32[5,64]{1,0:T(8,128)}, u32[]{:S(2)}) copy-start(f32[5,64]{1,0:T(8,128)} %param.21) | copy-start | bytes 3844
  794.7 27.2 %copy-start.70 = (f32[5,64]{1,0:T(8,128)S(1)}, f32[5,64]{1,0:T(8,128)}, u32[]{:S(2)}) copy-start(f32[5,64]{1,0:T(8,128)} %param.22) | copy-start | bytes 3844
  (64 other events, 457.8 us)
Sparse Core Ops, SparseCore 0:
  10.7 52.0 all-gather.3
  65.0 226.3 all-gather.5
  664.6 85.1 reduce-scatter.16
  754.0 60.9 reduce-scatter.18
  817.2 32.1 all-reduce.2
  853.4 148.9 reduce-scatter.10
  1006.0 148.0 reduce-scatter.12
  1158.1 148.0 reduce-scatter.14
  1309.8 148.0 reduce-scatter.8
where the time goes:
time: 1500 us; the launch traced here: 1490 us
  waiting for transfers between devices  795 us (53%)
  local copies, waits for them, and re-layouts  285 us (19%)
  matrix products  221 us (15%)
  other arithmetic  123 us (8%)
  blocking collectives  34.4 us (2%)
  starting transfers between devices  20.2 us (1%)
  between operations  15.3 us (1%)
    reduce_scatter x4, waiting for transfers between devices, body(): lax.psum_scatter(full_grad, 'dp', scatter_dimension=0, tiled=True)  606 us
    dot_general x4, matrix products, body(): jnp.dot(arrived, expert_weight[:, 0, expert_item], preferred_element_type...  85 us
    reduce_scatter x1, waiting for transfers between devices, body(): lax.psum_scatter(attn_whole, 'dp', scatter_dimension=0, tiled=True)  66.8 us
    unnamed x163, local copies, waits for them, and re-layouts  51.9 us
    dot_general x10, matrix products, contract_last(): lax.dot_general(left, right, (((1,), (1,)), ((), ())), preferred_element_...  43 us
    dot_general x10, matrix products, contract_rows(): lax.dot_general(left, right, (((0,), (0,)), ((), ())), preferred_element_...  40.8 us
    all_to_all x1, waiting for transfers between devices, body(): lax.all_to_all(jnp.stack(sent_back, 1), 'expert', split_axis=0, concat_ax...  36.3 us
  transfers between devices with their start and end apart: 13, of which 10 were waited for; matrix products, arithmetic and copies ran while one was open for 22% of the time, Pallas kernels for 0%

commit v1 on v0

--- a/solution.py
+++ b/solution.py
@@ -1,6 +1,10 @@
+import functools
+
 import jax
 import jax.numpy as jnp
 from jax import lax
+from jax.experimental import pallas as pl
+from jax.experimental.pallas import tpu as pltpu
 from jax.sharding import PartitionSpec as P
 
 D = 512
@@ -9,12 +13,35 @@
 SEQ = 197
 TOP = 2
 STEP = 10
-
+PAD = 256
+SENT = 208
+CORES = 2
+COLUMNS = 2
 
 LN_EPS = 1e-06
 BETA_ONE = 0.9
 BETA_TWO = 0.999
 ADAM_EPS = 1e-08
+MESH = pl.DeviceIdType.MESH
+F32 = jnp.float32
+BF16 = jnp.bfloat16
+VMEM_LIMIT = 60 * 1024 * 1024
+
+
+def dot(left, right):
+    return jnp.dot(left, right, preferred_element_type=F32)
+
+
+def contract_rows(left, right):
+    return lax.dot_general(
+        left, right, (((0,), (0,)), ((), ())), preferred_element_type=F32
+    )
+
+
+def contract_last(left, right):
+    return lax.dot_general(
+        left, right, (((1,), (1,)), ((), ())), preferred_element_type=F32
+    )
 
 
 def normalize(values):
@@ -29,32 +56,668 @@
     return inverse * (grad_normed - first_mean - normed * second_mean)
 
 
-def gelu_slope(preact):
-    return (
-        0.5 * (1.0 + lax.erf(preact * 0.7071067811865476))
-        + preact * jnp.exp(-0.5 * preact * preact) * 0.3989422804014327
-    )
-
-
-def slot_places(routes, experts):
-    flat_routes = routes.reshape(-1)
-    onehot = (flat_routes[:, None] == jnp.arange(experts, dtype=jnp.int32)[None, :]).astype(
-        jnp.int32
-    )
-    before = jnp.cumsum(onehot, axis=0) - onehot
-    return jnp.sum(before * onehot, axis=1)
-
-
-def contract_rows(left, right):
-    return lax.dot_general(
-        left, right, (((0,), (0,)), ((), ())), preferred_element_type=jnp.float32
-    )
-
-
-def contract_last(left, right):
-    return lax.dot_general(
-        left, right, (((1,), (1,)), ((), ())), preferred_element_type=jnp.float32
-    )
+def remote(source, target, send_sem, recv_sem, device):
+    return pltpu.make_async_remote_copy(
+        src_ref=source,
+        dst_ref=target,
+        send_sem=send_sem,
+        recv_sem=recv_sem,
+        device_id=device,
+        device_id_type=MESH,
+    )
+
+
+def greet(devices):
+    barrier = pltpu.get_barrier_semaphore()
+    for device in devices:
+        pl.semaphore_signal(barrier, inc=1, device_id=device, device_id_type=MESH)
+    pl.semaphore_wait(barrier, len(devices))
+
+
+def softmax_rows(query, key_rows, half, lane):
+    own = jnp.where(lane // HEAD_DIM == half, query, jnp.zeros_like(query))
+    scores = contract_last(own, key_rows) * HEAD_DIM ** (-0.5)
+    column = lax.broadcasted_iota(jnp.int32, scores.shape, 1)
+    scores = jnp.where(column < SEQ, scores, -1e30)
+    powers = jnp.exp(scores - jnp.max(scores, axis=-1, keepdims=True))
+    return powers * (1.0 / jnp.sum(powers, axis=-1, keepdims=True))
+
+
+def front_kernel(
+    shards, lines, tok, cot, route, comb, attn, vec, expw,
+    u_all, g_all, place_out, comb_out, wfull, attnw, vec_out, middle, qkv, att,
+    route_all, comb_all, vslots, chosen,
+    attn_send, attn_recv, vec_send, vec_recv, pass_sem, table_send, table_recv,
+    g_sem, u_send, u_recv, own_sem, up_send, up_recv, down_send, down_recv, x_send, x_recv,
+):
+    dp, me = lax.axis_index("dp"), lax.axis_index("expert")
+    z, x = dp // COLUMNS, dp % COLUMNS
+    y, core = me // CORES, me % CORES
+    images = tok.shape[0]
+    local = expw.shape[0]
+    rows = attn.shape[0]
+    half = rows // CORES
+    mate = (dp, y * CORES + 1 - core)
+    over = (dp, (1 - y) * CORES + core)
+    corner = (dp, (1 - y) * CORES + 1 - core)
+    above = (jnp.minimum(z + 1, lines - 1) * COLUMNS + x, me)
+    below = (jnp.maximum(z - 1, 0) * COLUMNS + x, me)
+    beside = (z * COLUMNS + 1 - x, me)
+    peers = [(lax.rem(dp + k, shards), me) for k in range(1, shards)]
+    sources = [lax.rem(dp + shards - k, shards) for k in range(1, shards)]
+    greet(peers + [mate, over, corner])
+    mine = pl.ds(pl.multiple_of(core * half, half), half)
+
+    for k, peer in enumerate(peers):
+        remote(attn.at[mine], attnw.at[dp, mine], attn_send.at[k], attn_recv.at[dp], peer).start()
+        remote(vec, vslots.at[dp], vec_send.at[k], vec_recv.at[dp], peer).start()
+    tables = []
+    for k, partner in enumerate((mate, over, corner)):
+        tables.append(remote(route, route_all.at[me], table_send.at[k, 0], table_recv.at[me, 0], partner))
+        tables.append(remote(comb, comb_all.at[me], table_send.at[k, 1], table_recv.at[me, 1], partner))
+    for copy in tables:
+        copy.start()
+    g_own = cot.at[:, pl.ds(0, SENT)]
+    g_mate = remote(g_own, g_all.at[me, :, pl.ds(0, SENT)], g_sem.at[0], g_sem.at[1], mate)
+    g_over = remote(g_own, g_all.at[me, :, pl.ds(0, SENT)], g_sem.at[2], g_sem.at[3], over)
+    g_mate.start()
+    g_over.start()
+
+    def up(e, hop, source):
+        shard = (z - hop) * COLUMNS + x
+        return remote(source, wfull.at[e, :, shard], up_send.at[e, hop], up_recv.at[e, hop], above)
+
+    def down(e, hop, source):
+        shard = (z + hop) * COLUMNS + x
+        return remote(source, wfull.at[e, :, shard], down_send.at[e, hop], down_recv.at[e, hop], below)
+
+    def across(e, place, source):
+        shard = place * COLUMNS + x
+        return remote(source, wfull.at[e, :, shard], x_send.at[e, place], x_recv.at[e, place], beside)
+
+    def start_own(e):
+        @pl.when(z < lines - 1)
+        def _():
+            up(e, 0, expw.at[e]).start()
+
+        @pl.when(z > 0)
+        def _():
+            down(e, 0, expw.at[e]).start()
+
+        across(e, z, expw.at[e]).start()
+
+    def hand_on(step):
+        e, hop = step // (lines - 1), step % (lines - 1)
+
+        @pl.when(jnp.logical_and(hop == 0, e + 2 < local))
+        def _():
+            start_own(e + 2)
+
+        from_below = jnp.maximum(z - 1 - hop, 0)
+        from_above = jnp.minimum(z + 1 + hop, lines - 1)
+
+        @pl.when(z - 1 - hop >= 0)
+        def _():
+            held = wfull.at[e, :, from_below * COLUMNS + x]
+            remote(held, held, up_send.at[e, hop], up_recv.at[e, hop], above).wait_recv()
+
+            @pl.when(z < lines - 1)
+            def _():
+                remote(held, held, up_send.at[e, hop + 1], up_recv.at[e, hop + 1], above).start()
+
+            remote(held, held, x_send.at[e, from_below], x_recv.at[e, from_below], beside).start()
+
+        @pl.when(z + 1 + hop <= lines - 1)
+        def _():
+            held = wfull.at[e, :, from_above * COLUMNS + x]
+            remote(held, held, down_send.at[e, hop], down_recv.at[e, hop], below).wait_recv()
+
+            @pl.when(z > 0)
+            def _():
+                remote(held, held, down_send.at[e, hop + 1], down_recv.at[e, hop + 1], below).start()
+
+            remote(held, held, x_send.at[e, from_above], x_recv.at[e, from_above], beside).start()
+
+    start_own(0)
+    start_own(1)
+    own_copy = pltpu.make_async_copy(expw, wfull.at[:, :, dp], own_sem)
+    own_copy.start()
+
+    attnw[dp, mine] = attn[mine]
+    vslots[dp] = vec[...]
+    route_all[me] = route[...]
+    comb_all[me] = comb[...]
+    g_all[me] = cot[...]
+    empty = jnp.zeros((images, PAD - SENT, D), BF16)
+    for k in range(1, 4):
+        other = lax.rem(me + k, 4)
+        u_all[other, :, SENT:, :] = empty
+        g_all[other, :, SENT:, :] = empty
+
+    for k, (peer, source) in enumerate(zip(peers, sources)):
+        remote(attn.at[mine], attnw.at[source, mine], attn_send.at[k], attn_recv.at[source], peer).wait()
+        remote(vec, vslots.at[source], vec_send.at[k], vec_recv.at[source], peer).wait()
+    halves = attnw.at[:, mine]
+    to_mate = remote(halves, halves, pass_sem.at[0], pass_sem.at[1], mate)
+    to_mate.start()
+
+    lane = lax.broadcasted_iota(jnp.int32, (128, D), 1)
+    entry = lax.broadcasted_iota(jnp.int32, (128, D), 0)
+    width = D // shards
+    vectors = jnp.zeros((8, D), F32)
+    for d in range(shards):
+        spread = jnp.where(jnp.logical_and(entry < width, lane == entry + d * width), 1.0, 0.0)
+        vectors = vectors + dot(vslots[d].astype(BF16), spread.astype(BF16))
+    vec_out[...] = vectors
+    gain_one, shift_one = vectors[0:1], vectors[1:2]
+    gain_two, shift_two, shift_out = vectors[2:3], vectors[3:4], vectors[4:5]
+
+    others = remote(attnw.at[:, pl.ds(pl.multiple_of((1 - core) * half, half), half)],
+                    attnw.at[:, pl.ds(pl.multiple_of((1 - core) * half, half), half)],
+                    pass_sem.at[0], pass_sem.at[1], mate)
+    others.wait_recv()
+    pair_lane = lax.broadcasted_iota(jnp.int32, (PAD, 2 * HEAD_DIM), 1)
+
+    def one_image(i, carry):
+        inputs = tok[i].astype(F32)
+        normed, _ = normalize(inputs)
+        lowered = (normed * gain_one + shift_one).astype(BF16)
+        for part in range(3):
+            columns = pl.ds(part * D, D)
+            qkv[i, :, columns] = dot(lowered, attnw[:, :, columns].reshape(D, D)).astype(BF16)
+        for pair in range(HEADS // 2):
+            offset = pair * 2 * HEAD_DIM
+            query = qkv[i, :, offset : offset + 128]
+            key_rows = qkv[i, :, D + offset : D + offset + 128]
+            value = qkv[i, :, 2 * D + offset : 2 * D + offset + 128]
+            results = []
+            for which in range(2):
+                probs = softmax_rows(query, key_rows, which, pair_lane)
+                results.append(dot(probs.astype(BF16), value))
+            joined = jnp.where(pair_lane < HEAD_DIM, results[0], results[1])
+            att[i, :, offset : offset + 128] = joined.astype(BF16)
+        mid = inputs + dot(att[i], attnw[:, :, 3 * D :].reshape(D, D)) + shift_out
+        middle[i] = mid
+        normed_two, _ = normalize(mid)
+        u_all[me, i] = (normed_two * gain_two + shift_two).astype(BF16)
+        part = u_all.at[me, i, pl.ds(0, SENT)]
+        remote(part, part, u_send.at[i, 0], u_recv.at[i, 0], over).start()
+        remote(part, part, u_send.at[i, 1], u_recv.at[i, 1], mate).start()
+
+        @pl.when(i % 2 == 1)
+        def _():
+            hand_on(i // 2)
+
+        return carry
+
+    lax.fori_loop(0, images, one_image, 0)
+
+    g_over_part = g_all.at[(1 - y) * CORES + core, :, pl.ds(0, SENT)]
+    remote(g_over_part, g_over_part, g_sem.at[2], g_sem.at[3], over).wait()
+    g_pass = remote(g_over_part, g_over_part, g_sem.at[4], g_sem.at[5], mate)
+    g_pass.start()
+
+    def pass_u(i, carry):
+        part = u_all.at[(1 - y) * CORES + core, i, pl.ds(0, SENT)]
+        remote(part, part, u_send.at[i, 0], u_recv.at[i, 0], over).wait_recv()
+        remote(part, part, u_send.at[i, 2], u_recv.at[i, 2], mate).start()
+        return carry
+
+    lax.fori_loop(0, images, pass_u, 0)
+
+    for k, partner in enumerate((mate, over, corner)):
+        source = partner[1]
+        remote(route, route_all.at[source], table_send.at[k, 0], table_recv.at[source, 0], partner).wait()
+        remote(comb, comb_all.at[source], table_send.at[k, 1], table_recv.at[source, 1], partner).wait()
+    for s in range(4):
+        for el in range(local):
+            named = me * local + el
+            row = s * local + el
+            hits = [route_all[s, t : t + 1, :] == named for t in range(TOP)]
+            chosen[row : row + 1, :] = sum(jnp.where(h, 1.0, 0.0) for h in hits)
+            comb_out[row : row + 1, :] = sum(
+                jnp.where(h, comb_all[s, t : t + 1, :], 0.0) for t, h in enumerate(hits)
+            )
+    earlier = lax.broadcasted_iota(jnp.int32, (PAD, PAD), 0) < lax.broadcasted_iota(
+        jnp.int32, (PAD, PAD), 1
+    )
+    earlier = jnp.where(earlier, 1.0, 0.0).astype(BF16)
+    total = jnp.zeros((4 * local, 1), F32)
+    for i in range(images):
+        block = chosen[:, i * PAD : (i + 1) * PAD]
+        position = total + dot(block.astype(BF16), earlier)
+        place_out[:, i * PAD : (i + 1) * PAD] = jnp.where(block > 0.0, position, -1.0).astype(
+            jnp.int32
+        )
+        total = total + jnp.sum(block, axis=1, keepdims=True)
+
+    def hand_on_rest(step, carry):
+        hand_on(step)
+        return carry
+
+    lax.fori_loop(images // 2, local * (lines - 1), hand_on_rest, 0)
+
+    def wait_images(i, carry):
+        part = u_all.at[me, i, pl.ds(0, SENT)]
+        remote(part, part, u_send.at[i, 0], u_recv.at[i, 0], over).wait_send()
+        remote(part, part, u_send.at[i, 1], u_recv.at[i, 1], mate).wait()
+        remote(part, part, u_send.at[i, 2], u_recv.at[i, 2], mate).wait()
+        return carry
+
+    lax.fori_loop(0, images, wait_images, 0)
+    to_mate.wait_send()
+    g_mate.wait()
+    g_pass.wait()
+    own_copy.wait()
+
+    def wait_weights(e, carry):
+        one = wfull.at[e, :, dp]
+        for hop in range(lines - 1):
+            @pl.when(jnp.logical_and(z - hop >= 0, z < lines - 1))
+            def _():
+                remote(one, one, up_send.at[e, hop], up_recv.at[e, hop], above).wait_send()
+
+            @pl.when(jnp.logical_and(z + hop <= lines - 1, z > 0))
+            def _():
+                remote(one, one, down_send.at[e, hop], down_recv.at[e, hop], below).wait_send()
+
+        for place in range(lines):
+            remote(one, one, x_send.at[e, place], x_recv.at[e, place], beside).wait()
+        return carry
+
+    lax.fori_loop(0, local, wait_weights, 0)
+
+
+def front(shards, group, tok, cot, route, comb, attn, vec, expw):
+    lines = shards // COLUMNS
+    images, local = tok.shape[0], expw.shape[0]
+    width = images * PAD
+    dma = pltpu.SemaphoreType.DMA
+    vm = pl.BlockSpec(memory_space=pltpu.VMEM)
+    hbm = pl.BlockSpec(memory_space=pl.ANY)
+    shape = jax.ShapeDtypeStruct
+    return pl.pallas_call(
+        functools.partial(front_kernel, shards, lines),
+        out_shape=(
+            shape((group, images, PAD, D), BF16),
+            shape((group, images, PAD, D), BF16),
+            shape((group * local, width), jnp.int32),
+            shape((group * local, width), F32),
+            shape((local, 2, shards) + expw.shape[2:], BF16),
+            shape((shards,) + attn.shape, BF16),
+            shape((8, D), F32),
+            shape((images, PAD, D), F32),
+            shape((images, PAD, 3 * D), BF16),
+            shape((images, PAD, D), BF16),
+        ),
+        in_specs=[vm] * 6 + [hbm],
+        out_specs=[vm] * 4 + [hbm] + [vm] * 5,
+        scratch_shapes=[
+            pltpu.VMEM((group, 8, width), jnp.int32),
+            pltpu.VMEM((group, 8, width), F32),
+            pltpu.VMEM((shards, 8, 128), F32),
+            pltpu.VMEM((group * local, width), F32),
+            dma((shards,)), dma((shards,)), dma((shards,)), dma((shards,)),
+            dma((2,)), dma((3, 2)), dma((group, 2)),
+            dma((6,)), dma((images, 3)), dma((images, 3)), dma(()),
+            dma((local, lines)), dma((local, lines)), dma((local, lines)), dma((local, lines)),
+            dma((local, lines)), dma((local, lines)),
+        ],
+        compiler_params=pltpu.CompilerParams(
+            collective_id=0, has_side_effects=True, vmem_limit_bytes=VMEM_LIMIT
+        ),
+    )(tok, cot, route, comb, attn, vec, expw)
+
+
+def gelu_parts(preact):
+    size = jnp.abs(preact)
+    inner = 1.0 / (1.0 + 0.23164189 * size)
+    series = inner * (
+        0.127414796
+        + inner * (-0.142248368 + inner * (0.7107068705 + inner * (-0.7265760135 + inner * 0.5307027145)))
+    )
+    bell = jnp.exp(-0.5 * preact * preact)
+    tail = series * bell
+    area = jnp.where(preact >= 0.0, 1.0 - tail, tail)
+    return preact * area, area + preact * bell * 0.3989422804014327
+
+
+def expert_kernel(
+    lines, place, comb, u_all, g_all, wfull,
+    grads, own_out, got_mate, got_corner, got_over,
+    ubuf, gbuf, wbuf, work, x_t, m_t, yacc, dacc, mine, sent, xr, zr, zs, fin,
+    load_sem, w_sem, fin_sem, own_sem, x_send, x_recv, up_send, up_recv, down_send, down_recv,
+    back_send, back_recv, credit_x, credit_up, credit_down,
+):
+    dp, me = lax.axis_index("dp"), lax.axis_index("expert")
+    z, x = dp // COLUMNS, dp % COLUMNS
+    y, core = me // CORES, me % CORES
+    group, images = u_all.shape[0], u_all.shape[1]
+    local = wfull.shape[0]
+    slots = x_t.shape[1] // group
+    ff = wfull.shape[-1]
+    tile = work.shape[-1]
+    tiles = ff // tile
+    last = lines - 1
+    mate = (dp, y * CORES + 1 - core)
+    over = (dp, (1 - y) * CORES + core)
+    above = (lax.rem(z + 1, lines) * COLUMNS + x, me)
+    below = (lax.rem(z + last, lines) * COLUMNS + x, me)
+    beside = (z * COLUMNS + 1 - x, me)
+    greet([above, below, beside, mate, over])
+
+    def load(step):
+        slot = step % 2
+        s = step % group
+        return (
+            pltpu.make_async_copy(u_all.at[s], ubuf.at[slot], load_sem.at[slot, 0]),
+            pltpu.make_async_copy(g_all.at[s], gbuf.at[slot], load_sem.at[slot, 1]),
+        )
+
+    def load_weights(e):
+        return pltpu.make_async_copy(wfull.at[e], wbuf, w_sem)
+
+    def send_across(e, k):
+        slot = e % 2
+        return remote(sent.at[slot, k], xr.at[slot, k], x_send.at[slot, k], x_recv.at[slot, k], beside)
+
+    def send_up(k, hop):
+        return remote(zs.at[k, 0], zr.at[k, 0, hop], up_send.at[k], up_recv.at[k, hop], above)
+
+    def send_down(k, hop):
+        return remote(zs.at[k, 1], zr.at[k, 1, hop], down_send.at[k], down_recv.at[k, hop], below)
+
+    def partial(e, k, owner):
+        slot = e % 2
+        return mine[slot, k, owner].astype(F32) + xr[slot, k, owner].astype(F32)
+
+    def one_hop(e, k, hop, way, ahead, send, credit, owner):
+        @pl.when(jnp.logical_and(ahead <= hop, ahead < last))
+        def _():
+            if hop > 0:
+                @pl.when(ahead <= hop - 1)
+                def _():
+                    send(k, hop - 1).wait_send()
+
+            @pl.when(jnp.logical_and(ahead == hop, e >= 1))
+            def _():
+                pl.semaphore_wait(credit.at[k], 1)
+
+            value = partial(e, k, owner)
+            if hop > 0:
+                @pl.when(ahead >= 1)
+                def _():
+                    send(k, hop - 1).wait_recv()
+                    zs[k, way] = (value + zr[k, way, hop - 1].astype(F32)).astype(BF16)
+
+                @pl.when(ahead < 1)
+                def _():
+                    zs[k, way] = value.astype(BF16)
+            else:
+                zs[k, way] = value.astype(BF16)
+            send(k, hop).start()
+
+    def hop_step(e, k, hop):
+        if hop == 0:
+            send_across(e, k).wait_recv()
+        one_hop(e, k, hop, 0, z, send_up, credit_up, jnp.minimum(z + last - hop, last))
+        one_hop(e, k, hop, 1, last - z, send_down, credit_down, jnp.maximum(z - last + hop, 0))
+
+    def finish(e, k):
+        copy = pltpu.make_async_copy(fin.at[k], grads.at[e, k], fin_sem.at[k])
+
+        @pl.when(e >= 1)
+        def _():
+            copy.wait()
+
+        fin[k] = partial(e, k, z)
+
+        @pl.when(z > 0)
+        def _():
+            send_up(k, last - 1).wait_recv()
+            fin[k] += zr[k, 0, last - 1].astype(F32)
+            send_down(k, last - 1).wait_send()
+
+        @pl.when(z < last)
+        def _():
+            send_down(k, last - 1).wait_recv()
+            fin[k] += zr[k, 1, last - 1].astype(F32)
+            send_up(k, last - 1).wait_send()
+
+        copy.start()
+
+        @pl.when(jnp.logical_and(e + 1 < local, z > 0))
+        def _():
+            pl.semaphore_signal(credit_up.at[k], inc=1, device_id=below, device_id_type=MESH)
+
+        @pl.when(jnp.logical_and(e + 1 < local, z < last))
+        def _():
+            pl.semaphore_signal(credit_down.at[k], inc=1, device_id=above, device_id_type=MESH)
+
+        @pl.when(e + 2 < local)
+        def _():
+            pl.semaphore_signal(credit_x.at[k], inc=1, device_id=beside, device_id_type=MESH)
+
+    def weight_grad(e, k):
+        slot = e % 2
+        left = x_t if k == 0 else m_t
+
+        @pl.when(e >= 2)
+        def _():
+            send_across(e, k).wait_send()
+
+        rows = wfull.shape[3]
+
+        def one_tile(j, carry):
+            right = work[tiles * (1 - k) + j, : group * slots, :]
+            block = dot(left[...], right).astype(BF16)
+            columns = pl.ds(pl.multiple_of(j * tile, tile), tile)
+            for d in range(lines * COLUMNS):
+                part = block[d * rows : (d + 1) * rows]
+
+                @pl.when(x == d % COLUMNS)
+                def _():
+                    mine[slot, k, d // COLUMNS, :, columns] = part
+
+                @pl.when(x != d % COLUMNS)
+                def _():
+                    sent[slot, k, d // COLUMNS, :, columns] = part
+
+            return carry
+
+        lax.fori_loop(0, tiles, one_tile, 0)
+
+        @pl.when(e >= 2)
+        def _():
+            pl.semaphore_wait(credit_x.at[k], 1)
+
+        send_across(e, k).start()
+
+    slot_row = lax.broadcasted_iota(jnp.int32, (slots, images * PAD), 0)
+
+    def one_source(e, s):
+        step = e * group + s
+        buffer = step % 2
+        for copy in load(step):
+            copy.wait()
+
+        @pl.when(step + 1 < local * group)
+        def _():
+            for copy in load(step + 1):
+                copy.start()
+
+        row = s * local + e
+        hit = slot_row == place[pl.ds(row, 1), :]
+        pick = jnp.where(hit, 1.0, 0.0).astype(BF16)
+        share = jnp.sum(jnp.where(hit, comb[pl.ds(row, 1), :], 0.0), axis=1, keepdims=True)
+        arrived = dot(pick, ubuf[buffer].reshape(images * PAD, D)).astype(BF16)
+        grad = (share * dot(pick, gbuf[buffer].reshape(images * PAD, D))).astype(BF16)
+        here = pl.ds(pl.multiple_of(s * slots, slots), slots)
+        x_t[:, here] = arrived.T
+        m_t[:, here] = grad.T
+
+        def one_tile(j, carry):
+            columns = pl.ds(pl.multiple_of(j * tile, tile), tile)
+            preact = dot(arrived, wbuf[0, :, :, columns].reshape(D, tile))
+            hidden, slope = gelu_parts(preact)
+            work[j, here, :] = hidden.astype(BF16)
+            grad_hidden = dot(grad, wbuf[1, :, :, columns].reshape(D, tile))
+            work[tiles + j, here, :] = (grad_hidden * slope).astype(BF16)
+            return carry
+
+        lax.fori_loop(0, tiles, one_tile, 0)
+        made = jnp.zeros((slots, D), F32)
+        back = jnp.zeros((slots, D), F32)
+        for j in range(tiles):
+            columns = pl.ds(j * tile, tile)
+            made += contract_last(work[j, here, :], wbuf[1, :, :, columns].reshape(D, tile))
+            back += contract_last(work[tiles + j, here, :], wbuf[0, :, :, columns].reshape(D, tile))
+        made = (share * made.astype(BF16).astype(F32)).astype(BF16)
+        back = back.astype(BF16)
+        for i in range(images):
+            part = pick[:, i * PAD : (i + 1) * PAD]
+            rows = pl.ds(i * SENT, SENT)
+            for total, values in ((yacc, made), (dacc, back)):
+                placed = contract_rows(part, values)[:SENT]
+
+                @pl.when(e == 0)
+                def _():
+                    total[s, rows, :] = placed
+
+                @pl.when(e > 0)
+                def _():
+                    total[s, rows, :] += placed
+
+    load_weights(0).start()
+    for copy in load(0):
+        copy.start()
+
+    def one_expert(e, carry):
+        load_weights(e).wait()
+
+        def step(s, carry):
+            one_source(e, s)
+            before = e - 2
+            for turn, actions in enumerate((
+                (lambda: hop_step(before, 0, 0),),
+                (lambda: hop_step(before, 0, 1), lambda: hop_step(before, 1, 0)),
+                (lambda: hop_step(before, 0, 2), lambda: hop_step(before, 1, 1)),
+                (lambda: finish(before, 0), lambda: hop_step(before, 1, 2)),
+            )):
+                @pl.when(jnp.logical_and(before >= 0, s == turn))
+                def _():
+                    for action in actions:
+                        action()
+
+            return carry
+
+        lax.fori_loop(0, group, step, 0)
+
+        @pl.when(e + 1 < local)
+        def _():
+            load_weights(e + 1).start()
+
+        weight_grad(e, 0)
+
+        @pl.when(e >= 2)
+        def _():
+            finish(e - 2, 1)
+
+        weight_grad(e, 1)
+        return carry
+
+    lax.fori_loop(0, local, one_expert, 0)
+
+    corner_s = (1 - y) * CORES + 1 - core
+    mate_s = y * CORES + 1 - core
+    over_s = (1 - y) * CORES + core
+    sums = (dacc, yacc)
+    for n, total in enumerate(sums):
+        work[2 * n] = total[corner_s].astype(BF16)
+        remote(work.at[2 * n], got_corner.at[n], back_send.at[n, 0], back_recv.at[n, 0], mate).start()
+        work[2 * n + 1] = total[mate_s].astype(BF16)
+        remote(work.at[2 * n + 1], got_mate.at[n], back_send.at[n, 1], back_recv.at[n, 1], mate).start()
+    for n, total in enumerate(sums):
+        pltpu.make_async_copy(total.at[me], own_out.at[n], own_sem.at[n]).start()
+    for n, total in enumerate(sums):
+        remote(work.at[2 * n], got_corner.at[n], back_send.at[n, 0], back_recv.at[n, 0], mate).wait_recv()
+        landed = pltpu.make_async_copy(got_corner.at[n], work.at[4 + n], own_sem.at[2])
+        landed.start()
+        landed.wait()
+        work[4 + n] = (total[over_s] + work[4 + n].astype(F32)).astype(BF16)
+        remote(work.at[4 + n], got_over.at[n], back_send.at[n, 2], back_recv.at[n, 2], over).start()
+
+    def drain(e, carry):
+        hop_step(e, 0, 0)
+        hop_step(e, 0, 1)
+        hop_step(e, 0, 2)
+        hop_step(e, 1, 0)
+        finish(e, 0)
+        hop_step(e, 1, 1)
+        hop_step(e, 1, 2)
+        finish(e, 1)
+        for k in range(2):
+            send_across(e, k).wait_send()
+        return carry
+
+    lax.fori_loop(local - 2, local, drain, 0)
+    for n, total in enumerate(sums):
+        remote(work.at[2 * n], got_corner.at[n], back_send.at[n, 0], back_recv.at[n, 0], mate).wait_send()
+        remote(work.at[2 * n + 1], got_mate.at[n], back_send.at[n, 1], back_recv.at[n, 1], mate).wait()
+        remote(work.at[4 + n], got_over.at[n], back_send.at[n, 2], back_recv.at[n, 2], over).wait()
+        pltpu.make_async_copy(total.at[me], own_out.at[n], own_sem.at[n]).wait()
+        pltpu.make_async_copy(fin.at[n], grads.at[0, n], fin_sem.at[n]).wait()
+
+
+def experts_step(shards, capacity, place, comb, u_all, g_all, wfull):
+    lines = shards // COLUMNS
+    group, images = u_all.shape[:2]
+    local, _, _, rows, ff = wfull.shape
+    slots = -(-capacity // 128) * 128
+    tile = 512
+    tiles = ff // tile
+    sent_rows = images * SENT
+    dma = pltpu.SemaphoreType.DMA
+    regular = pltpu.SemaphoreType.REGULAR
+    vm = pl.BlockSpec(memory_space=pltpu.VMEM)
+    hbm = pl.BlockSpec(memory_space=pl.ANY)
+    shape = jax.ShapeDtypeStruct
+    hops = lines - 1
+    return pl.pallas_call(
+        functools.partial(expert_kernel, lines),
+        out_shape=(
+            shape((local, 2, rows, ff), F32),
+            shape((2, sent_rows, D), F32),
+            shape((2, sent_rows, D), BF16),
+            shape((2, sent_rows, D), BF16),
+            shape((2, sent_rows, D), BF16),
+        ),
+        in_specs=[vm] * 2 + [hbm] * 3,
+        out_specs=[hbm] * 5,
+        scratch_shapes=[
+            pltpu.VMEM((2, images, PAD, D), BF16),
+            pltpu.VMEM((2, images, PAD, D), BF16),
+            pltpu.VMEM((2, shards, rows, ff), BF16),
+            pltpu.VMEM((2 * tiles, max(sent_rows, group * slots), tile), BF16),
+            pltpu.VMEM((D, group * slots), BF16),
+            pltpu.VMEM((D, group * slots), BF16),
+            pltpu.VMEM((group, sent_rows, D), F32),
+            pltpu.VMEM((group, sent_rows, D), F32),
+            pltpu.VMEM((2, 2, lines, rows, ff), BF16),
+            pltpu.VMEM((2, 2, lines, rows, ff), BF16),
+            pltpu.VMEM((2, 2, lines, rows, ff), BF16),
+            pltpu.VMEM((2, 2, hops, rows, ff), BF16),
+            pltpu.VMEM((2, 2, rows, ff), BF16),
+            pltpu.VMEM((2, rows, ff), F32),
+            dma((2, 2)), dma(()), dma((2,)), dma((3,)),
+            dma((2, 2)), dma((2, 2)), dma((2,)), dma((2, hops)), dma((2,)), dma((2, hops)),
+            dma((2, 3)), dma((2, 3)),
+            regular((2,)), regular((2,)), regular((2,)),
+        ],
+        compiler_params=pltpu.CompilerParams(
+            collective_id=1, has_side_effects=True, vmem_limit_bytes=VMEM_LIMIT
+        ),
+    )(place, comb, u_all, g_all, wfull)
 
 
 def adam_update(master, first, second, gradient, step_rate, decay_rate):
@@ -68,7 +731,314 @@
     return (master, first, second)
 
 
-def body(
+def back_kernel(
+    lines, tok, cot, middle, qkv, att, attnw, vectors, own, got_mate, got_over,
+    attn_old, first_old, second_old, vec_old, vec_first_old, vec_second_old,
+    mixed, grad_tok, attn_new, first_new, second_new, vec_new, vec_first_new, vec_second_new,
+    g_low, g_mid, dqkv, lowered, d_att, v_sum,
+    part_own, part_a, sum_a, part_b, sum_b, part_c, sum_c, part_d, sum_d, whole,
+    v_stage, v_got, v_lines,
+    a_sem, b_sem, c_sem, d_send, d_recv, e_send, e_recv, v_sem, vd_send, vd_recv,
+):
+    dp, me = lax.axis_index("dp"), lax.axis_index("expert")
+    z, x = dp // COLUMNS, dp % COLUMNS
+    y, core = me // CORES, me % CORES
+    images = tok.shape[0]
+    shards, rows = attnw.shape[:2]
+    half, quarter = rows // 2, rows // 4
+    mate = (dp, y * CORES + 1 - core)
+    over = (dp, (1 - y) * CORES + core)
+    corner = (dp, (1 - y) * CORES + 1 - core)
+    beside = (z * COLUMNS + 1 - x, me)
+    along = [(lax.rem(z + k, lines) * COLUMNS + x, me) for k in range(1, lines)]
+    greet([mate, over, corner, beside] + along)
+    gain_one, shift_one = vectors[0:1], vectors[1:2]
+    gain_two = vectors[2:3]
+    v_sum[...] = jnp.zeros_like(v_sum)
+
+    def rows_of(start, size):
+        return pl.ds(pl.multiple_of(start, quarter), size)
+
+    kept, given = rows_of(core * half, half), rows_of((1 - core) * half, half)
+    kept_y, given_y = rows_of(y * quarter, quarter), rows_of((1 - y) * quarter, quarter)
+    final_rows = rows_of(core * half + y * quarter, quarter)
+
+    def move_a(p):
+        return remote(part_own.at[p, :, given], part_a.at[p], a_sem.at[p, 0], a_sem.at[p, 1], mate)
+
+    def move_b(p):
+        return remote(sum_a.at[p, :, given_y], part_b.at[p], b_sem.at[p, 0], b_sem.at[p, 1], over)
+
+    def move_c(p):
+        return remote(sum_b.at[p, :, 1 - x], part_c.at[p], c_sem.at[p, 0], c_sem.at[p, 1], beside)
+
+    def move_d(p, k):
+        target = lax.rem(z + k, lines)
+        return remote(sum_c.at[p, target], part_d.at[p, z], d_send.at[p, k - 1], d_recv.at[p, z], along[k - 1])
+
+    def arrived_d(p, k):
+        source = lax.rem(z + lines - k, lines)
+        return remote(sum_c.at[p, source], part_d.at[p, source], d_send.at[p, k - 1], d_recv.at[p, source], along[k - 1])
+
+    def move_e(p, k):
+        columns = pl.ds(p * D, D)
+        mine = whole.at[final_rows, columns]
+        return remote(mine, mine, e_send.at[p, k], e_recv.at[p, k], (mate, over, corner)[k])
+
+    def stage_b(p):
+        move_a(p).wait()
+        sum_a[p] = (part_own[p, :, kept].astype(F32) + part_a[p].astype(F32)).astype(BF16)
+        move_b(p).start()
+
+    def stage_c(p):
+        move_b(p).wait()
+        total = sum_a[p, :, kept_y].astype(F32) + part_b[p].astype(F32)
+        sum_b[p] = total.astype(BF16).reshape(lines, COLUMNS, quarter, D)
+        move_c(p).start()
+
+    def stage_d(p):
+        move_c(p).wait()
+        total = sum_b[p, :, x].astype(F32) + part_c[p].astype(F32)
+        sum_c[p] = total.astype(BF16)
+        sum_d[p] = total
+        for k in range(1, lines):
+            move_d(p, k).start()
+
+    def stage_e(p):
+        total = sum_d[p, z]
+        for k in range(1, lines):
+            arrived_d(p, k).wait_recv()
+            total = total + part_d[p, lax.rem(z + lines - k, lines)].astype(F32)
+        whole[final_rows, pl.ds(p * D, D)] = total
+        for k in range(3):
+            move_e(p, k).start()
+
+    def settle(p):
+        for k in range(1, lines):
+            move_d(p, k).wait_send()
+        for k in range(3):
+            move_e(p, k).wait()
+
+    def scatter_part(p, left, right):
+        block = contract_rows(left, right).astype(BF16)
+        part_own[p] = block.reshape(shards, rows, D)
+        move_a(p).start()
+
+    def before_attention(i, carry):
+        here = pl.ds(pl.multiple_of(i * SENT, SENT), SENT)
+        mid = middle[i]
+        returned = own[1, here] + got_mate[1, here].astype(F32) + got_over[1, here].astype(F32)
+        mixed[i, :SENT] = (mid[:SENT] + returned).astype(BF16)
+        normed, inverse = normalize(mid)
+        grad = own[0, here] + got_mate[0, here].astype(F32) + got_over[0, here].astype(F32)
+        grad = jnp.concatenate([grad, jnp.zeros((PAD - SENT, D), F32)], axis=0)
+        v_sum[2:3] += jnp.sum(grad * normed, axis=0, keepdims=True)
+        v_sum[3:4] += jnp.sum(grad, axis=0, keepdims=True)
+        total = cot[i].astype(F32) + norm_back(grad * gain_two, normed, inverse)
+        v_sum[4:5] += jnp.sum(total, axis=0, keepdims=True)
+        g_mid[i] = total
+        low = total.astype(BF16)
+        g_low[i] = low
+        d_att[i] = contract_last(low, attnw[:, :, 3 * D :].reshape(D, D)).astype(BF16)
+        return carry
+
+    lax.fori_loop(0, images, before_attention, 0)
+    scatter_part(3, att[...].reshape(images * PAD, D), g_low[...].reshape(images * PAD, D))
+    pair_lane = lax.broadcasted_iota(jnp.int32, (PAD, 2 * HEAD_DIM), 1)
+
+    def attention(i, carry):
+        for pair in range(HEADS // 2):
+            offset = pair * 2 * HEAD_DIM
+            query = qkv[i, :, offset : offset + 128]
+            key_rows = qkv[i, :, D + offset : D + offset + 128]
+            value = qkv[i, :, 2 * D + offset : 2 * D + offset + 128]
+            grad = d_att[i, :, offset : offset + 128]
+            results = []
+            for which in range(2):
+                probs = softmax_rows(query, key_rows, which, pair_lane)
+                grad_own = jnp.where(pair_lane // HEAD_DIM == which, grad, jnp.zeros_like(grad))
+                grad_probs = contract_last(grad_own, value)
+                inner = jnp.sum(probs * grad_probs, axis=-1, keepdims=True)
+                grad_scores = (probs * (grad_probs - inner)).astype(BF16)
+                results.append((
+                    dot(grad_scores, key_rows) * HEAD_DIM ** (-0.5),
+                    contract_rows(grad_scores, query) * HEAD_DIM ** (-0.5),
+                    contract_rows(probs.astype(BF16), grad),
+                ))
+            for part in range(3):
+                joined = jnp.where(pair_lane < HEAD_DIM, results[0][part], results[1][part])
+                dqkv[i, :, part * D + offset : part * D + offset + 128] = joined.astype(BF16)
+        grad = jnp.zeros((PAD, D), F32)
+        for part in range(3):
+            columns = pl.ds(part * D, D)
+            grad += contract_last(dqkv[i, :, columns], attnw[:, :, columns].reshape(D, D))
+        normed, inverse = normalize(tok[i].astype(F32))
+        lowered[i] = (normed * gain_one + shift_one).astype(BF16)
+        v_sum[0:1] += jnp.sum(grad * normed, axis=0, keepdims=True)
+        v_sum[1:2] += jnp.sum(grad, axis=0, keepdims=True)
+        grad_tok[i] = (g_mid[i] + norm_back(grad * gain_one, normed, inverse)).astype(BF16)
+        for turn, stage in enumerate((stage_b, stage_c, stage_d, stage_e)):
+            @pl.when(i == turn)
+            def _():
+                stage(3)
+
+        return carry
+
+    lax.fori_loop(0, images, attention, 0)
+
+    def v_move(n, partner):
+        return remote(v_stage.at[n], v_got.at[n], v_sem.at[n, 0], v_sem.at[n, 1], partner)
+
+    v_stage[0] = v_sum[...]
+    v_move(0, mate).start()
+    for p in range(3):
+        scatter_part(p, lowered[...].reshape(images * PAD, D), dqkv[:, :, p * D : (p + 1) * D].reshape(images * PAD, D))
+    for n, (stage, partner) in enumerate(((stage_b, over), (stage_c, beside), (stage_d, None))):
+        for p in range(3):
+            stage(p)
+        v_move(n, (mate, over, beside)[n]).wait()
+        total = v_stage[n] + v_got[n]
+        if partner is not None:
+            v_stage[n + 1] = total
+            v_move(n + 1, partner).start()
+        else:
+            v_lines[z] = total
+            for k in range(1, lines):
+                remote(v_lines.at[z], v_lines.at[z], vd_send.at[k - 1], vd_recv.at[z], along[k - 1]).start()
+    for p in range(3):
+        stage_e(p)
+    for k in range(1, lines):
+        source = lax.rem(z + lines - k, lines)
+        remote(v_lines.at[source], v_lines.at[source], vd_send.at[k - 1], vd_recv.at[source], along[k - 1]).wait()
+    total = v_lines[0]
+    for n in range(1, lines):
+        total = total + v_lines[n]
+    width = D // shards
+    for d in range(shards):
+        @pl.when(dp == d)
+        def _():
+            gradient = total[: vec_old.shape[0], d * width : (d + 1) * width]
+            new = adam_update(vec_old[...], vec_first_old[...], vec_second_old[...], gradient, 0.2, 0.0)
+            vec_new[...], vec_first_new[...], vec_second_new[...] = new
+
+    for p in (3, 0, 1, 2):
+        settle(p)
+        columns = pl.ds(p * D, D)
+        new = adam_update(
+            attn_old[:, columns], first_old[:, columns], second_old[:, columns], whole[:, columns], 0.03, 0.1
+        )
+        attn_new[:, columns], first_new[:, columns], second_new[:, columns] = new
+
+
+def back(shards, tok, cot, middle, qkv, att, attnw, vectors, own, got_mate, got_over, attn_state, vec_state):
+    lines = shards // COLUMNS
+    images = tok.shape[0]
+    rows = attnw.shape[1]
+    half, quarter = rows // 2, rows // 4
+    dma = pltpu.SemaphoreType.DMA
+    vm = pl.BlockSpec(memory_space=pltpu.VMEM)
+    shape = jax.ShapeDtypeStruct
+    state = [shape(a.shape, F32) for a in attn_state + vec_state]
+    return pl.pallas_call(
+        functools.partial(back_kernel, lines),
+        out_shape=[shape((images, PAD, D), BF16)] * 2 + state,
+        in_specs=[vm] * 16,
+        out_specs=[vm] * 8,
+        scratch_shapes=[
+            pltpu.VMEM((images, PAD, D), BF16),
+            pltpu.VMEM((images, PAD, D), F32),
+            pltpu.VMEM((images, PAD, 3 * D), BF16),
+            pltpu.VMEM((images, PAD, D), BF16),
+            pltpu.VMEM((images, PAD, D), BF16),
+            pltpu.VMEM((8, D), F32),
+            pltpu.VMEM((4, shards, rows, D), BF16),
+            pltpu.VMEM((4, shards, half, D), BF16),
+            pltpu.VMEM((4, shards, half, D), BF16),
+            pltpu.VMEM((4, shards, quarter, D), BF16),
+            pltpu.VMEM((4, lines, COLUMNS, quarter, D), BF16),
+            pltpu.VMEM((4, lines, quarter, D), BF16),
+            pltpu.VMEM((4, lines, quarter, D), BF16),
+            pltpu.VMEM((4, lines, quarter, D), BF16),
+            pltpu.VMEM((4, lines, quarter, D), F32),
+            pltpu.VMEM((rows, 4 * D), F32),
+            pltpu.VMEM((3, 8, D), F32),
+            pltpu.VMEM((3, 8, D), F32),
+            pltpu.VMEM((lines, 8, D), F32),
+            dma((4, 2)), dma((4, 2)), dma((4, 2)), dma((4, lines - 1)), dma((4, lines)),
+            dma((4, 3)), dma((4, 3)), dma((3, 2)), dma((lines - 1,)), dma((lines,)),
+        ],
+        compiler_params=pltpu.CompilerParams(
+            collective_id=2, has_side_effects=True, vmem_limit_bytes=VMEM_LIMIT
+        ),
+    )(tok, cot, middle, qkv, att, attnw, vectors, own, got_mate, got_over, *attn_state, *vec_state)
+
+
+def by_image(rows):
+    images = rows.shape[0] // SEQ
+    return jnp.pad(rows.reshape((images, SEQ) + rows.shape[1:]), ((0, 0), (0, PAD - SEQ), (0, 0)))
+
+
+def as_lanes(table, fill):
+    images = table.shape[0] // SEQ
+    wide = table.T.reshape(TOP, images, SEQ)
+    wide = jnp.pad(wide, ((0, 8 - TOP), (0, 0), (0, PAD - SEQ)), constant_values=fill)
+    return wide.reshape(8, images * PAD)
+
+
+def to_tokens(rows, count):
+    return rows[:, :SEQ].reshape(count, D)
+
+
+def chip_body(shards, group):
+    def run(
+        tokens, cotangent, routes, combine, attn_master, attn_first, attn_second,
+        vector_master, vector_first, vector_second, expert_master, expert_first, expert_second,
+    ):
+        count = tokens.shape[0]
+        experts = expert_master.shape[2] * group
+        capacity = max(2, 4 * count // experts)
+        width = vector_master.shape[1]
+        tok, cot = by_image(tokens), by_image(cotangent)
+        vec = jnp.pad(
+            vector_master, ((0, 8 - vector_master.shape[0]), (0, 128 - width))
+        )
+        shard = jnp.transpose(expert_master.astype(BF16), (2, 1, 0, 3))
+        u_all, g_all, place, comb, wfull, attnw, vectors, middle, qkv, att = front(
+            shards, group, tok, cot, as_lanes(routes, -1), as_lanes(combine, 0.0),
+            attn_master.astype(BF16), vec, shard,
+        )
+        grads, own, got_mate, _, got_over = experts_step(
+            shards, capacity, place, comb, u_all, g_all, wfull
+        )
+        mixed, grad_tokens, *state = back(
+            shards, tok, cot, middle, qkv, att, attnw, vectors, own, got_mate, got_over,
+            [attn_master, attn_first, attn_second], [vector_master, vector_first, vector_second],
+        )
+        expert_new = adam_update(
+            expert_master, expert_first, expert_second, jnp.transpose(grads, (2, 1, 0, 3)), 0.02, 0.1
+        )
+        return (to_tokens(mixed, count), to_tokens(grad_tokens, count), *state, *expert_new)
+
+    return run
+
+
+def gelu_slope(preact):
+    return (
+        0.5 * (1.0 + lax.erf(preact * 0.7071067811865476))
+        + preact * jnp.exp(-0.5 * preact * preact) * 0.3989422804014327
+    )
+
+
+def slot_places(routes, experts):
+    flat_routes = routes.reshape(-1)
+    onehot = (flat_routes[:, None] == jnp.arange(experts, dtype=jnp.int32)[None, :]).astype(
+        jnp.int32
+    )
+    before = jnp.cumsum(onehot, axis=0) - onehot
+    return jnp.sum(before * onehot, axis=1)
+
+
+def general_body(
     tokens,
     cotangent,
     routes,
@@ -253,6 +1223,9 @@
 
 
 def solution(mesh):
+    shards, group = mesh.shape["dp"], mesh.shape["expert"]
+    chips = shards == 4 * COLUMNS and group == 2 * CORES
+    body = chip_body(shards, group) if chips else general_body
     return jax.shard_map(
         body,
         mesh=mesh,

time: 1500 us -> 607 us (0.40)
  waiting for transfers between devices: 795 us -> 0 us
  Pallas kernels: 0 us -> 550 us
  local copies, waits for them, and re-layouts: 285 us -> 36.3 us
  matrix products: 221 us -> 0 us
  other arithmetic: 123 us -> 15.7 us
  blocking collectives: 34.4 us -> 0 us
  starting transfers between devices: 20.2 us -> 0 us
    reduce_scatter x5 -> x0, waiting for transfers between devices: 672 us -> none  [the longest x4 606 us: body(): lax.psum_scatter(full_grad, 'dp', scatter_dimension=0, tiled=True)]
    pallas_call x0 -> x3, Pallas kernels: none -> 550 us  [the longest x1 260 us: experts_step(): pl.pallas_call(functools.partial(expert_kernel, lines), out_shape=(shape(...]
    dot_general x36 -> x0, matrix products: 221 us -> none  [the longest x4 85 us: body(): jnp.dot(arrived, expert_weight[:, 0, expert_item], preferred_element_type...]
    all_to_all x4 -> x0, waiting for transfers between devices: 53.5 us -> none  [the longest x1 36.3 us: body(): lax.all_to_all(jnp.stack(sent_back, 1), 'expert', split_axis=0, concat_ax...]
    slice x5 -> x2, local copies, waits for them, and re-layouts: 53 us -> 1.48 us  [to_tokens(): return rows[:, :SEQ].reshape(count, D)]
    another operation x20 -> x0, local copies, waits for them, and re-layouts: 41.3 us -> none  [the longest x5 10.5 us: body(): jnp.stack(sent_back, 1)]
    reshape x10 -> x6, local copies, waits for them, and re-layouts: 46.4 us -> 5.81 us  [the longest x2 2.48 us: to_tokens(): return rows[:, :SEQ].reshape(count, D)]
    reduce_sum x9 -> x0, other arithmetic: 39.1 us -> none  [the longest x1 22.4 us: body(): mixed = middle + jnp.sum(combine[:, :, None] * collect(returned), axis=1)]
  transfers between devices with their start and end apart: 13 -> 0, of which waited for: 10 -> 0; matrix products, arithmetic and copies ran while one was open for 22% -> 0% of each run, Pallas kernels for 0% -> 0%
where the time goes in v1:
time: 607 us; the launch traced here: 603 us
  Pallas kernels  550 us (91%)
  local copies, waits for them, and re-layouts  36.3 us (6%)
  other arithmetic  15.7 us (3%)
    pallas_call x1, Pallas kernels, experts_step(): pl.pallas_call(functools.partial(expert_kernel, lines), out_shape=(shape(...  260 us
    pallas_call x1, Pallas kernels, front(): pl.pallas_call(functools.partial(front_kernel, shards, lines), out_shape=...  223 us
    pallas_call x1, Pallas kernels, back(): pl.pallas_call(functools.partial(back_kernel, lines), out_shape=[shape((i...  66.8 us
    unnamed x30, local copies, waits for them, and re-layouts  25.3 us
    sub x1, other arithmetic, adam_update(): master - step_rate * (first_hat / (jnp.sqrt(second_hat) + ADAM_EPS) + dec...  14 us

profile of v1, /device:TPU:0, one launch (start us, length us, event | category | flops | bytes accessed | tf_op | source)
XLA Modules:
  0.0 603.3 jit_solution(4917899241520388986)
XLA Ops:
  0.7 1.4 pad.23.vec
  2.0 0.8 reshape.48
  2.8 0.8 reshape.50
  3.6 0.6 copy.51
  4.2 0.6 copy.50
  4.9 1.8 convert_element_type.11.attn
  6.6 1.5 reshape.46
  8.1 1.2 pad.19.tok
  9.6 1.2 pad.20.cot
  10.8 5.7 copy.64
  16.5 223.1 %shard_map.212 = (bf16[4,5,256,512]{3,2,1,0:T(8,128)(2,1)}, bf16[4,5,256,512]{3,2,1,0:T(8,128)(2,1)}, s32[16,1280]{1,0:T(8,128)}, f32[16,1280]{1,0:T(8,128)}, bf...) custom-call(bf16[5,256,512]{2,1,0:T(8,128)(2,1)} %pad.19.tok, ...), custom_call_target="tpu_custom_call" | custom-call | tf_op jit(solution)/shard_map/pallas_call | solution.py:339
  239.6 260.3 %shard_map.213 = (f32[4,2,64,2048]{3,2,1,0:T(8,128)}, f32[2,1040,512]{2,1,0:T(8,128)}, bf16[2,1040,512]{2,1,0:T(8,128)(2,1)}, bf16[2,1040,512]{2,1,0:T(8,128)(2,1)}, bf16[2,1040,512]{2,1,0:T(8,128)(2,1)}) custom-call(s32[16,1280]{1,0:T(8,128)} %get-tuple-element.38.place, f32[16,1280]{1,0:T(8,128)} %get-tuple-element.39.comb, ...), custom_call_target="tpu_custom_call" | custom-call | tf_op jit(solution)/shard_map/pallas_call | solution.py:686
  499.9 66.8 %shard_map.214 = (bf16[5,256,512]{2,1,0:T(8,128)(2,1)}, bf16[5,256,512]{2,1,0:T(8,128)(2,1)}, f32[64,2048]{1,0:T(8,128)}, f32[64,2048]{1,0:T(8,128)}, f32[64,204...) custom-call(bf16[5,256,512]{2,1,0:T(8,128)(2,1)} %pad.19.tok, bf16[5,256,512]{2,1,0:T(8,128)(2,1)} %pad.20.cot, ...), custom_call_target="tpu_custom_call" | custom-call | tf_op jit(solution)/shard_map/pallas_call | solution.py:942
  566.7 1.4 slice.6
  568.1 1.2 reshape.52
  569.5 1.2 reshape.53
  570.7 14.0 %multiply_subtract_fusion = (f32[64,2,4,2048]{3,0,1,2:T(8,128)S(1)}, f32[64,2,4,2048]{3,0,1,2:T(8,128)S(1)}, f32[64,2,4,2048]{3,0,1,2:T(8,128)S(1)}) fusion(f32[64,2,4,2048]{3,2,1,0:T(4,128)} %param.23, f32[4,2,64,2048]{3,2,1,0:T(8,128)} %get-tuple-element.54, f32[64,2,4,2048]{3,2,1,0:T(4,128)} %param.24, f32[64,2,4,2048]{3,2,1,0:T(4,128)} %param.25), kind=kLoop, calls=%fused_computation.6 | loop fusion | flops 15728640 | bytes 29360128 | tf_op jit(solution)/shard_map/sub | solution.py:728
  584.7 4.7 copy.47
  589.4 4.7 copy.48
  594.1 4.7 copy.49
  598.9 0.8 copy.71
  599.7 0.8 copy.72
  600.5 0.8 copy.73
  601.8 0.6 copy.75
  (22 shorter events, 1.6 us)
Async XLA Ops:
  0.6 8.7 %copy-start = (bf16[985,512]{1,0:T(8,128)(2,1)S(1)}, bf16[985,512]{1,0:T(8,128)(2,1)}, u32[]{:S(2)}) copy-start(bf16[985,512]{1,0:T(8,128)(2,1)} %param.14) | copy-start | bytes 3025924
  566.7 2.6 copy-start.1
  594.1 4.7 copy-start.4
  594.1 5.5 copy-start.3
  594.1 6.3 %copy-start.2 = (f32[64,2048]{1,0:T(8,128)S(1)}, f32[64,2048]{1,0:T(8,128)}, u32[]{:S(2)}) copy-start(f32[64,2048]{1,0:T(8,128)} %get-tuple-element.106) | copy-start | bytes 1572868
  594.1 7.1 %copy-start.7 = (f32[5,64]{1,0:T(8,128)S(1)}, f32[5,64]{1,0:T(8,128)}, u32[]{:S(2)}) copy-start(f32[5,64]{1,0:T(8,128)} %get-tuple-element.107) | copy-start | bytes 3844
  594.1 7.7 %copy-start.6 = (f32[5,64]{1,0:T(8,128)S(1)}, f32[5,64]{1,0:T(8,128)}, u32[]{:S(2)}) copy-start(f32[5,64]{1,0:T(8,128)} %get-tuple-element.108) | copy-start | bytes 3844
  594.1 8.3 %copy-start.5 = (f32[5,64]{1,0:T(8,128)S(1)}, f32[5,64]{1,0:T(8,128)}, u32[]{:S(2)}) copy-start(f32[5,64]{1,0:T(8,128)} %get-tuple-element.109) | copy-start | bytes 3844

commit v2 on v0

--- a/solution.py
+++ b/solution.py
@@ -1,6 +1,10 @@
+import functools
+
 import jax
 import jax.numpy as jnp
 from jax import lax
+from jax.experimental import pallas as pl
+from jax.experimental.pallas import tpu as pltpu
 from jax.sharding import PartitionSpec as P
 
 D = 512
@@ -9,12 +13,35 @@
 SEQ = 197
 TOP = 2
 STEP = 10
-
+PAD = 256
+SENT = 208
+CORES = 2
+COLUMNS = 2
 
 LN_EPS = 1e-06
 BETA_ONE = 0.9
 BETA_TWO = 0.999
 ADAM_EPS = 1e-08
+MESH = pl.DeviceIdType.MESH
+F32 = jnp.float32
+BF16 = jnp.bfloat16
+VMEM_LIMIT = 63 * 1024 * 1024
+
+
+def dot(left, right):
+    return jnp.dot(left, right, preferred_element_type=F32)
+
+
+def contract_rows(left, right):
+    return lax.dot_general(
+        left, right, (((0,), (0,)), ((), ())), preferred_element_type=F32
+    )
+
+
+def contract_last(left, right):
+    return lax.dot_general(
+        left, right, (((1,), (1,)), ((), ())), preferred_element_type=F32
+    )
 
 
 def normalize(values):
@@ -29,32 +56,44 @@
     return inverse * (grad_normed - first_mean - normed * second_mean)
 
 
-def gelu_slope(preact):
-    return (
-        0.5 * (1.0 + lax.erf(preact * 0.7071067811865476))
-        + preact * jnp.exp(-0.5 * preact * preact) * 0.3989422804014327
-    )
-
-
-def slot_places(routes, experts):
-    flat_routes = routes.reshape(-1)
-    onehot = (flat_routes[:, None] == jnp.arange(experts, dtype=jnp.int32)[None, :]).astype(
-        jnp.int32
-    )
-    before = jnp.cumsum(onehot, axis=0) - onehot
-    return jnp.sum(before * onehot, axis=1)
-
-
-def contract_rows(left, right):
-    return lax.dot_general(
-        left, right, (((0,), (0,)), ((), ())), preferred_element_type=jnp.float32
-    )
-
-
-def contract_last(left, right):
-    return lax.dot_general(
-        left, right, (((1,), (1,)), ((), ())), preferred_element_type=jnp.float32
-    )
+def remote(source, target, send_sem, recv_sem, device):
+    return pltpu.make_async_remote_copy(
+        src_ref=source,
+        dst_ref=target,
+        send_sem=send_sem,
+        recv_sem=recv_sem,
+        device_id=device,
+        device_id_type=MESH,
+    )
+
+
+def greet(devices):
+    barrier = pltpu.get_barrier_semaphore()
+    for device in devices:
+        pl.semaphore_signal(barrier, inc=1, device_id=device, device_id_type=MESH)
+    pl.semaphore_wait(barrier, len(devices))
+
+
+def softmax_rows(query, key_rows, half, lane):
+    own = jnp.where(lane // HEAD_DIM == half, query, jnp.zeros_like(query))
+    scores = contract_last(own, key_rows) * HEAD_DIM ** (-0.5)
+    column = lax.broadcasted_iota(jnp.int32, scores.shape, 1)
+    scores = jnp.where(column < SEQ, scores, -1e30)
+    powers = jnp.exp(scores - jnp.max(scores, axis=-1, keepdims=True))
+    return powers * (1.0 / jnp.sum(powers, axis=-1, keepdims=True))
+
+
+def gelu_parts(preact):
+    size = jnp.abs(preact)
+    inner = 1.0 / (1.0 + 0.23164189 * size)
+    series = inner * (
+        0.127414796
+        + inner * (-0.142248368 + inner * (0.7107068705 + inner * (-0.7265760135 + inner * 0.5307027145)))
+    )
+    bell = jnp.exp(-0.5 * preact * preact)
+    tail = series * bell
+    area = jnp.where(preact >= 0.0, 1.0 - tail, tail)
+    return preact * area, area + preact * bell * 0.3989422804014327
 
 
 def adam_update(master, first, second, gradient, step_rate, decay_rate):
@@ -68,7 +107,1101 @@
     return (master, first, second)
 
 
-def body(
+ROUTE_FIRST = (1,)
+SUM_FIRST = (0, 2)
+CHAINS = (0, 2, 1, 3)
+
+
+def block_kernel(
+    shards, lines, slots,
+    route, comb, attn, vec, vec_old, vec_first_old, vec_second_old,
+    tok, cot, expw, attn_old, first_old, second_old,
+    vec_new, vec_first_new, vec_second_new,
+    u_all, g_all, wfull, middle, qkv, att, own_out, d_mate, d_corner, d_over, y_stage, y_got,
+    grads, mixed, grad_tok, attn_new, first_new, second_new,
+    attnw, route_all, comb_all, vslots, chosen, place, shares,
+    gst, xr, xo, xst, zr, zs, fin,
+    part_a, part_b, part_c, part_d, whole, v_sum, v_stage, v_got, v_lines,
+    attn_send, attn_recv, vec_send, vec_recv, pass_sem, table_send, table_recv,
+    g_sem, u_send, u_recv, own_sem, up_send, up_recv, down_send, down_recv, x_send, x_recv,
+    out_sem, in_sem, load_sem, w_sem, fin_sem,
+    rx_send, rx_recv, ro_send, ro_recv, ru_send, ru_recv, rd_send, rd_recv, credit_up, credit_down,
+    back_send, back_recv, y_send, y_recv,
+    a_sem, b_sem, c_sem, d_send, d_recv, e_send, e_recv, v_sem, vd_send, vd_recv,
+):
+    dp, me = lax.axis_index("dp"), lax.axis_index("expert")
+    z, x = dp // COLUMNS, dp % COLUMNS
+    y, core = me // CORES, me % CORES
+    group, images = u_all.shape[:2]
+    local, _, rows, ff = expw.shape
+    last = lines - 1
+    half, quarter = rows // 2, rows // 4
+    tile = 512
+    tiles = ff // tile
+    mate_s, over_s, corner_s = y * CORES + 1 - core, (1 - y) * CORES + core, (1 - y) * CORES + 1 - core
+    mate, over, corner = (dp, mate_s), (dp, over_s), (dp, corner_s)
+    above = (lax.rem(z + 1, lines) * COLUMNS + x, me)
+    below = (lax.rem(z + last, lines) * COLUMNS + x, me)
+    beside = (z * COLUMNS + 1 - x, me)
+    along = [(lax.rem(z + k, lines) * COLUMNS + x, me) for k in range(1, lines)]
+    peers = [(lax.rem(dp + k, shards), me) for k in range(1, shards)]
+    sources = [lax.rem(dp + shards - k, shards) for k in range(1, shards)]
+    partners = (mate, over, corner)
+    greet(peers + list(partners))
+    mine = pl.ds(pl.multiple_of(core * half, half), half)
+    theirs = pl.ds(pl.multiple_of((1 - core) * half, half), half)
+    sent_images = pl.ds(0, SENT)
+
+    for k, peer in enumerate(peers):
+        remote(attn.at[mine], attnw.at[dp, mine], attn_send.at[k], attn_recv.at[dp], peer).start()
+        remote(vec, vslots.at[dp], vec_send.at[k], vec_recv.at[dp], peer).start()
+    for k, partner in enumerate(partners):
+        remote(route, route_all.at[me], table_send.at[k, 0], table_recv.at[me, 0], partner).start()
+        remote(comb, comb_all.at[me], table_send.at[k, 1], table_recv.at[me, 1], partner).start()
+
+    def held(e, chain, at):
+        column = x if chain == 0 else 1 - x
+        return wfull.at[e, :, at * COLUMNS + column]
+
+    def up(e, chain, hop, ref):
+        return remote(ref, ref, up_send.at[e * 2 + chain, hop], up_recv.at[e * 2 + chain, hop], above)
+
+    def down(e, chain, hop, ref):
+        return remote(ref, ref, down_send.at[e * 2 + chain, hop], down_recv.at[e * 2 + chain, hop], below)
+
+    def across(e, at, ref):
+        return remote(ref, ref, x_send.at[e, at], x_recv.at[e, at], beside)
+
+    def start_own(e):
+        target = held(e, 0, z)
+        remote(expw.at[e], target, x_send.at[e, z], x_recv.at[e, z], beside).start()
+
+        @pl.when(z < last)
+        def _():
+            remote(expw.at[e], target, up_send.at[e * 2, 0], up_recv.at[e * 2, 0], above).start()
+
+        @pl.when(z > 0)
+        def _():
+            remote(expw.at[e], target, down_send.at[e * 2, 0], down_recv.at[e * 2, 0], below).start()
+
+    def start_other(e):
+        ref = held(e, 1, z)
+        across(e, z, ref).wait_recv()
+
+        @pl.when(z < last)
+        def _():
+            up(e, 1, 0, ref).start()
+
+        @pl.when(z > 0)
+        def _():
+            down(e, 1, 0, ref).start()
+
+    def hand_on(e, chain, hop):
+        cross = e not in ROUTE_FIRST
+        from_below = jnp.maximum(z - 1 - hop, 0)
+        from_above = jnp.minimum(z + 1 + hop, last)
+
+        @pl.when(z - 1 - hop >= 0)
+        def _():
+            ref = held(e, chain, from_below)
+            up(e, chain, hop, ref).wait_recv()
+
+            @pl.when(z < last)
+            def _():
+                up(e, chain, hop + 1, ref).start()
+
+            if cross:
+                across(e, from_below, ref).start()
+
+        @pl.when(z + 1 + hop <= last)
+        def _():
+            ref = held(e, chain, from_above)
+            down(e, chain, hop, ref).wait_recv()
+
+            @pl.when(z > 0)
+            def _():
+                down(e, chain, hop + 1, ref).start()
+
+            if cross:
+                across(e, from_above, ref).start()
+
+    def weights_here(e):
+        if e not in ROUTE_FIRST:
+            for at in range(lines):
+                across(e, at, held(e, 1, at)).wait_recv()
+
+    def settle_weights(e):
+        ref = held(e, 0, z)
+        for chain in range(2 if e in ROUTE_FIRST else 1):
+            for hop in range(last):
+                @pl.when(jnp.logical_and(z - hop >= 0, z < last))
+                def _():
+                    up(e, chain, hop, ref).wait_send()
+
+                @pl.when(jnp.logical_and(z + hop <= last, z > 0))
+                def _():
+                    down(e, chain, hop, ref).wait_send()
+
+        if e in ROUTE_FIRST:
+            across(e, z, ref).wait_send()
+        else:
+            for at in range(lines):
+                across(e, at, ref).wait_send()
+
+    start_own(0)
+    start_own(1)
+    g_own = cot.at[:, sent_images]
+    g_mine = g_all.at[me]
+    remote(g_own, g_mine, g_sem.at[0], g_sem.at[1], mate).start()
+    remote(g_own, g_mine, g_sem.at[2], g_sem.at[3], over).start()
+    own_copy = pltpu.make_async_copy(expw, wfull.at[:, :, dp], own_sem.at[0])
+    own_copy.start()
+    g_copy = pltpu.make_async_copy(g_own, g_mine, own_sem.at[1])
+    g_copy.start()
+
+    attnw[dp, mine] = attn[mine]
+    vslots[dp] = vec[...]
+    route_all[me] = route[...]
+    comb_all[me] = comb[...]
+
+    for k, partner in enumerate(partners):
+        source = partner[1]
+        remote(route, route_all.at[source], table_send.at[k, 0], table_recv.at[source, 0], partner).wait()
+        remote(comb, comb_all.at[source], table_send.at[k, 1], table_recv.at[source, 1], partner).wait()
+    for s in range(group):
+        for el in range(local):
+            named = me * local + el
+            row = s * local + el
+            hits = [route_all[s, t : t + 1, :] == named for t in range(TOP)]
+            chosen[row : row + 1, :] = sum(jnp.where(h, 1.0, 0.0) for h in hits)
+            shares[row : row + 1, :] = sum(
+                jnp.where(h, comb_all[s, t : t + 1, :], 0.0) for t, h in enumerate(hits)
+            )
+    earlier = lax.broadcasted_iota(jnp.int32, (PAD, PAD), 0) < lax.broadcasted_iota(
+        jnp.int32, (PAD, PAD), 1
+    )
+    earlier = jnp.where(earlier, 1.0, 0.0).astype(BF16)
+    count = jnp.zeros((group * local, 1), F32)
+    for i in range(images):
+        block = chosen[:, i * PAD : (i + 1) * PAD]
+        position = count + dot(block.astype(BF16), earlier)
+        place[:, i * PAD : (i + 1) * PAD] = jnp.where(block > 0.0, position, -1.0).astype(jnp.int32)
+        count = count + jnp.sum(block, axis=1, keepdims=True)
+
+    for k, (peer, source) in enumerate(zip(peers, sources)):
+        remote(attn.at[mine], attnw.at[source, mine], attn_send.at[k], attn_recv.at[source], peer).wait()
+        remote(vec, vslots.at[source], vec_send.at[k], vec_recv.at[source], peer).wait()
+    to_mate = remote(attnw.at[:, mine], attnw.at[:, mine], pass_sem.at[0], pass_sem.at[1], mate)
+    to_mate.start()
+    lane = lax.broadcasted_iota(jnp.int32, (128, D), 1)
+    entry = lax.broadcasted_iota(jnp.int32, (128, D), 0)
+    width = D // shards
+    vectors = jnp.zeros((8, D), F32)
+    for d in range(shards):
+        spread = jnp.where(jnp.logical_and(entry < width, lane == entry + d * width), 1.0, 0.0)
+        vectors = vectors + dot(vslots[d].astype(BF16), spread.astype(BF16))
+    gain_one, shift_one = vectors[0:1], vectors[1:2]
+    gain_two, shift_two, shift_out = vectors[2:3], vectors[3:4], vectors[4:5]
+    remote(attnw.at[:, theirs], attnw.at[:, theirs], pass_sem.at[0], pass_sem.at[1], mate).wait_recv()
+    pair_lane = lax.broadcasted_iota(jnp.int32, (PAD, 2 * HEAD_DIM), 1)
+
+    def u_part(s, i):
+        return u_all.at[s, i]
+
+    def u_to(k, s, i, partner):
+        return remote(u_part(s, i), u_part(s, i), u_send.at[i, k], u_recv.at[i, k], partner)
+
+    def forward(tok_v, qkv_v, att_v, mid_v, u_v):
+        fetch = pltpu.make_async_copy(tok, tok_v, in_sem.at[0])
+        fetch.start()
+        fetch.wait()
+
+        def outs(i):
+            return (
+                pltpu.make_async_copy(u_v.at[i, sent_images], u_all.at[me, i], out_sem.at[i, 0]),
+                pltpu.make_async_copy(qkv_v.at[i], qkv.at[i], out_sem.at[i, 1]),
+                pltpu.make_async_copy(att_v.at[i], att.at[i], out_sem.at[i, 2]),
+                pltpu.make_async_copy(mid_v.at[i], middle.at[i], out_sem.at[i, 3]),
+            )
+
+        def send_image(i):
+            outs(i)[0].wait()
+            u_to(0, me, i, over).start()
+            u_to(1, me, i, mate).start()
+
+        def one_image(i, carry):
+            inputs = tok_v[i].astype(F32)
+            normed, _ = normalize(inputs)
+            lowered = (normed * gain_one + shift_one).astype(BF16)
+            for part in range(3):
+                columns = pl.ds(part * D, D)
+                qkv_v[i, :, columns] = dot(lowered, attnw[:, :, columns].reshape(D, D)).astype(BF16)
+            for pair in range(HEADS // 2):
+                offset = pair * 2 * HEAD_DIM
+                query = qkv_v[i, :, offset : offset + 128]
+                key_rows = qkv_v[i, :, D + offset : D + offset + 128]
+                value = qkv_v[i, :, 2 * D + offset : 2 * D + offset + 128]
+                results = []
+                for which in range(2):
+                    probs = softmax_rows(query, key_rows, which, pair_lane)
+                    results.append(dot(probs.astype(BF16), value))
+                joined = jnp.where(pair_lane < HEAD_DIM, results[0], results[1])
+                att_v[i, :, offset : offset + 128] = joined.astype(BF16)
+            mid = inputs + dot(att_v[i], attnw[:, :, 3 * D :].reshape(D, D)) + shift_out
+            mid_v[i] = mid
+            normed_two, _ = normalize(mid)
+            u_v[i] = (normed_two * gain_two + shift_two).astype(BF16)
+            for copy in outs(i):
+                copy.start()
+
+            @pl.when(i > 0)
+            def _():
+                send_image(i - 1)
+
+            for turn, actions in enumerate((
+                (lambda: start_other(1), lambda: start_own(2)),
+                (lambda: hand_on(0, 0, 1),),
+                (lambda: hand_on(1, 0, 0),),
+                (lambda: hand_on(0, 0, 2),),
+                (lambda: hand_on(1, 1, 0), lambda: start_own(3)),
+            )):
+                @pl.when(i == turn)
+                def _():
+                    for action in actions:
+                        action()
+
+            return carry
+
+        hand_on(0, 0, 0)
+        lax.fori_loop(0, images, one_image, 0)
+        send_image(images - 1)
+        for i in range(images):
+            for copy in outs(i)[1:]:
+                copy.wait()
+
+    pl.run_scoped(
+        forward,
+        pltpu.VMEM((images, PAD, D), BF16),
+        pltpu.VMEM((images, PAD, 3 * D), BF16),
+        pltpu.VMEM((images, PAD, D), BF16),
+        pltpu.VMEM((images, PAD, D), F32),
+        pltpu.VMEM((images, PAD, D), BF16),
+    )
+    g_over = g_all.at[over_s]
+    remote(g_over, g_over, g_sem.at[2], g_sem.at[3], over).wait()
+    remote(g_over, g_over, g_sem.at[4], g_sem.at[5], mate).start()
+    g_mate = g_all.at[mate_s]
+    remote(g_mate, g_mate, g_sem.at[0], g_sem.at[1], mate).wait()
+    g_corner = g_all.at[corner_s]
+    remote(g_corner, g_corner, g_sem.at[4], g_sem.at[5], mate).wait()
+    g_copy.wait()
+    own_copy.wait()
+
+    def slot_of(e):
+        return e % 2 if e < local - 1 else 2
+
+    def cross_sum(e, k):
+        return remote(
+            gst.at[slot_of(e), k, pl.ds(lines, lines)], xr.at[e // 2, k],
+            rx_send.at[e // 2, k], rx_recv.at[e // 2, k], beside,
+        )
+
+    def swap(e, k):
+        return remote(xst.at[k], xo.at[e // 2, k], ro_send.at[e // 2, k], ro_recv.at[e // 2, k], beside)
+
+    def partial(e, k, owner, which):
+        value = gst[slot_of(e), k, which * lines + owner].astype(F32)
+        if e not in SUM_FIRST:
+            value = value + xr[e // 2, k, owner].astype(F32)
+        return value
+
+    def z_send(e, k, way, hop):
+        sent, landed = zs.at[k, way], zr.at[k, way, hop]
+        if e not in SUM_FIRST:
+            sent, landed = sent.at[0], landed.at[0]
+        if way == 0:
+            return remote(sent, landed, ru_send.at[k], ru_recv.at[k, hop], above)
+        return remote(sent, landed, rd_send.at[k], rd_recv.at[k, hop], below)
+
+    def one_hop(e, k, hop, way):
+        ahead = z if way == 0 else last - z
+        owner = jnp.minimum(z + last - hop, last) if way == 0 else jnp.maximum(z - last + hop, 0)
+        credit = (credit_up, credit_down)[way]
+        both = range(2 if e in SUM_FIRST else 1)
+
+        @pl.when(jnp.logical_and(ahead <= hop, ahead < last))
+        def _():
+            if hop > 0:
+                @pl.when(ahead <= hop - 1)
+                def _():
+                    z_send(e, k, way, hop - 1).wait_send()
+
+            if CHAINS.index(e) > 0:
+                @pl.when(ahead == hop)
+                def _():
+                    pl.semaphore_wait(credit.at[k], 1)
+
+            if hop > 0:
+                @pl.when(ahead >= 1)
+                def _():
+                    z_send(e, k, way, hop - 1).wait_recv()
+                    for which in both:
+                        total = partial(e, k, owner, which) + zr[k, way, hop - 1, which].astype(F32)
+                        zs[k, way, which] = total.astype(BF16)
+
+                @pl.when(ahead < 1)
+                def _():
+                    for which in both:
+                        zs[k, way, which] = partial(e, k, owner, which).astype(BF16)
+            else:
+                for which in both:
+                    zs[k, way, which] = partial(e, k, owner, which).astype(BF16)
+            z_send(e, k, way, hop).start()
+
+    def hop_step(e, k, hop):
+        if hop == 0 and e not in SUM_FIRST:
+            cross_sum(e, k).wait_recv()
+        one_hop(e, k, hop, 0)
+        one_hop(e, k, hop, 1)
+
+    def to_result(e, k):
+        return pltpu.make_async_copy(fin.at[k], grads.at[e, k], fin_sem.at[k])
+
+    def finish(e, k):
+        turn = CHAINS.index(e)
+        if turn > 0:
+            to_result(e, k).wait()
+        fin[k] = partial(e, k, z, 0)
+
+        @pl.when(z > 0)
+        def _():
+            z_send(e, k, 0, last - 1).wait_recv()
+            fin[k] += zr[k, 0, last - 1, 0].astype(F32)
+            z_send(e, k, 1, last - 1).wait_send()
+
+        @pl.when(z < last)
+        def _():
+            z_send(e, k, 1, last - 1).wait_recv()
+            fin[k] += zr[k, 1, last - 1, 0].astype(F32)
+            z_send(e, k, 0, last - 1).wait_send()
+
+        if e in SUM_FIRST:
+            own = partial(e, k, z, 1)
+
+            @pl.when(z == 0)
+            def _():
+                xst[k] = (own + zr[k, 1, last - 1, 1].astype(F32)).astype(BF16)
+
+            @pl.when(z == last)
+            def _():
+                xst[k] = (own + zr[k, 0, last - 1, 1].astype(F32)).astype(BF16)
+
+            @pl.when(jnp.logical_and(z > 0, z < last))
+            def _():
+                arrived = zr[k, 0, last - 1, 1].astype(F32) + zr[k, 1, last - 1, 1].astype(F32)
+                xst[k] = (own + arrived).astype(BF16)
+
+            swap(e, k).start()
+        else:
+            to_result(e, k).start()
+        if turn + 1 < local:
+            @pl.when(z > 0)
+            def _():
+                pl.semaphore_signal(credit_up.at[k], inc=1, device_id=below, device_id_type=MESH)
+
+            @pl.when(z < last)
+            def _():
+                pl.semaphore_signal(credit_down.at[k], inc=1, device_id=above, device_id_type=MESH)
+
+    def collect(e, k):
+        swap(e, k).wait()
+        fin[k] += xo[e // 2, k].astype(F32)
+        to_result(e, k).start()
+
+    def source_of(e, t):
+        r = t if e == local - 1 else group - 1 - t
+        across_y = (1 - y) + (r // CORES) * (2 * y - 1)
+        return across_y * CORES + (1 - core) + (r % CORES) * (2 * core - 1)
+
+    def experts(ubuf, gbuf, work, x_t, m_t, dacc, made_all, d_stage):
+        def load(s):
+            return (
+                pltpu.make_async_copy(u_all.at[s], ubuf.at[:, sent_images], load_sem.at[0]),
+                pltpu.make_async_copy(g_all.at[s], gbuf.at[:, sent_images], load_sem.at[1]),
+            )
+
+        def load_weights(e):
+            return pltpu.make_async_copy(wfull.at[e], gst.at[2], w_sem)
+
+        def weight_grad(e, k):
+            left = x_t if k == 0 else m_t
+
+            def one_tile(j, carry):
+                right = work[tiles * (1 - k) + j]
+                block = dot(left[...], right).astype(BF16)
+                columns = pl.ds(pl.multiple_of(j * tile, tile), tile)
+                for d in range(shards):
+                    which = lax.rem(x + d % COLUMNS, COLUMNS)
+                    index = which * lines + d // COLUMNS
+                    gst[slot_of(e), k, index, :, columns] = block[d * rows : (d + 1) * rows]
+                return carry
+
+            lax.fori_loop(0, tiles, one_tile, 0)
+            if e not in SUM_FIRST:
+                cross_sum(e, k).start()
+
+        def pick_of(s, e, i):
+            slot_row = lax.broadcasted_iota(jnp.int32, (slots, PAD), 0)
+            return slot_row == place[pl.ds(s * local + e, 1), i * PAD : (i + 1) * PAD]
+
+        def one_source(e, t, after_gather):
+            s = source_of(e, t)
+            for copy in load(s):
+                copy.wait()
+            arrived = jnp.zeros((slots, D), F32)
+            grad = jnp.zeros((slots, D), F32)
+            share = jnp.zeros((slots, 1), F32)
+            for i in range(images):
+                hit = pick_of(s, e, i)
+                pick = jnp.where(hit, 1.0, 0.0).astype(BF16)
+                weight = shares[pl.ds(s * local + e, 1), i * PAD : (i + 1) * PAD]
+                share += jnp.sum(jnp.where(hit, weight, 0.0), axis=1, keepdims=True)
+                arrived += dot(pick, ubuf[i])
+                grad += dot(pick, gbuf[i])
+            arrived = arrived.astype(BF16)
+            grad = (share * grad).astype(BF16)
+            here = pl.ds(pl.multiple_of(t * slots, slots), slots)
+            x_t[:, here] = arrived.T
+            m_t[:, here] = grad.T
+            after_gather()
+
+            def one_tile(j, carry):
+                columns = pl.ds(pl.multiple_of(j * tile, tile), tile)
+                preact = dot(arrived, gst[2, 0, :, :, columns].reshape(D, tile))
+                hidden, slope = gelu_parts(preact)
+                work[j, here, :] = hidden.astype(BF16)
+                grad_hidden = dot(grad, gst[2, 1, :, :, columns].reshape(D, tile))
+                work[tiles + j, here, :] = (grad_hidden * slope).astype(BF16)
+                return carry
+
+            lax.fori_loop(0, tiles, one_tile, 0)
+            made = jnp.zeros((slots, D), F32)
+            back = jnp.zeros((slots, D), F32)
+            for j in range(tiles):
+                columns = pl.ds(j * tile, tile)
+                made += contract_last(work[j, here, :], gst[2, 1, :, :, columns].reshape(D, tile))
+                back += contract_last(work[tiles + j, here, :], gst[2, 0, :, :, columns].reshape(D, tile))
+            made_all[s, e * slots : (e + 1) * slots] = (share * made.astype(BF16).astype(F32)).astype(BF16)
+            back = back.astype(BF16)
+            for i in range(images):
+                pick = jnp.where(pick_of(s, e, i), 1.0, 0.0).astype(BF16)
+                placed = contract_rows(pick, back)[:SENT]
+                if e == 0:
+                    dacc[s, i * SENT : (i + 1) * SENT] = placed
+                else:
+                    dacc[s, i * SENT : (i + 1) * SENT] += placed
+
+        def next_load(e, t):
+            @pl.when(t + 1 < group)
+            def _():
+                if e == 0:
+                    @pl.when(t == 0)
+                    def _():
+                        for i in range(images):
+                            u_to(1, mate_s, i, mate).wait()
+
+                    @pl.when(t == 1)
+                    def _():
+                        for i in range(images):
+                            u_to(0, over_s, i, over).wait()
+                            u_to(2, over_s, i, mate).start()
+
+                    @pl.when(t == 2)
+                    def _():
+                        for i in range(images):
+                            u_to(2, corner_s, i, mate).wait()
+
+                for copy in load(source_of(e, t + 1)):
+                    copy.start()
+
+            if e + 1 < local:
+                @pl.when(t + 1 == group)
+                def _():
+                    for copy in load(source_of(e + 1, 0)):
+                        copy.start()
+
+        def to_corner():
+            return remote(d_stage.at[0], d_corner, back_send.at[0], back_recv.at[0], mate)
+
+        def to_mate_sum():
+            return remote(d_stage.at[1], d_mate, back_send.at[1], back_recv.at[1], mate)
+
+        def to_over():
+            return remote(d_stage.at[2], d_over, back_send.at[2], back_recv.at[2], over)
+
+        def sums_corner():
+            d_stage[0] = dacc[corner_s].astype(BF16)
+            to_corner().start()
+
+        def sums_mate():
+            d_stage[1] = dacc[mate_s].astype(BF16)
+            to_mate_sum().start()
+            to_corner().wait_recv()
+            landed = pltpu.make_async_copy(d_corner, d_stage.at[2], load_sem.at[2])
+            landed.start()
+            landed.wait()
+            d_stage[2] = (dacc[over_s] + d_stage[2].astype(F32)).astype(BF16)
+            to_over().start()
+
+        plan = {
+            (0, 0): (lambda: hand_on(1, 0, 1),),
+            (0, 2): (lambda: hand_on(1, 1, 1),),
+            (1, 0): (lambda: hand_on(2, 0, 1), lambda: hop_step(0, 1, 1)),
+            (1, 1): (lambda: hop_step(0, 0, 2),),
+            (1, 2): (lambda: hand_on(2, 0, 2),),
+            (1, 3): (lambda: hop_step(0, 1, 2),),
+            (2, 0): (lambda: hand_on(3, 0, 1), lambda: collect(0, 0)),
+            (2, 1): (lambda: collect(0, 1),),
+            (2, 2): (lambda: hand_on(3, 0, 2),),
+            (3, 0): (sums_corner, lambda: hop_step(2, 0, 1)),
+            (3, 1): (lambda: hop_step(2, 1, 1),),
+            (3, 2): (sums_mate, lambda: hop_step(2, 0, 2)),
+            (3, 3): (lambda: hop_step(2, 1, 2),),
+        }
+        after_grad = {
+            (0, 0): (lambda: hop_step(0, 0, 0),),
+            (0, 1): (lambda: hop_step(0, 1, 0), lambda: hand_on(1, 0, 2), lambda: hand_on(1, 1, 2),
+                     lambda: hand_on(2, 0, 0), lambda: hop_step(0, 0, 1)),
+            (1, 0): (lambda: finish(0, 0),),
+            (1, 1): (lambda: finish(0, 1), lambda: hand_on(3, 0, 0)),
+            (2, 0): (lambda: hop_step(2, 0, 0),),
+            (2, 1): (lambda: hop_step(2, 1, 0),),
+            (3, 0): (lambda: finish(2, 0),),
+            (3, 1): (lambda: finish(2, 1),),
+        }
+
+        empty = jnp.zeros((images, PAD - SENT, D), BF16)
+        ubuf[:, SENT:, :] = empty
+        gbuf[:, SENT:, :] = empty
+        for copy in load(source_of(0, 0)):
+            copy.start()
+        for e in range(local):
+            weights_here(e)
+            load_weights(e).start()
+            load_weights(e).wait()
+
+            def step(t, carry, e=e):
+                one_source(e, t, lambda: next_load(e, t))
+                for turn in range(group):
+                    actions = plan.get((e, turn), ())
+                    if actions:
+                        @pl.when(t == turn)
+                        def _():
+                            for action in actions:
+                                action()
+
+                return carry
+
+            lax.fori_loop(0, group, step, 0)
+            for k in range(2):
+                weight_grad(e, k)
+                for action in after_grad.get((e, k), ()):
+                    action()
+
+        pltpu.make_async_copy(dacc.at[me], own_out.at[0], own_sem.at[2]).start()
+
+        def one_sum(s, i):
+            total = jnp.zeros((PAD, D), F32)
+            for e in range(local):
+                pick = jnp.where(pick_of(s, e, i), 1.0, 0.0).astype(BF16)
+                total += contract_rows(pick, made_all[s, e * slots : (e + 1) * slots])
+            return total[:SENT]
+
+        def stage(k):
+            return pltpu.make_async_copy(d_stage.at[k], y_stage.at[k], own_sem.at[3])
+
+        for k, (s, partner) in enumerate(zip((mate_s, over_s, corner_s), partners)):
+            (to_corner, to_mate_sum, to_over)[k]().wait_send()
+            for i in range(images):
+                d_stage[k, i * SENT : (i + 1) * SENT] = one_sum(s, i).astype(BF16)
+            stage(k).start()
+            stage(k).wait()
+            remote(y_stage.at[k], y_got.at[k], y_send.at[k], y_recv.at[k], partner).start()
+        for i in range(images):
+            dacc[corner_s, i * SENT : (i + 1) * SENT] = one_sum(me, i)
+        pltpu.make_async_copy(dacc.at[corner_s], own_out.at[1], own_sem.at[4]).start()
+        pltpu.make_async_copy(dacc.at[corner_s], own_out.at[1], own_sem.at[4]).wait()
+        pltpu.make_async_copy(dacc.at[me], own_out.at[0], own_sem.at[2]).wait()
+
+    count_rows = images * SENT
+    pl.run_scoped(
+        experts,
+        pltpu.VMEM((images, PAD, D), BF16),
+        pltpu.VMEM((images, PAD, D), BF16),
+        pltpu.VMEM((2 * tiles, group * slots, tile), BF16),
+        pltpu.VMEM((D, group * slots), BF16),
+        pltpu.VMEM((D, group * slots), BF16),
+        pltpu.VMEM((group, count_rows, D), F32),
+        pltpu.VMEM((group, local * slots, D), BF16),
+        pltpu.VMEM((3, count_rows, D), BF16),
+    )
+    remote(d_mate, d_mate, back_send.at[1], back_recv.at[1], mate).wait_recv()
+    remote(d_over, d_over, back_send.at[2], back_recv.at[2], over).wait_recv()
+
+    def rows_of(start, size):
+        return pl.ds(pl.multiple_of(start, quarter), size)
+
+    kept_y, given_y = rows_of(y * quarter, quarter), rows_of((1 - y) * quarter, quarter)
+    final_rows = rows_of(core * half + y * quarter, quarter)
+
+    def backward(g_low, g_mid, d_att, v_fetch):
+        v_sum[...] = jnp.zeros_like(v_sum)
+
+        def before_attention(cot_v, mid_v, own_v, mate_v, over_v):
+            fetches = [
+                pltpu.make_async_copy(source, target, in_sem.at[n])
+                for n, (source, target) in enumerate((
+                    (cot, cot_v), (middle, mid_v), (own_out.at[0], own_v), (d_mate, mate_v), (d_over, over_v),
+                ))
+            ]
+            for fetch in fetches:
+                fetch.start()
+            for fetch in fetches:
+                fetch.wait()
+
+            def one_image(i, carry):
+                here = pl.ds(pl.multiple_of(i * SENT, SENT), SENT)
+                normed, inverse = normalize(mid_v[i])
+                grad = own_v[here] + mate_v[here].astype(F32) + over_v[here].astype(F32)
+                grad = jnp.concatenate([grad, jnp.zeros((PAD - SENT, D), F32)], axis=0)
+                v_sum[2:3] += jnp.sum(grad * normed, axis=0, keepdims=True)
+                v_sum[3:4] += jnp.sum(grad, axis=0, keepdims=True)
+                total = cot_v[i].astype(F32) + norm_back(grad * gain_two, normed, inverse)
+                v_sum[4:5] += jnp.sum(total, axis=0, keepdims=True)
+                g_mid[i] = total
+                low = total.astype(BF16)
+                g_low[i] = low
+                d_att[i] = contract_last(low, attnw[:, :, 3 * D :].reshape(D, D)).astype(BF16)
+                return carry
+
+            lax.fori_loop(0, images, one_image, 0)
+
+        pl.run_scoped(
+            before_attention,
+            pltpu.VMEM((images, PAD, D), BF16),
+            pltpu.VMEM((images, PAD, D), F32),
+            pltpu.VMEM((count_rows, D), F32),
+            pltpu.VMEM((count_rows, D), BF16),
+            pltpu.VMEM((count_rows, D), BF16),
+        )
+
+        def through_attention(
+            tok_v, qkv_v, att_v, dqkv, lowered, part_own, sum_a, sum_b, sum_c, sum_d, gt_v, old_v, new_v
+        ):
+            def move_a(p):
+                return remote(part_own.at[p, :, theirs], part_a.at[p], a_sem.at[p, 0], a_sem.at[p, 1], mate)
+
+            def move_b(p):
+                return remote(sum_a.at[p, :, given_y], part_b.at[p], b_sem.at[p, 0], b_sem.at[p, 1], over)
+
+            def move_c(p):
+                return remote(sum_b.at[p, :, 1 - x], part_c.at[p], c_sem.at[p, 0], c_sem.at[p, 1], beside)
+
+            def move_d(p, k):
+                target = lax.rem(z + k, lines)
+                return remote(
+                    sum_c.at[p, target], part_d.at[p, z], d_send.at[p, k - 1], d_recv.at[p, z], along[k - 1]
+                )
+
+            def arrived_d(p, k):
+                source = lax.rem(z + lines - k, lines)
+                return remote(
+                    sum_c.at[p, source], part_d.at[p, source], d_send.at[p, k - 1], d_recv.at[p, source],
+                    along[k - 1],
+                )
+
+            def move_e(p, k):
+                own = whole.at[final_rows, pl.ds(p * D, D)]
+                return remote(own, own, e_send.at[p, k], e_recv.at[p, k], partners[k])
+
+            def stage_b(p):
+                move_a(p).wait()
+                sum_a[p] = (part_own[p, :, mine].astype(F32) + part_a[p].astype(F32)).astype(BF16)
+                move_b(p).start()
+
+            def stage_c(p):
+                move_b(p).wait()
+                total = sum_a[p, :, kept_y].astype(F32) + part_b[p].astype(F32)
+                sum_b[p] = total.astype(BF16).reshape(lines, COLUMNS, quarter, D)
+                move_c(p).start()
+
+            def stage_d(p):
+                move_c(p).wait()
+                total = sum_b[p, :, x].astype(F32) + part_c[p].astype(F32)
+                sum_c[p] = total.astype(BF16)
+                sum_d[p] = total
+                for k in range(1, lines):
+                    move_d(p, k).start()
+
+            def stage_e(p):
+                total = sum_d[p, z]
+                for k in range(1, lines):
+                    arrived_d(p, k).wait_recv()
+                    total = total + part_d[p, lax.rem(z + lines - k, lines)].astype(F32)
+                whole[final_rows, pl.ds(p * D, D)] = total
+                for k in range(3):
+                    move_e(p, k).start()
+
+            def settle(p):
+                for k in range(1, lines):
+                    move_d(p, k).wait_send()
+                for k in range(3):
+                    move_e(p, k).wait()
+
+            def scatter_part(p, left, right):
+                block = contract_rows(left, right).astype(BF16)
+                part_own[p] = block.reshape(shards, rows, D)
+                move_a(p).start()
+
+            fetches = [
+                pltpu.make_async_copy(source, target, in_sem.at[n])
+                for n, (source, target) in enumerate((
+                    (tok, tok_v), (qkv, qkv_v), (att, att_v),
+                    (attn_old, old_v.at[0]), (first_old, old_v.at[1]), (second_old, old_v.at[2]),
+                ))
+            ]
+            for fetch in fetches:
+                fetch.start()
+            for fetch in fetches:
+                fetch.wait()
+            scatter_part(3, att_v[...].reshape(images * PAD, D), g_low[...].reshape(images * PAD, D))
+
+            def result(i):
+                return pltpu.make_async_copy(gt_v.at[i], grad_tok.at[i], out_sem.at[i, 0])
+
+            def one_image(i, carry):
+                for pair in range(HEADS // 2):
+                    offset = pair * 2 * HEAD_DIM
+                    query = qkv_v[i, :, offset : offset + 128]
+                    key_rows = qkv_v[i, :, D + offset : D + offset + 128]
+                    value = qkv_v[i, :, 2 * D + offset : 2 * D + offset + 128]
+                    grad = d_att[i, :, offset : offset + 128]
+                    results = []
+                    for which in range(2):
+                        probs = softmax_rows(query, key_rows, which, pair_lane)
+                        grad_own = jnp.where(pair_lane // HEAD_DIM == which, grad, jnp.zeros_like(grad))
+                        grad_probs = contract_last(grad_own, value)
+                        inner = jnp.sum(probs * grad_probs, axis=-1, keepdims=True)
+                        grad_scores = (probs * (grad_probs - inner)).astype(BF16)
+                        results.append((
+                            dot(grad_scores, key_rows) * HEAD_DIM ** (-0.5),
+                            contract_rows(grad_scores, query) * HEAD_DIM ** (-0.5),
+                            contract_rows(probs.astype(BF16), grad),
+                        ))
+                    for part in range(3):
+                        joined = jnp.where(pair_lane < HEAD_DIM, results[0][part], results[1][part])
+                        dqkv[i, :, part * D + offset : part * D + offset + 128] = joined.astype(BF16)
+                grad = jnp.zeros((PAD, D), F32)
+                for part in range(3):
+                    columns = pl.ds(part * D, D)
+                    grad += contract_last(dqkv[i, :, columns], attnw[:, :, columns].reshape(D, D))
+                normed, inverse = normalize(tok_v[i].astype(F32))
+                lowered[i] = (normed * gain_one + shift_one).astype(BF16)
+                v_sum[0:1] += jnp.sum(grad * normed, axis=0, keepdims=True)
+                v_sum[1:2] += jnp.sum(grad, axis=0, keepdims=True)
+                gt_v[i] = (g_mid[i] + norm_back(grad * gain_one, normed, inverse)).astype(BF16)
+                result(i).start()
+                for turn, actions in enumerate((
+                    (lambda: stage_b(3), lambda: collect(2, 0), lambda: collect(2, 1), lambda: hop_step(1, 0, 0)),
+                    (lambda: stage_c(3), lambda: hop_step(1, 1, 0), lambda: hop_step(1, 0, 1)),
+                    (lambda: stage_d(3), lambda: hop_step(1, 1, 1), lambda: hop_step(1, 0, 2)),
+                    (lambda: stage_e(3), lambda: hop_step(1, 1, 2), lambda: finish(1, 0)),
+                    (lambda: finish(1, 1), lambda: hop_step(3, 0, 0)),
+                )):
+                    @pl.when(i == turn)
+                    def _():
+                        for action in actions:
+                            action()
+
+                return carry
+
+            lax.fori_loop(0, images, one_image, 0)
+
+            def v_move(n, partner):
+                return remote(v_stage.at[n], v_got.at[n], v_sem.at[n, 0], v_sem.at[n, 1], partner)
+
+            v_stage[0] = v_sum[...]
+            v_move(0, mate).start()
+            for p in range(3):
+                scatter_part(
+                    p, lowered[...].reshape(images * PAD, D),
+                    dqkv[:, :, p * D : (p + 1) * D].reshape(images * PAD, D),
+                )
+            tail = {
+                0: (lambda: hop_step(3, 0, 1),),
+                1: (lambda: hop_step(3, 1, 0), lambda: hop_step(3, 0, 2)),
+                2: (lambda: hop_step(3, 1, 1), lambda: finish(3, 0)),
+            }
+            for n, stage in enumerate((stage_b, stage_c, stage_d)):
+                for p in range(3):
+                    stage(p)
+                v_move(n, (mate, over, beside)[n]).wait()
+                total = v_stage[n] + v_got[n]
+                if n < 2:
+                    v_stage[n + 1] = total
+                    v_move(n + 1, (over, beside)[n]).start()
+                else:
+                    v_lines[z] = total
+                    for k in range(1, lines):
+                        remote(
+                            v_lines.at[z], v_lines.at[z], vd_send.at[k - 1], vd_recv.at[z], along[k - 1]
+                        ).start()
+                for action in tail[n]:
+                    action()
+            for p in range(3):
+                stage_e(p)
+            hop_step(3, 1, 2)
+            for k in range(1, lines):
+                source = lax.rem(z + lines - k, lines)
+                remote(
+                    v_lines.at[source], v_lines.at[source], vd_send.at[k - 1], vd_recv.at[source], along[k - 1]
+                ).wait()
+            total = v_lines[0]
+            for n in range(1, lines):
+                total = total + v_lines[n]
+            for d in range(shards):
+                @pl.when(dp == d)
+                def _():
+                    gradient = total[: vec_old.shape[0], d * width : (d + 1) * width]
+                    new = adam_update(
+                        vec_old[...], vec_first_old[...], vec_second_old[...], gradient, 0.2, 0.0
+                    )
+                    vec_new[...], vec_first_new[...], vec_second_new[...] = new
+
+            for p in (3, 0, 1, 2):
+                settle(p)
+            for p in range(4):
+                columns = pl.ds(p * D, D)
+                new = adam_update(
+                    old_v[0, :, columns], old_v[1, :, columns], old_v[2, :, columns], whole[:, columns],
+                    0.03, 0.1,
+                )
+                for n in range(3):
+                    new_v[n, :, columns] = new[n]
+            results = [
+                pltpu.make_async_copy(new_v.at[n], target, in_sem.at[n])
+                for n, target in enumerate((attn_new, first_new, second_new))
+            ]
+            for copy in results:
+                copy.start()
+            for copy in results:
+                copy.wait()
+            for i in range(images):
+                result(i).wait()
+
+        pl.run_scoped(
+            through_attention,
+            pltpu.VMEM((images, PAD, D), BF16),
+            pltpu.VMEM((images, PAD, 3 * D), BF16),
+            pltpu.VMEM((images, PAD, D), BF16),
+            pltpu.VMEM((images, PAD, 3 * D), BF16),
+            pltpu.VMEM((images, PAD, D), BF16),
+            pltpu.VMEM((4, shards, rows, D), BF16),
+            pltpu.VMEM((4, shards, half, D), BF16),
+            pltpu.VMEM((4, lines, COLUMNS, quarter, D), BF16),
+            pltpu.VMEM((4, lines, quarter, D), BF16),
+            pltpu.VMEM((4, lines, quarter, D), F32),
+            pltpu.VMEM((images, PAD, D), BF16),
+            pltpu.VMEM((3, rows, 4 * D), F32),
+            pltpu.VMEM((3, rows, 4 * D), F32),
+        )
+
+    pl.run_scoped(
+        backward,
+        pltpu.VMEM((images, PAD, D), BF16),
+        pltpu.VMEM((images, PAD, D), F32),
+        pltpu.VMEM((images, PAD, D), BF16),
+        pltpu.VMEM((8, 128), F32),
+    )
+
+    def output(mid_v, own_v, got_v, out_v):
+        for k, partner in enumerate(partners):
+            remote(y_stage.at[k], y_got.at[k], y_send.at[k], y_recv.at[k], partner).wait()
+        fetches = [
+            pltpu.make_async_copy(source, target, in_sem.at[n])
+            for n, (source, target) in enumerate(((middle, mid_v), (own_out.at[1], own_v), (y_got, got_v)))
+        ]
+        for fetch in fetches:
+            fetch.start()
+        for fetch in fetches:
+            fetch.wait()
+        for i in range(images):
+            here = pl.ds(i * SENT, SENT)
+            returned = own_v[here]
+            for k in range(3):
+                returned = returned + got_v[k, here].astype(F32)
+            out_v[i, :SENT] = (mid_v[i, :SENT] + returned).astype(BF16)
+        copy = pltpu.make_async_copy(out_v, mixed, in_sem.at[3])
+        copy.start()
+        copy.wait()
+
+    pl.run_scoped(
+        output,
+        pltpu.VMEM((images, PAD, D), F32),
+        pltpu.VMEM((count_rows, D), F32),
+        pltpu.VMEM((3, count_rows, D), BF16),
+        pltpu.VMEM((images, PAD, D), BF16),
+    )
+    finish(3, 1)
+    to_mate.wait_send()
+    for e in range(local):
+        settle_weights(e)
+        if e not in SUM_FIRST:
+            for k in range(2):
+                cross_sum(e, k).wait_send()
+    for k in range(2):
+        to_result(3, k).wait()
+
+
+def block(shards, capacity, route, comb, attn, vec, tok, cot, expw, attn_state, vec_state, group):
+    lines = shards // COLUMNS
+    images = tok.shape[0]
+    local, _, rows, ff = expw.shape
+    slots = -(-capacity // 128) * 128
+    half, quarter = rows // 2, rows // 4
+    wide = images * PAD
+    count_rows = images * SENT
+    dma = pltpu.SemaphoreType.DMA
+    regular = pltpu.SemaphoreType.REGULAR
+    vm = pl.BlockSpec(memory_space=pltpu.VMEM)
+    hbm = pl.BlockSpec(memory_space=pl.ANY)
+    shape = jax.ShapeDtypeStruct
+    states = [shape(a.shape, F32) for a in vec_state]
+    attn_states = [shape(a.shape, F32) for a in attn_state]
+    last = lines - 1
+    outs = pl.pallas_call(
+        functools.partial(block_kernel, shards, lines, slots),
+        out_shape=states + [
+            shape((group, images, SENT, D), BF16),
+            shape((group, images, SENT, D), BF16),
+            shape((local, 2, shards, rows, ff), BF16),
+            shape((images, PAD, D), F32),
+            shape((images, PAD, 3 * D), BF16),
+            shape((images, PAD, D), BF16),
+            shape((2, count_rows, D), F32),
+            shape((count_rows, D), BF16),
+            shape((count_rows, D), BF16),
+            shape((count_rows, D), BF16),
+            shape((3, count_rows, D), BF16),
+            shape((3, count_rows, D), BF16),
+            shape((local, 2, rows, ff), F32),
+            shape((images, PAD, D), BF16),
+            shape((images, PAD, D), BF16),
+        ] + attn_states,
+        in_specs=[vm] * 7 + [hbm] * 6,
+        out_specs=[vm] * 3 + [hbm] * 18,
+        scratch_shapes=[
+            pltpu.VMEM((shards,) + attn.shape, BF16),
+            pltpu.VMEM((group, 8, wide), jnp.int32),
+            pltpu.VMEM((group, 8, wide), F32),
+            pltpu.VMEM((shards, 8, 128), F32),
+            pltpu.VMEM((group * local, wide), F32),
+            pltpu.VMEM((group * local, wide), jnp.int32),
+            pltpu.VMEM((group * local, wide), F32),
+            pltpu.VMEM((3, 2, shards, rows, ff), BF16),
+            pltpu.VMEM((2, 2, lines, rows, ff), BF16),
+            pltpu.VMEM((2, 2, rows, ff), BF16),
+            pltpu.VMEM((2, rows, ff), BF16),
+            pltpu.VMEM((2, 2, last, 2, rows, ff), BF16),
+            pltpu.VMEM((2, 2, 2, rows, ff), BF16),
+            pltpu.VMEM((2, rows, ff), F32),
+            pltpu.VMEM((4, shards, half, D), BF16),
+            pltpu.VMEM((4, shards, quarter, D), BF16),
+            pltpu.VMEM((4, lines, quarter, D), BF16),
+            pltpu.VMEM((4, lines, quarter, D), BF16),
+            pltpu.VMEM((rows, 4 * D), F32),
+            pltpu.VMEM((8, D), F32),
+            pltpu.VMEM((3, 8, D), F32),
+            pltpu.VMEM((3, 8, D), F32),
+            pltpu.VMEM((lines, 8, D), F32),
+            dma((shards,)), dma((shards,)), dma((shards,)), dma((shards,)),
+            dma((2,)), dma((3, 2)), dma((group, 2)),
+            dma((6,)), dma((images, 3)), dma((images, 3)), dma((5,)),
+            dma((2 * local, lines)), dma((2 * local, lines)), dma((2 * local, lines)), dma((2 * local, lines)),
+            dma((local, lines)), dma((local, lines)),
+            dma((images, 4)), dma((6,)), dma((3,)), dma(()), dma((2,)),
+            dma((2, 2)), dma((2, 2)), dma((2, 2)), dma((2, 2)),
+            dma((2,)), dma((2, last)), dma((2,)), dma((2, last)),
+            regular((2,)), regular((2,)),
+            dma((3,)), dma((3,)), dma((3,)), dma((3,)),
+            dma((4, 2)), dma((4, 2)), dma((4, 2)), dma((4, last)), dma((4, lines)),
+            dma((4, 3)), dma((4, 3)), dma((3, 2)), dma((last,)), dma((lines,)),
+        ],
+        compiler_params=pltpu.CompilerParams(
+            collective_id=0, has_side_effects=True, vmem_limit_bytes=VMEM_LIMIT
+        ),
+    )(route, comb, attn, vec, *vec_state, tok, cot, expw, *attn_state)
+    vec_new, grads, mixed, grad_tok, attn_new = outs[:3], outs[15], outs[16], outs[17], outs[18:]
+    return mixed, grad_tok, grads, attn_new, vec_new
+
+
+def by_image(rows):
+    images = rows.shape[0] // SEQ
+    return jnp.pad(rows.reshape((images, SEQ) + rows.shape[1:]), ((0, 0), (0, PAD - SEQ), (0, 0)))
+
+
+def as_lanes(table, fill):
+    images = table.shape[0] // SEQ
+    wide = table.T.reshape(TOP, images, SEQ)
+    wide = jnp.pad(wide, ((0, 8 - TOP), (0, 0), (0, PAD - SEQ)), constant_values=fill)
+    return wide.reshape(8, images * PAD)
+
+
+def to_tokens(rows, count):
+    return rows[:, :SEQ].reshape(count, D)
+
+
+def chip_body(shards, group):
+    def run(
+        tokens, cotangent, routes, combine, attn_master, attn_first, attn_second,
+        vector_master, vector_first, vector_second, expert_master, expert_first, expert_second,
+    ):
+        count = tokens.shape[0]
+        experts = expert_master.shape[2] * group
+        capacity = max(2, 4 * count // experts)
+        width = vector_master.shape[1]
+        vec = jnp.pad(vector_master, ((0, 8 - vector_master.shape[0]), (0, 128 - width)))
+        shard = jnp.transpose(expert_master.astype(BF16), (2, 1, 0, 3))
+        mixed, grad_tokens, grads, attn_new, vec_new = block(
+            shards, capacity, as_lanes(routes, -1), as_lanes(combine, 0.0), attn_master.astype(BF16), vec,
+            by_image(tokens), by_image(cotangent), shard,
+            [attn_master, attn_first, attn_second], [vector_master, vector_first, vector_second], group,
+        )
+        expert_new = adam_update(
+            expert_master, expert_first, expert_second, jnp.transpose(grads, (2, 1, 0, 3)), 0.02, 0.1
+        )
+        return (to_tokens(mixed, count), to_tokens(grad_tokens, count), *attn_new, *vec_new, *expert_new)
+
+    return run
+
+
+def gelu_slope(preact):
+    return (
+        0.5 * (1.0 + lax.erf(preact * 0.7071067811865476))
+        + preact * jnp.exp(-0.5 * preact * preact) * 0.3989422804014327
+    )
+
+
+def slot_places(routes, experts):
+    flat_routes = routes.reshape(-1)
+    onehot = (flat_routes[:, None] == jnp.arange(experts, dtype=jnp.int32)[None, :]).astype(
+        jnp.int32
+    )
+    before = jnp.cumsum(onehot, axis=0) - onehot
+    return jnp.sum(before * onehot, axis=1)
+
+
+def general_body(
     tokens,
     cotangent,
     routes,
@@ -253,6 +1386,9 @@
 
 
 def solution(mesh):
+    shards, group = mesh.shape["dp"], mesh.shape["expert"]
+    chips = shards == 4 * COLUMNS and group == 2 * CORES
+    body = chip_body(shards, group) if chips else general_body
     return jax.shard_map(
         body,
         mesh=mesh,

time: 1500 us -> 517 us (0.34)
  waiting for transfers between devices: 795 us -> 0 us
  Pallas kernels: 0 us -> 455 us
  local copies, waits for them, and re-layouts: 285 us -> 36.3 us
  matrix products: 221 us -> 0 us
  other arithmetic: 123 us -> 15.7 us
  blocking collectives: 34.4 us -> 0 us
  starting transfers between devices: 20.2 us -> 0 us
    reduce_scatter x5 -> x0, waiting for transfers between devices: 672 us -> none  [the longest x4 606 us: body(): lax.psum_scatter(full_grad, 'dp', scatter_dimension=0, tiled=True)]
    pallas_call x0 -> x1, Pallas kernels: none -> 455 us  [block(): pl.pallas_call(functools.partial(block_kernel, shards, lines, slots), out...]
    dot_general x36 -> x0, matrix products: 221 us -> none  [the longest x4 85 us: body(): jnp.dot(arrived, expert_weight[:, 0, expert_item], preferred_element_type...]
    all_to_all x4 -> x0, waiting for transfers between devices: 53.5 us -> none  [the longest x1 36.3 us: body(): lax.all_to_all(jnp.stack(sent_back, 1), 'expert', split_axis=0, concat_ax...]
    slice x5 -> x2, local copies, waits for them, and re-layouts: 53 us -> 1.48 us  [to_tokens(): return rows[:, :SEQ].reshape(count, D)]
    another operation x20 -> x0, local copies, waits for them, and re-layouts: 41.3 us -> none  [the longest x5 10.5 us: body(): jnp.stack(sent_back, 1)]
    reshape x10 -> x6, local copies, waits for them, and re-layouts: 46.4 us -> 5.81 us  [the longest x2 2.48 us: to_tokens(): return rows[:, :SEQ].reshape(count, D)]
    reduce_sum x9 -> x0, other arithmetic: 39.1 us -> none  [the longest x1 22.4 us: body(): mixed = middle + jnp.sum(combine[:, :, None] * collect(returned), axis=1)]
  transfers between devices with their start and end apart: 13 -> 0, of which waited for: 10 -> 0; matrix products, arithmetic and copies ran while one was open for 22% -> 0% of each run, Pallas kernels for 0% -> 0%
where the time goes in v2:
time: 517 us; the launch traced here: 508 us
  Pallas kernels  455 us (88%)
  local copies, waits for them, and re-layouts  36.3 us (7%)
  other arithmetic  15.7 us (3%)
    pallas_call x1, Pallas kernels, block(): pl.pallas_call(functools.partial(block_kernel, shards, lines, slots), out...  455 us
    unnamed x30, local copies, waits for them, and re-layouts  25.3 us
    sub x1, other arithmetic, adam_update(): master - step_rate * (first_hat / (jnp.sqrt(second_hat) + ADAM_EPS) + dec...  14 us

profile of v2, /device:TPU:0, one launch (start us, length us, event | category | flops | bytes accessed | tf_op | source)
XLA Modules:
  0.0 508.0 jit_solution(15409313769175485381)
XLA Ops:
  0.7 1.4 pad.21.vec
  2.0 0.8 reshape.46
  2.8 0.8 reshape.48
  3.6 0.6 copy.51
  4.2 0.6 copy.50
  4.9 1.8 convert_element_type.11.attn
  6.6 1.5 reshape.50
  8.1 1.2 pad.22.tok
  9.6 1.2 pad.23.cot
  10.8 5.7 %copy.64 = bf16[64,2,4,2048]{3,0,1,2:T(8,128)(2,1)} copy(f32[64,2,4,2048]{3,2,1,0:T(4,128)} %param.23) | data formatting | bytes 6291456 | tf_op args[10]
  16.5 454.8 %shard_map.212 = (f32[5,64]{1,0:T(8,128)}, f32[5,64]{1,0:T(8,128)}, f32[5,64]{1,0:T(8,128)}, bf16[4,5,208,512]{3,2,1,0:T(8,128)(2,1)}, bf16[4,5,208,512]{3,2,1,0...) custom-call(s32[8,1280]{1,0:T(8,128)} %bitcast.20, ...), custom_call_target="tpu_custom_call" | custom-call | tf_op jit(solution)/shard_map/pallas_call | solution.py:1082
  471.3 1.4 slice.6
  472.7 1.2 reshape.52
  474.0 1.2 reshape.53
  475.3 14.0 %multiply_subtract_fusion = (f32[64,2,4,2048]{3,0,1,2:T(8,128)S(1)}, f32[64,2,4,2048]{3,0,1,2:T(8,128)S(1)}, f32[64,2,4,2048]{3,0,1,2:T(8,128)S(1)}) fusion(f32[64,2,4,2048]{3,2,1,0:T(4,128)} %param.23, f32[4,2,64,2048]{3,2,1,0:T(8,128)} %get-tuple-element.28, f32[64,2,4,2048]{3,2,1,0:T(4,128)} %param.24, f32[64,2,4,2048]{3,2,1,0:T(4,128)} %param.25), kind=kLoop, calls=%fused_computation.6 | loop fusion | flops 15728640 | bytes 29360128 | tf_op jit(solution)/shard_map/sub | solution.py:104
  489.2 4.7 copy.47
  493.9 4.7 copy.48
  498.7 4.7 copy.49
  503.4 0.8 copy.71
  504.2 0.8 copy.72
  505.0 0.8 copy.73
  505.8 0.6 copy.74
  506.4 0.6 copy.75
  507.0 0.6 copy.76
  (20 shorter events, 0.4 us)
Async XLA Ops:
  0.6 8.7 %copy-start = (bf16[985,512]{1,0:T(8,128)(2,1)S(1)}, bf16[985,512]{1,0:T(8,128)(2,1)}, u32[]{:S(2)}) copy-start(bf16[985,512]{1,0:T(8,128)(2,1)} %param.14) | copy-start | bytes 3025924
  471.3 2.6 copy-start.1
  498.7 4.7 copy-start.4
  498.7 5.5 %copy-start.3 = (f32[64,2048]{1,0:T(8,128)S(1)}, f32[64,2048]{1,0:T(8,128)}, u32[]{:S(2)}) copy-start(f32[64,2048]{1,0:T(8,128)} %get-tuple-element.79) | copy-start | bytes 1572868
  498.7 6.3 %copy-start.2 = (f32[64,2048]{1,0:T(8,128)S(1)}, f32[64,2048]{1,0:T(8,128)}, u32[]{:S(2)}) copy-start(f32[64,2048]{1,0:T(8,128)} %get-tuple-element.80) | copy-start | bytes 1572868
  498.7 7.1 %copy-start.7 = (f32[5,64]{1,0:T(8,128)S(1)}, f32[5,64]{1,0:T(8,128)}, u32[]{:S(2)}) copy-start(f32[5,64]{1,0:T(8,128)} %get-tuple-element.81) | copy-start | bytes 3844
  498.7 7.7 %copy-start.6 = (f32[5,64]{1,0:T(8,128)S(1)}, f32[5,64]{1,0:T(8,128)}, u32[]{:S(2)}) copy-start(f32[5,64]{1,0:T(8,128)} %get-tuple-element.82) | copy-start | bytes 3844
  498.7 8.3 %copy-start.5 = (f32[5,64]{1,0:T(8,128)S(1)}, f32[5,64]{1,0:T(8,128)}, u32[]{:S(2)}) copy-start(f32[5,64]{1,0:T(8,128)} %get-tuple-element.83) | copy-start | bytes 3844

commit v3 on v2

--- a/solution.py
+++ b/solution.py
@@ -4,6 +4,7 @@
 import jax.numpy as jnp
 from jax import lax
 from jax.experimental import pallas as pl
+from jax.experimental.layout import Layout, with_layout_constraint
 from jax.experimental.pallas import tpu as pltpu
 from jax.sharding import PartitionSpec as P
 
@@ -85,7 +86,9 @@
 
 def gelu_parts(preact):
     size = jnp.abs(preact)
-    inner = 1.0 / (1.0 + 0.23164189 * size)
+    below = 1.0 + 0.23164189 * size
+    inner = pl.reciprocal(below, approx=True)
+    inner = inner * (2.0 - below * inner)
     series = inner * (
         0.127414796
         + inner * (-0.142248368 + inner * (0.7107068705 + inner * (-0.7265760135 + inner * 0.5307027145)))
@@ -107,19 +110,19 @@
     return (master, first, second)
 
 
-ROUTE_FIRST = (1,)
-SUM_FIRST = (0, 2)
-CHAINS = (0, 2, 1, 3)
+ROUTE_FIRST = ()
+SUM_FIRST = (0, 1)
+CHAINS = (0, 1, 2, 3)
 
 
 def block_kernel(
     shards, lines, slots,
-    route, comb, attn, vec, vec_old, vec_first_old, vec_second_old,
+    route, comb, attn_f, vec_old, vec_first_old, vec_second_old,
     tok, cot, expw, attn_old, first_old, second_old,
     vec_new, vec_first_new, vec_second_new,
-    u_all, g_all, wfull, middle, qkv, att, own_out, d_mate, d_corner, d_over, y_stage, y_got,
+    u_all, g_all, wfull, middle, qkv, att_t, low_t, own_out, d_mate, d_corner, d_over, y_stage, y_got,
     grads, mixed, grad_tok, attn_new, first_new, second_new,
-    attnw, route_all, comb_all, vslots, chosen, place, shares,
+    attn, vec, attnw, route_all, comb_all, vslots, chosen, place, shares,
     gst, xr, xo, xst, zr, zs, fin,
     part_a, part_b, part_c, part_d, whole, v_sum, v_stage, v_got, v_lines,
     attn_send, attn_recv, vec_send, vec_recv, pass_sem, table_send, table_recv,
@@ -152,6 +155,9 @@
     theirs = pl.ds(pl.multiple_of((1 - core) * half, half), half)
     sent_images = pl.ds(0, SENT)
 
+    attn[...] = attn_f[...].astype(BF16)
+    vec[...] = jnp.zeros_like(vec)
+    vec[: vec_old.shape[0], : vec_old.shape[1]] = vec_old[...]
     for k, peer in enumerate(peers):
         remote(attn.at[mine], attnw.at[dp, mine], attn_send.at[k], attn_recv.at[dp], peer).start()
         remote(vec, vslots.at[dp], vec_send.at[k], vec_recv.at[dp], peer).start()
@@ -254,10 +260,6 @@
     g_mine = g_all.at[me]
     remote(g_own, g_mine, g_sem.at[0], g_sem.at[1], mate).start()
     remote(g_own, g_mine, g_sem.at[2], g_sem.at[3], over).start()
-    own_copy = pltpu.make_async_copy(expw, wfull.at[:, :, dp], own_sem.at[0])
-    own_copy.start()
-    g_copy = pltpu.make_async_copy(g_own, g_mine, own_sem.at[1])
-    g_copy.start()
 
     attnw[dp, mine] = attn[mine]
     vslots[dp] = vec[...]
@@ -311,7 +313,7 @@
     def u_to(k, s, i, partner):
         return remote(u_part(s, i), u_part(s, i), u_send.at[i, k], u_recv.at[i, k], partner)
 
-    def forward(tok_v, qkv_v, att_v, mid_v, u_v):
+    def forward(tok_v, qkv_v, att_v, mid_v, u_v, att_tv, low_tv):
         fetch = pltpu.make_async_copy(tok, tok_v, in_sem.at[0])
         fetch.start()
         fetch.wait()
@@ -320,8 +322,9 @@
             return (
                 pltpu.make_async_copy(u_v.at[i, sent_images], u_all.at[me, i], out_sem.at[i, 0]),
                 pltpu.make_async_copy(qkv_v.at[i], qkv.at[i], out_sem.at[i, 1]),
-                pltpu.make_async_copy(att_v.at[i], att.at[i], out_sem.at[i, 2]),
-                pltpu.make_async_copy(mid_v.at[i], middle.at[i], out_sem.at[i, 3]),
+                pltpu.make_async_copy(mid_v.at[i], middle.at[i], out_sem.at[i, 2]),
+                pltpu.make_async_copy(att_tv.at[i], att_t.at[i], out_sem.at[i, 3]),
+                pltpu.make_async_copy(low_tv.at[i], low_t.at[i], out_sem.at[i, 4]),
             )
 
         def send_image(i):
@@ -351,6 +354,8 @@
             mid_v[i] = mid
             normed_two, _ = normalize(mid)
             u_v[i] = (normed_two * gain_two + shift_two).astype(BF16)
+            att_tv[i] = att_v[i].T
+            low_tv[i] = lowered.T
             for copy in outs(i):
                 copy.start()
 
@@ -359,11 +364,11 @@
                 send_image(i - 1)
 
             for turn, actions in enumerate((
-                (lambda: start_other(1), lambda: start_own(2)),
+                (lambda: start_own(2),),
                 (lambda: hand_on(0, 0, 1),),
                 (lambda: hand_on(1, 0, 0),),
                 (lambda: hand_on(0, 0, 2),),
-                (lambda: hand_on(1, 1, 0), lambda: start_own(3)),
+                (lambda: hand_on(1, 0, 1), lambda: start_own(3)),
             )):
                 @pl.when(i == turn)
                 def _():
@@ -386,6 +391,8 @@
         pltpu.VMEM((images, PAD, D), BF16),
         pltpu.VMEM((images, PAD, D), F32),
         pltpu.VMEM((images, PAD, D), BF16),
+        pltpu.VMEM((images, D, PAD), BF16),
+        pltpu.VMEM((images, D, PAD), BF16),
     )
     g_over = g_all.at[over_s]
     remote(g_over, g_over, g_sem.at[2], g_sem.at[3], over).wait()
@@ -394,25 +401,23 @@
     remote(g_mate, g_mate, g_sem.at[0], g_sem.at[1], mate).wait()
     g_corner = g_all.at[corner_s]
     remote(g_corner, g_corner, g_sem.at[4], g_sem.at[5], mate).wait()
-    g_copy.wait()
-    own_copy.wait()
 
     def slot_of(e):
         return e % 2 if e < local - 1 else 2
 
     def cross_sum(e, k):
         return remote(
-            gst.at[slot_of(e), k, pl.ds(lines, lines)], xr.at[e // 2, k],
-            rx_send.at[e // 2, k], rx_recv.at[e // 2, k], beside,
+            gst.at[slot_of(e), k, pl.ds(lines, lines)], xr.at[e % 2, k],
+            rx_send.at[e % 2, k], rx_recv.at[e % 2, k], beside,
         )
 
     def swap(e, k):
-        return remote(xst.at[k], xo.at[e // 2, k], ro_send.at[e // 2, k], ro_recv.at[e // 2, k], beside)
+        return remote(xst.at[k], xo.at[e % 2, k], ro_send.at[e % 2, k], ro_recv.at[e % 2, k], beside)
 
     def partial(e, k, owner, which):
         value = gst[slot_of(e), k, which * lines + owner].astype(F32)
         if e not in SUM_FIRST:
-            value = value + xr[e // 2, k, owner].astype(F32)
+            value = value + xr[e % 2, k, owner].astype(F32)
         return value
 
     def z_send(e, k, way, hop):
@@ -515,7 +520,7 @@
 
     def collect(e, k):
         swap(e, k).wait()
-        fin[k] += xo[e // 2, k].astype(F32)
+        fin[k] += xo[e % 2, k].astype(F32)
         to_result(e, k).start()
 
     def source_of(e, t):
@@ -524,14 +529,28 @@
         return across_y * CORES + (1 - core) + (r % CORES) * (2 * core - 1)
 
     def experts(ubuf, gbuf, work, x_t, m_t, dacc, made_all, d_stage):
-        def load(s):
-            return (
-                pltpu.make_async_copy(u_all.at[s], ubuf.at[:, sent_images], load_sem.at[0]),
-                pltpu.make_async_copy(g_all.at[s], gbuf.at[:, sent_images], load_sem.at[1]),
-            )
+        def load_u(s):
+            return pltpu.make_async_copy(u_all.at[s], ubuf.at[:, sent_images], load_sem.at[0])
+
+        def load_g(ref):
+            return pltpu.make_async_copy(ref, gbuf.at[:, sent_images], load_sem.at[1])
+
+        def start_load(s):
+            load_u(s).start()
+
+            @pl.when(s == me)
+            def _():
+                load_g(g_own).start()
+
+            @pl.when(s != me)
+            def _():
+                load_g(g_all.at[s]).start()
 
         def load_weights(e):
-            return pltpu.make_async_copy(wfull.at[e], gst.at[2], w_sem)
+            copies = [pltpu.make_async_copy(expw.at[e], gst.at[2, :, dp], w_sem.at[0])]
+            for k, d in enumerate(sources):
+                copies.append(pltpu.make_async_copy(wfull.at[e, :, d], gst.at[2, :, d], w_sem.at[k + 1]))
+            return copies
 
         def weight_grad(e, k):
             left = x_t if k == 0 else m_t
@@ -556,8 +575,8 @@
 
         def one_source(e, t, after_gather):
             s = source_of(e, t)
-            for copy in load(s):
-                copy.wait()
+            load_u(s).wait()
+            load_g(g_own).wait()
             arrived = jnp.zeros((slots, D), F32)
             grad = jnp.zeros((slots, D), F32)
             share = jnp.zeros((slots, 1), F32)
@@ -621,14 +640,12 @@
                         for i in range(images):
                             u_to(2, corner_s, i, mate).wait()
 
-                for copy in load(source_of(e, t + 1)):
-                    copy.start()
+                start_load(source_of(e, t + 1))
 
             if e + 1 < local:
                 @pl.when(t + 1 == group)
                 def _():
-                    for copy in load(source_of(e + 1, 0)):
-                        copy.start()
+                    start_load(source_of(e + 1, 0))
 
         def to_corner():
             return remote(d_stage.at[0], d_corner, back_send.at[0], back_recv.at[0], mate)
@@ -654,41 +671,40 @@
             to_over().start()
 
         plan = {
-            (0, 0): (lambda: hand_on(1, 0, 1),),
-            (0, 2): (lambda: hand_on(1, 1, 1),),
-            (1, 0): (lambda: hand_on(2, 0, 1), lambda: hop_step(0, 1, 1)),
-            (1, 1): (lambda: hop_step(0, 0, 2),),
-            (1, 2): (lambda: hand_on(2, 0, 2),),
-            (1, 3): (lambda: hop_step(0, 1, 2),),
-            (2, 0): (lambda: hand_on(3, 0, 1), lambda: collect(0, 0)),
-            (2, 1): (lambda: collect(0, 1),),
-            (2, 2): (lambda: hand_on(3, 0, 2),),
-            (3, 0): (sums_corner, lambda: hop_step(2, 0, 1)),
-            (3, 1): (lambda: hop_step(2, 1, 1),),
-            (3, 2): (sums_mate, lambda: hop_step(2, 0, 2)),
-            (3, 3): (lambda: hop_step(2, 1, 2),),
+            (0, 0): (lambda: hand_on(1, 0, 2),),
+            (0, 1): (lambda: hand_on(2, 0, 0),),
+            (0, 3): (lambda: hand_on(2, 0, 1),),
+            (1, 0): (lambda: hand_on(2, 0, 2), lambda: hand_on(3, 0, 0)),
+            (1, 1): (lambda: hop_step(0, 0, 1),),
+            (1, 2): (lambda: hand_on(3, 0, 1),),
+            (1, 3): (lambda: hop_step(0, 1, 1), lambda: hand_on(3, 0, 2)),
+            (2, 0): (lambda: hop_step(0, 1, 2),),
+            (2, 1): (lambda: finish(0, 0),),
+            (2, 2): (lambda: finish(0, 1), lambda: hop_step(1, 0, 0)),
+            (2, 3): (lambda: hop_step(1, 1, 0),),
+            (3, 0): (sums_corner, lambda: collect(0, 0), lambda: collect(0, 1)),
+            (3, 1): (lambda: hop_step(1, 0, 1),),
+            (3, 2): (sums_mate, lambda: hop_step(1, 1, 1)),
+            (3, 3): (lambda: hop_step(1, 0, 2),),
         }
         after_grad = {
             (0, 0): (lambda: hop_step(0, 0, 0),),
-            (0, 1): (lambda: hop_step(0, 1, 0), lambda: hand_on(1, 0, 2), lambda: hand_on(1, 1, 2),
-                     lambda: hand_on(2, 0, 0), lambda: hop_step(0, 0, 1)),
-            (1, 0): (lambda: finish(0, 0),),
-            (1, 1): (lambda: finish(0, 1), lambda: hand_on(3, 0, 0)),
-            (2, 0): (lambda: hop_step(2, 0, 0),),
-            (2, 1): (lambda: hop_step(2, 1, 0),),
-            (3, 0): (lambda: finish(2, 0),),
-            (3, 1): (lambda: finish(2, 1),),
+            (0, 1): (lambda: hop_step(0, 1, 0),),
+            (1, 1): (lambda: hop_step(0, 0, 2),),
+            (3, 1): (lambda: hop_step(1, 1, 2),),
         }
 
         empty = jnp.zeros((images, PAD - SENT, D), BF16)
         ubuf[:, SENT:, :] = empty
         gbuf[:, SENT:, :] = empty
-        for copy in load(source_of(0, 0)):
-            copy.start()
+        start_load(source_of(0, 0))
         for e in range(local):
             weights_here(e)
-            load_weights(e).start()
-            load_weights(e).wait()
+            copies = load_weights(e)
+            for copy in copies:
+                copy.start()
+            for copy in copies:
+                copy.wait()
 
             def step(t, carry, e=e):
                 one_source(e, t, lambda: next_load(e, t))
@@ -708,7 +724,8 @@
                 for action in after_grad.get((e, k), ()):
                     action()
 
-        pltpu.make_async_copy(dacc.at[me], own_out.at[0], own_sem.at[2]).start()
+        own_sum = pltpu.make_async_copy(dacc.at[me], own_out, own_sem.at[2])
+        own_sum.start()
 
         def one_sum(s, i):
             total = jnp.zeros((PAD, D), F32)
@@ -728,10 +745,11 @@
             stage(k).wait()
             remote(y_stage.at[k], y_got.at[k], y_send.at[k], y_recv.at[k], partner).start()
         for i in range(images):
-            dacc[corner_s, i * SENT : (i + 1) * SENT] = one_sum(me, i)
-        pltpu.make_async_copy(dacc.at[corner_s], own_out.at[1], own_sem.at[4]).start()
-        pltpu.make_async_copy(dacc.at[corner_s], own_out.at[1], own_sem.at[4]).wait()
-        pltpu.make_async_copy(dacc.at[me], own_out.at[0], own_sem.at[2]).wait()
+            d_stage[0, i * SENT : (i + 1) * SENT] = one_sum(me, i).astype(BF16)
+        last_stage = pltpu.make_async_copy(d_stage.at[0], y_stage.at[3], own_sem.at[3])
+        last_stage.start()
+        last_stage.wait()
+        own_sum.wait()
 
     count_rows = images * SENT
     pl.run_scoped(
@@ -754,14 +772,14 @@
     kept_y, given_y = rows_of(y * quarter, quarter), rows_of((1 - y) * quarter, quarter)
     final_rows = rows_of(core * half + y * quarter, quarter)
 
-    def backward(g_low, g_mid, d_att, v_fetch):
+    def backward(g_low, g_mid, d_att):
         v_sum[...] = jnp.zeros_like(v_sum)
 
         def before_attention(cot_v, mid_v, own_v, mate_v, over_v):
             fetches = [
                 pltpu.make_async_copy(source, target, in_sem.at[n])
                 for n, (source, target) in enumerate((
-                    (cot, cot_v), (middle, mid_v), (own_out.at[0], own_v), (d_mate, mate_v), (d_over, over_v),
+                    (cot, cot_v), (middle, mid_v), (own_out, own_v), (d_mate, mate_v), (d_over, over_v),
                 ))
             ]
             for fetch in fetches:
@@ -796,7 +814,7 @@
         )
 
         def through_attention(
-            tok_v, qkv_v, att_v, dqkv, lowered, part_own, sum_a, sum_b, sum_c, sum_d, gt_v, old_v, new_v
+            tok_v, qkv_v, att_tv, low_tv, dqkv, part_own, sum_a, sum_b, sum_c, sum_d, gt_v, old_v, got_v,
         ):
             def move_a(p):
                 return remote(part_own.at[p, :, theirs], part_a.at[p], a_sem.at[p, 0], a_sem.at[p, 1], mate)
@@ -858,15 +876,34 @@
                 for k in range(3):
                     move_e(p, k).wait()
 
-            def scatter_part(p, left, right):
-                block = contract_rows(left, right).astype(BF16)
-                part_own[p] = block.reshape(shards, rows, D)
+            def scatter_part(p, left_t, right):
+                block = jnp.zeros((D, D), F32)
+                for i in range(images):
+                    block += dot(left_t[i], right(i))
+                part_own[p] = block.astype(BF16).reshape(shards, rows, D)
                 move_a(p).start()
+
+            def block_output():
+                for k, partner in enumerate(partners):
+                    remote(y_stage.at[k], y_got.at[k], y_send.at[k], y_recv.at[k], partner).wait()
+                fetch_output.wait()
+                for k in range(4):
+                    source = y_stage.at[3] if k == 3 else y_got.at[k]
+                    landed = pltpu.make_async_copy(source, got_v, in_sem.at[3])
+                    landed.start()
+                    landed.wait()
+                    for i in range(images):
+                        part = got_v[i * SENT : (i + 1) * SENT].astype(F32)
+                        if k < 3:
+                            g_mid[i, :SENT] += part
+                        else:
+                            g_low[i, :SENT] = (g_mid[i, :SENT] + part).astype(BF16)
+                pltpu.make_async_copy(g_low, mixed, in_sem.at[5]).start()
 
             fetches = [
                 pltpu.make_async_copy(source, target, in_sem.at[n])
                 for n, (source, target) in enumerate((
-                    (tok, tok_v), (qkv, qkv_v), (att, att_v),
+                    (tok, tok_v), (qkv, qkv_v), (att_t, att_tv), (low_t, low_tv),
                     (attn_old, old_v.at[0]), (first_old, old_v.at[1]), (second_old, old_v.at[2]),
                 ))
             ]
@@ -874,7 +911,13 @@
                 fetch.start()
             for fetch in fetches:
                 fetch.wait()
-            scatter_part(3, att_v[...].reshape(images * PAD, D), g_low[...].reshape(images * PAD, D))
+            finish(1, 0)
+            finish(1, 1)
+            hop_step(2, 0, 0)
+            hop_step(2, 1, 0)
+            scatter_part(3, att_tv, lambda i: g_low[i])
+
+            key_index = lax.broadcasted_iota(jnp.int32, (PAD, PAD), 0)
 
             def result(i):
                 return pltpu.make_async_copy(gt_v.at[i], grad_tok.at[i], out_sem.at[i, 0])
@@ -888,15 +931,22 @@
                     grad = d_att[i, :, offset : offset + 128]
                     results = []
                     for which in range(2):
-                        probs = softmax_rows(query, key_rows, which, pair_lane)
-                        grad_own = jnp.where(pair_lane // HEAD_DIM == which, grad, jnp.zeros_like(grad))
-                        grad_probs = contract_last(grad_own, value)
-                        inner = jnp.sum(probs * grad_probs, axis=-1, keepdims=True)
+                        own_half = pair_lane // HEAD_DIM == which
+                        scores = contract_last(
+                            jnp.where(own_half, key_rows, jnp.zeros_like(key_rows)), query
+                        ) * HEAD_DIM ** (-0.5)
+                        scores = jnp.where(key_index < SEQ, scores, -1e30)
+                        powers = jnp.exp(scores - jnp.max(scores, axis=0, keepdims=True))
+                        probs = powers * (1.0 / jnp.sum(powers, axis=0, keepdims=True))
+                        grad_probs = contract_last(
+                            jnp.where(own_half, value, jnp.zeros_like(value)), grad
+                        )
+                        inner = jnp.sum(probs * grad_probs, axis=0, keepdims=True)
                         grad_scores = (probs * (grad_probs - inner)).astype(BF16)
                         results.append((
-                            dot(grad_scores, key_rows) * HEAD_DIM ** (-0.5),
-                            contract_rows(grad_scores, query) * HEAD_DIM ** (-0.5),
-                            contract_rows(probs.astype(BF16), grad),
+                            contract_rows(grad_scores, key_rows) * HEAD_DIM ** (-0.5),
+                            dot(grad_scores, query) * HEAD_DIM ** (-0.5),
+                            dot(probs.astype(BF16), grad),
                         ))
                     for part in range(3):
                         joined = jnp.where(pair_lane < HEAD_DIM, results[0][part], results[1][part])
@@ -906,17 +956,17 @@
                     columns = pl.ds(part * D, D)
                     grad += contract_last(dqkv[i, :, columns], attnw[:, :, columns].reshape(D, D))
                 normed, inverse = normalize(tok_v[i].astype(F32))
-                lowered[i] = (normed * gain_one + shift_one).astype(BF16)
                 v_sum[0:1] += jnp.sum(grad * normed, axis=0, keepdims=True)
                 v_sum[1:2] += jnp.sum(grad, axis=0, keepdims=True)
                 gt_v[i] = (g_mid[i] + norm_back(grad * gain_one, normed, inverse)).astype(BF16)
                 result(i).start()
                 for turn, actions in enumerate((
-                    (lambda: stage_b(3), lambda: collect(2, 0), lambda: collect(2, 1), lambda: hop_step(1, 0, 0)),
-                    (lambda: stage_c(3), lambda: hop_step(1, 1, 0), lambda: hop_step(1, 0, 1)),
-                    (lambda: stage_d(3), lambda: hop_step(1, 1, 1), lambda: hop_step(1, 0, 2)),
-                    (lambda: stage_e(3), lambda: hop_step(1, 1, 2), lambda: finish(1, 0)),
-                    (lambda: finish(1, 1), lambda: hop_step(3, 0, 0)),
+                    (lambda: stage_b(3), lambda: hop_step(2, 0, 1), lambda: hop_step(2, 1, 1)),
+                    (lambda: stage_c(3), lambda: collect(1, 0), lambda: collect(1, 1),
+                     lambda: hop_step(2, 0, 2), lambda: hop_step(2, 1, 2)),
+                    (lambda: stage_d(3), lambda: finish(2, 0), lambda: finish(2, 1), lambda: hop_step(3, 0, 0)),
+                    (lambda: stage_e(3), lambda: hop_step(3, 1, 0), lambda: hop_step(3, 0, 1)),
+                    (lambda: hop_step(3, 1, 1), lambda: hop_step(3, 0, 2)),
                 )):
                     @pl.when(i == turn)
                     def _():
@@ -930,17 +980,16 @@
             def v_move(n, partner):
                 return remote(v_stage.at[n], v_got.at[n], v_sem.at[n, 0], v_sem.at[n, 1], partner)
 
+            fetch_output = pltpu.make_async_copy(middle, g_mid, in_sem.at[6])
+            fetch_output.start()
             v_stage[0] = v_sum[...]
             v_move(0, mate).start()
             for p in range(3):
-                scatter_part(
-                    p, lowered[...].reshape(images * PAD, D),
-                    dqkv[:, :, p * D : (p + 1) * D].reshape(images * PAD, D),
-                )
+                scatter_part(p, low_tv, lambda i: dqkv[i, :, p * D : (p + 1) * D])
             tail = {
-                0: (lambda: hop_step(3, 0, 1),),
-                1: (lambda: hop_step(3, 1, 0), lambda: hop_step(3, 0, 2)),
-                2: (lambda: hop_step(3, 1, 1), lambda: finish(3, 0)),
+                0: (lambda: hop_step(3, 1, 2), block_output),
+                1: (lambda: finish(3, 0),),
+                2: (lambda: finish(3, 1),),
             }
             for n, stage in enumerate((stage_b, stage_c, stage_d)):
                 for p in range(3):
@@ -960,7 +1009,6 @@
                     action()
             for p in range(3):
                 stage_e(p)
-            hop_step(3, 1, 2)
             for k in range(1, lines):
                 source = lax.rem(z + lines - k, lines)
                 remote(
@@ -987,9 +1035,9 @@
                     0.03, 0.1,
                 )
                 for n in range(3):
-                    new_v[n, :, columns] = new[n]
+                    old_v[n, :, columns] = new[n]
             results = [
-                pltpu.make_async_copy(new_v.at[n], target, in_sem.at[n])
+                pltpu.make_async_copy(old_v.at[n], target, in_sem.at[n])
                 for n, target in enumerate((attn_new, first_new, second_new))
             ]
             for copy in results:
@@ -998,14 +1046,15 @@
                 copy.wait()
             for i in range(images):
                 result(i).wait()
+            pltpu.make_async_copy(g_low, mixed, in_sem.at[5]).wait()
 
         pl.run_scoped(
             through_attention,
             pltpu.VMEM((images, PAD, D), BF16),
             pltpu.VMEM((images, PAD, 3 * D), BF16),
-            pltpu.VMEM((images, PAD, D), BF16),
+            pltpu.VMEM((images, D, PAD), BF16),
+            pltpu.VMEM((images, D, PAD), BF16),
             pltpu.VMEM((images, PAD, 3 * D), BF16),
-            pltpu.VMEM((images, PAD, D), BF16),
             pltpu.VMEM((4, shards, rows, D), BF16),
             pltpu.VMEM((4, shards, half, D), BF16),
             pltpu.VMEM((4, lines, COLUMNS, quarter, D), BF16),
@@ -1013,7 +1062,7 @@
             pltpu.VMEM((4, lines, quarter, D), F32),
             pltpu.VMEM((images, PAD, D), BF16),
             pltpu.VMEM((3, rows, 4 * D), F32),
-            pltpu.VMEM((3, rows, 4 * D), F32),
+            pltpu.VMEM((count_rows, D), BF16),
         )
 
     pl.run_scoped(
@@ -1021,38 +1070,8 @@
         pltpu.VMEM((images, PAD, D), BF16),
         pltpu.VMEM((images, PAD, D), F32),
         pltpu.VMEM((images, PAD, D), BF16),
-        pltpu.VMEM((8, 128), F32),
-    )
-
-    def output(mid_v, own_v, got_v, out_v):
-        for k, partner in enumerate(partners):
-            remote(y_stage.at[k], y_got.at[k], y_send.at[k], y_recv.at[k], partner).wait()
-        fetches = [
-            pltpu.make_async_copy(source, target, in_sem.at[n])
-            for n, (source, target) in enumerate(((middle, mid_v), (own_out.at[1], own_v), (y_got, got_v)))
-        ]
-        for fetch in fetches:
-            fetch.start()
-        for fetch in fetches:
-            fetch.wait()
-        for i in range(images):
-            here = pl.ds(i * SENT, SENT)
-            returned = own_v[here]
-            for k in range(3):
-                returned = returned + got_v[k, here].astype(F32)
-            out_v[i, :SENT] = (mid_v[i, :SENT] + returned).astype(BF16)
-        copy = pltpu.make_async_copy(out_v, mixed, in_sem.at[3])
-        copy.start()
-        copy.wait()
-
-    pl.run_scoped(
-        output,
-        pltpu.VMEM((images, PAD, D), F32),
-        pltpu.VMEM((count_rows, D), F32),
-        pltpu.VMEM((3, count_rows, D), BF16),
-        pltpu.VMEM((images, PAD, D), BF16),
-    )
-    finish(3, 1)
+    )
+
     to_mate.wait_send()
     for e in range(local):
         settle_weights(e)
@@ -1063,7 +1082,7 @@
         to_result(3, k).wait()
 
 
-def block(shards, capacity, route, comb, attn, vec, tok, cot, expw, attn_state, vec_state, group):
+def block(shards, capacity, route, comb, attn, tok, cot, expw, attn_state, vec_state, group):
     lines = shards // COLUMNS
     images = tok.shape[0]
     local, _, rows, ff = expw.shape
@@ -1087,20 +1106,23 @@
             shape((local, 2, shards, rows, ff), BF16),
             shape((images, PAD, D), F32),
             shape((images, PAD, 3 * D), BF16),
-            shape((images, PAD, D), BF16),
-            shape((2, count_rows, D), F32),
+            shape((images, D, PAD), BF16),
+            shape((images, D, PAD), BF16),
+            shape((count_rows, D), F32),
             shape((count_rows, D), BF16),
             shape((count_rows, D), BF16),
             shape((count_rows, D), BF16),
-            shape((3, count_rows, D), BF16),
+            shape((4, count_rows, D), BF16),
             shape((3, count_rows, D), BF16),
             shape((local, 2, rows, ff), F32),
             shape((images, PAD, D), BF16),
             shape((images, PAD, D), BF16),
         ] + attn_states,
-        in_specs=[vm] * 7 + [hbm] * 6,
-        out_specs=[vm] * 3 + [hbm] * 18,
+        in_specs=[vm] * 6 + [hbm] * 6,
+        out_specs=[vm] * 3 + [hbm] * 19,
         scratch_shapes=[
+            pltpu.VMEM(attn.shape, BF16),
+            pltpu.VMEM((8, 128), F32),
             pltpu.VMEM((shards,) + attn.shape, BF16),
             pltpu.VMEM((group, 8, wide), jnp.int32),
             pltpu.VMEM((group, 8, wide), F32),
@@ -1129,7 +1151,7 @@
             dma((6,)), dma((images, 3)), dma((images, 3)), dma((5,)),
             dma((2 * local, lines)), dma((2 * local, lines)), dma((2 * local, lines)), dma((2 * local, lines)),
             dma((local, lines)), dma((local, lines)),
-            dma((images, 4)), dma((6,)), dma((3,)), dma(()), dma((2,)),
+            dma((images, 5)), dma((8,)), dma((3,)), dma((shards,)), dma((2,)),
             dma((2, 2)), dma((2, 2)), dma((2, 2)), dma((2, 2)),
             dma((2,)), dma((2, last)), dma((2,)), dma((2, last)),
             regular((2,)), regular((2,)),
@@ -1140,8 +1162,8 @@
         compiler_params=pltpu.CompilerParams(
             collective_id=0, has_side_effects=True, vmem_limit_bytes=VMEM_LIMIT
         ),
-    )(route, comb, attn, vec, *vec_state, tok, cot, expw, *attn_state)
-    vec_new, grads, mixed, grad_tok, attn_new = outs[:3], outs[15], outs[16], outs[17], outs[18:]
+    )(route, comb, attn, *vec_state, tok, cot, expw, *attn_state)
+    vec_new, grads, mixed, grad_tok, attn_new = outs[:3], outs[16], outs[17], outs[18], outs[19:]
     return mixed, grad_tok, grads, attn_new, vec_new
 
 
@@ -1169,17 +1191,14 @@
         count = tokens.shape[0]
         experts = expert_master.shape[2] * group
         capacity = max(2, 4 * count // experts)
-        width = vector_master.shape[1]
-        vec = jnp.pad(vector_master, ((0, 8 - vector_master.shape[0]), (0, 128 - width)))
         shard = jnp.transpose(expert_master.astype(BF16), (2, 1, 0, 3))
         mixed, grad_tokens, grads, attn_new, vec_new = block(
-            shards, capacity, as_lanes(routes, -1), as_lanes(combine, 0.0), attn_master.astype(BF16), vec,
+            shards, capacity, as_lanes(routes, -1), as_lanes(combine, 0.0), attn_master,
             by_image(tokens), by_image(cotangent), shard,
             [attn_master, attn_first, attn_second], [vector_master, vector_first, vector_second], group,
         )
-        expert_new = adam_update(
-            expert_master, expert_first, expert_second, jnp.transpose(grads, (2, 1, 0, 3)), 0.02, 0.1
-        )
+        gradient = with_layout_constraint(jnp.transpose(grads, (2, 1, 0, 3)), Layout((0, 1, 2, 3)))
+        expert_new = adam_update(expert_master, expert_first, expert_second, gradient, 0.02, 0.1)
         return (to_tokens(mixed, count), to_tokens(grad_tokens, count), *attn_new, *vec_new, *expert_new)
 
     return run

time: 517 us -> 421 us (0.81)
  Pallas kernels: 455 us -> 374 us
  local copies, waits for them, and re-layouts: 36.3 us -> 20.9 us
    pallas_call x1, Pallas kernels: 455 us -> 374 us  [block(): pl.pallas_call(functools.partial(block_kernel, shards, lines, slots), out...]
    unnamed x30 -> x27, local copies, waits for them, and re-layouts: 25.3 us -> 11.2 us
where the time goes in v3:
time: 421 us; the launch traced here: 413 us
  Pallas kernels  374 us (89%)
  local copies, waits for them, and re-layouts  20.9 us (5%)
  other arithmetic  16.3 us (4%)
    pallas_call x1, Pallas kernels, block(): pl.pallas_call(functools.partial(block_kernel, shards, lines, slots), out...  374 us
    sub x1, other arithmetic, adam_update(): master - step_rate * (first_hat / (jnp.sqrt(second_hat) + ADAM_EPS) + dec...  16.3 us
    unnamed x27, local copies, waits for them, and re-layouts  11.2 us

profile of v3, /device:TPU:0, one launch (start us, length us, event | category | flops | bytes accessed | tf_op | source)
XLA Modules:
  0.0 412.6 jit_solution(12898124755775687083)
XLA Ops:
  0.7 0.9 reshape.46
  1.5 0.8 reshape.48
  2.3 0.6 copy.33
  2.9 0.6 copy.32
  3.6 1.5 reshape.50
  5.1 1.2 pad.17.tok
  6.3 0.3 reshape.51
  6.5 1.2 pad.18.cot
  7.7 5.7 %copy.41 = bf16[64,2,4,2048]{3,0,1,2:T(8,128)(2,1)} copy(f32[64,2,4,2048]{3,2,1,0:T(4,128)} %param.23) | data formatting | bytes 6291456 | tf_op args[10]
  13.5 374.3 %shard_map.212 = (f32[5,64]{1,0:T(8,128)}, f32[5,64]{1,0:T(8,128)}, f32[5,64]{1,0:T(8,128)}, bf16[4,5,208,512]{3,2,1,0:T(8,128)(2,1)}, bf16[4,5,208,512]{3,2,1,0...) custom-call(s32[8,1280]{1,0:T(8,128)} %bitcast.20, ...), custom_call_target="tpu_custom_call" | custom-call | tf_op jit(solution)/shard_map/pallas_call | solution.py:1101
  387.7 1.4 slice.6
  389.1 1.2 reshape.52
  390.4 0.0 copy-done.1
  390.4 0.1 slice.7
  390.5 1.2 reshape.53
  391.7 16.3 %multiply_subtract_fusion = (f32[64,2,4,2048]{3,2,1,0:T(4,128)}, f32[64,2,4,2048]{3,2,1,0:T(4,128)}, f32[64,2,4,2048]{3,2,1,0:T(4,128)}) fusion(f32[64,2,4,2048]{3,2,1,0:T(4,128)} %param.23, f32[4,2,64,2048]{3,2,1,0:T(8,128)} %get-tuple-element.28, f32[64,2,4,2048]{3,2,1,0:T(4,128)} %param.24, f32[64,2,4,2048]{3,2,1,0:T(4,128)} %param.25), kind=kLoop, calls=%fused_computation.5 | loop fusion | flops 15728640 | bytes 29360128 | tf_op jit(solution)/shard_map/sub | solution.py:107
  408.0 0.8 copy.48
  408.8 0.0 copy-done.3
  408.8 0.8 copy.49
  409.6 0.8 copy.50
  410.4 0.6 copy.51
  411.0 0.0 copy-done.6
  411.0 0.6 copy.52
  411.6 0.6 copy.53
  (15 shorter events, 0.0 us)
Async XLA Ops:
  0.6 5.6 %copy-start = (bf16[985,512]{1,0:T(8,128)(2,1)S(1)}, bf16[985,512]{1,0:T(8,128)(2,1)}, u32[]{:S(2)}) copy-start(bf16[985,512]{1,0:T(8,128)(2,1)} %param.14) | copy-start | bytes 3025924
  387.7 2.6 copy-start.1
  391.7 16.3 %copy-start.4 = (f32[64,2048]{1,0:T(8,128)S(1)}, f32[64,2048]{1,0:T(8,128)}, u32[]{:S(2)}) copy-start(f32[64,2048]{1,0:T(8,128)} %get-tuple-element.45) | copy-start | bytes 1572868
  391.7 17.1 %copy-start.3 = (f32[64,2048]{1,0:T(8,128)S(1)}, f32[64,2048]{1,0:T(8,128)}, u32[]{:S(2)}) copy-start(f32[64,2048]{1,0:T(8,128)} %get-tuple-element.46) | copy-start | bytes 1572868
  391.7 17.9 %copy-start.2 = (f32[64,2048]{1,0:T(8,128)S(1)}, f32[64,2048]{1,0:T(8,128)}, u32[]{:S(2)}) copy-start(f32[64,2048]{1,0:T(8,128)} %get-tuple-element.47) | copy-start | bytes 1572868
  391.7 18.7 %copy-start.7 = (f32[5,64]{1,0:T(8,128)S(1)}, f32[5,64]{1,0:T(8,128)}, u32[]{:S(2)}) copy-start(f32[5,64]{1,0:T(8,128)} %get-tuple-element.48) | copy-start | bytes 3844
  391.7 19.3 %copy-start.6 = (f32[5,64]{1,0:T(8,128)S(1)}, f32[5,64]{1,0:T(8,128)}, u32[]{:S(2)}) copy-start(f32[5,64]{1,0:T(8,128)} %get-tuple-element.49) | copy-start | bytes 3844
  391.7 19.9 %copy-start.5 = (f32[5,64]{1,0:T(8,128)S(1)}, f32[5,64]{1,0:T(8,128)}, u32[]{:S(2)}) copy-start(f32[5,64]{1,0:T(8,128)} %get-tuple-element.50) | copy-start | bytes 3844

commit v4 on v3

--- a/solution.py
+++ b/solution.py
@@ -4,7 +4,6 @@
 import jax.numpy as jnp
 from jax import lax
 from jax.experimental import pallas as pl
-from jax.experimental.layout import Layout, with_layout_constraint
 from jax.experimental.pallas import tpu as pltpu
 from jax.sharding import PartitionSpec as P
 
@@ -117,12 +116,12 @@
 
 def block_kernel(
     shards, lines, slots,
-    route, comb, attn_f, vec_old, vec_first_old, vec_second_old,
-    tok, cot, expw, attn_old, first_old, second_old,
+    route, comb, vec_old, vec_first_old, vec_second_old,
+    tok, cot, expw, attn_old,
     vec_new, vec_first_new, vec_second_new,
-    u_all, g_all, wfull, middle, qkv, att_t, low_t, own_out, d_mate, d_corner, d_over, y_stage, y_got,
-    grads, mixed, grad_tok, attn_new, first_new, second_new,
-    attn, vec, attnw, route_all, comb_all, vslots, chosen, place, shares,
+    u_all, g_all, wfull, middle, qkv, att_t, low_t, attn_full, own_out, d_mate, d_corner, d_over, y_stage, y_got,
+    grads, mixed, grad_tok, attn_grad,
+    attn, vec, route_all, comb_all, vslots, chosen, place, shares,
     gst, xr, xo, xst, zr, zs, fin,
     part_a, part_b, part_c, part_d, whole, v_sum, v_stage, v_got, v_lines,
     attn_send, attn_recv, vec_send, vec_recv, pass_sem, table_send, table_recv,
@@ -150,16 +149,19 @@
     peers = [(lax.rem(dp + k, shards), me) for k in range(1, shards)]
     sources = [lax.rem(dp + shards - k, shards) for k in range(1, shards)]
     partners = (mate, over, corner)
+    early = pltpu.make_async_copy(attn_old, whole, in_sem.at[0])
+    early.start()
     greet(peers + list(partners))
+    early.wait()
     mine = pl.ds(pl.multiple_of(core * half, half), half)
     theirs = pl.ds(pl.multiple_of((1 - core) * half, half), half)
     sent_images = pl.ds(0, SENT)
 
-    attn[...] = attn_f[...].astype(BF16)
+    attn[...] = whole[...].astype(BF16)
     vec[...] = jnp.zeros_like(vec)
     vec[: vec_old.shape[0], : vec_old.shape[1]] = vec_old[...]
     for k, peer in enumerate(peers):
-        remote(attn.at[mine], attnw.at[dp, mine], attn_send.at[k], attn_recv.at[dp], peer).start()
+        remote(attn.at[mine], gst.at[1, 0, dp, mine], attn_send.at[k], attn_recv.at[dp], peer).start()
         remote(vec, vslots.at[dp], vec_send.at[k], vec_recv.at[dp], peer).start()
     for k, partner in enumerate(partners):
         remote(route, route_all.at[me], table_send.at[k, 0], table_recv.at[me, 0], partner).start()
@@ -261,7 +263,7 @@
     remote(g_own, g_mine, g_sem.at[0], g_sem.at[1], mate).start()
     remote(g_own, g_mine, g_sem.at[2], g_sem.at[3], over).start()
 
-    attnw[dp, mine] = attn[mine]
+    gst[1, 0, dp, mine] = attn[mine]
     vslots[dp] = vec[...]
     route_all[me] = route[...]
     comb_all[me] = comb[...]
@@ -291,9 +293,9 @@
         count = count + jnp.sum(block, axis=1, keepdims=True)
 
     for k, (peer, source) in enumerate(zip(peers, sources)):
-        remote(attn.at[mine], attnw.at[source, mine], attn_send.at[k], attn_recv.at[source], peer).wait()
+        remote(attn.at[mine], gst.at[1, 0, source, mine], attn_send.at[k], attn_recv.at[source], peer).wait()
         remote(vec, vslots.at[source], vec_send.at[k], vec_recv.at[source], peer).wait()
-    to_mate = remote(attnw.at[:, mine], attnw.at[:, mine], pass_sem.at[0], pass_sem.at[1], mate)
+    to_mate = remote(gst.at[1, 0, :, mine], gst.at[1, 0, :, mine], pass_sem.at[0], pass_sem.at[1], mate)
     to_mate.start()
     lane = lax.broadcasted_iota(jnp.int32, (128, D), 1)
     entry = lax.broadcasted_iota(jnp.int32, (128, D), 0)
@@ -304,7 +306,7 @@
         vectors = vectors + dot(vslots[d].astype(BF16), spread.astype(BF16))
     gain_one, shift_one = vectors[0:1], vectors[1:2]
     gain_two, shift_two, shift_out = vectors[2:3], vectors[3:4], vectors[4:5]
-    remote(attnw.at[:, theirs], attnw.at[:, theirs], pass_sem.at[0], pass_sem.at[1], mate).wait_recv()
+    remote(gst.at[1, 0, :, theirs], gst.at[1, 0, :, theirs], pass_sem.at[0], pass_sem.at[1], mate).wait_recv()
     pair_lane = lax.broadcasted_iota(jnp.int32, (PAD, 2 * HEAD_DIM), 1)
 
     def u_part(s, i):
@@ -338,7 +340,7 @@
             lowered = (normed * gain_one + shift_one).astype(BF16)
             for part in range(3):
                 columns = pl.ds(part * D, D)
-                qkv_v[i, :, columns] = dot(lowered, attnw[:, :, columns].reshape(D, D)).astype(BF16)
+                qkv_v[i, :, columns] = dot(lowered, gst[1, 0, :, :, columns].reshape(D, D)).astype(BF16)
             for pair in range(HEADS // 2):
                 offset = pair * 2 * HEAD_DIM
                 query = qkv_v[i, :, offset : offset + 128]
@@ -350,7 +352,7 @@
                     results.append(dot(probs.astype(BF16), value))
                 joined = jnp.where(pair_lane < HEAD_DIM, results[0], results[1])
                 att_v[i, :, offset : offset + 128] = joined.astype(BF16)
-            mid = inputs + dot(att_v[i], attnw[:, :, 3 * D :].reshape(D, D)) + shift_out
+            mid = inputs + dot(att_v[i], gst[1, 0, :, :, 3 * D :].reshape(D, D)) + shift_out
             mid_v[i] = mid
             normed_two, _ = normalize(mid)
             u_v[i] = (normed_two * gain_two + shift_two).astype(BF16)
@@ -394,6 +396,8 @@
         pltpu.VMEM((images, D, PAD), BF16),
         pltpu.VMEM((images, D, PAD), BF16),
     )
+    keep_attn = pltpu.make_async_copy(gst.at[1, 0], attn_full, own_sem.at[0])
+    keep_attn.start()
     g_over = g_all.at[over_s]
     remote(g_over, g_over, g_sem.at[2], g_sem.at[3], over).wait()
     remote(g_over, g_over, g_sem.at[4], g_sem.at[5], mate).start()
@@ -401,6 +405,9 @@
     remote(g_mate, g_mate, g_sem.at[0], g_sem.at[1], mate).wait()
     g_corner = g_all.at[corner_s]
     remote(g_corner, g_corner, g_sem.at[4], g_sem.at[5], mate).wait()
+
+    to_mate.wait_send()
+    keep_attn.wait()
 
     def slot_of(e):
         return e % 2 if e < local - 1 else 2
@@ -470,7 +477,7 @@
         one_hop(e, k, hop, 1)
 
     def to_result(e, k):
-        return pltpu.make_async_copy(fin.at[k], grads.at[e, k], fin_sem.at[k])
+        return pltpu.make_async_copy(fin.at[k], grads.at[:, k, e], fin_sem.at[k])
 
     def finish(e, k):
         turn = CHAINS.index(e)
@@ -654,7 +661,7 @@
             return remote(d_stage.at[1], d_mate, back_send.at[1], back_recv.at[1], mate)
 
         def to_over():
-            return remote(d_stage.at[2], d_over, back_send.at[2], back_recv.at[2], over)
+            return remote(d_stage.at[0], d_over, back_send.at[2], back_recv.at[2], over)
 
         def sums_corner():
             d_stage[0] = dacc[corner_s].astype(BF16)
@@ -663,11 +670,11 @@
         def sums_mate():
             d_stage[1] = dacc[mate_s].astype(BF16)
             to_mate_sum().start()
-            to_corner().wait_recv()
-            landed = pltpu.make_async_copy(d_corner, d_stage.at[2], load_sem.at[2])
+            to_corner().wait()
+            landed = pltpu.make_async_copy(d_corner, d_stage.at[0], load_sem.at[2])
             landed.start()
             landed.wait()
-            d_stage[2] = (dacc[over_s] + d_stage[2].astype(F32)).astype(BF16)
+            d_stage[0] = (dacc[over_s] + d_stage[0].astype(F32)).astype(BF16)
             to_over().start()
 
         plan = {
@@ -676,22 +683,19 @@
             (0, 3): (lambda: hand_on(2, 0, 1),),
             (1, 0): (lambda: hand_on(2, 0, 2), lambda: hand_on(3, 0, 0)),
             (1, 1): (lambda: hop_step(0, 0, 1),),
-            (1, 2): (lambda: hand_on(3, 0, 1),),
-            (1, 3): (lambda: hop_step(0, 1, 1), lambda: hand_on(3, 0, 2)),
-            (2, 0): (lambda: hop_step(0, 1, 2),),
-            (2, 1): (lambda: finish(0, 0),),
-            (2, 2): (lambda: finish(0, 1), lambda: hop_step(1, 0, 0)),
-            (2, 3): (lambda: hop_step(1, 1, 0),),
+            (1, 2): (lambda: hop_step(0, 1, 1), lambda: hand_on(3, 0, 1)),
+            (1, 3): (lambda: hand_on(3, 0, 2),),
+            (2, 1): (lambda: finish(0, 0), lambda: hop_step(1, 0, 0)),
+            (2, 2): (lambda: finish(0, 1), lambda: hop_step(1, 1, 0)),
             (3, 0): (sums_corner, lambda: collect(0, 0), lambda: collect(0, 1)),
-            (3, 1): (lambda: hop_step(1, 0, 1),),
-            (3, 2): (sums_mate, lambda: hop_step(1, 1, 1)),
-            (3, 3): (lambda: hop_step(1, 0, 2),),
+            (3, 2): (sums_mate, lambda: hop_step(1, 0, 2)),
+            (3, 3): (lambda: hop_step(1, 1, 2),),
         }
         after_grad = {
             (0, 0): (lambda: hop_step(0, 0, 0),),
             (0, 1): (lambda: hop_step(0, 1, 0),),
-            (1, 1): (lambda: hop_step(0, 0, 2),),
-            (3, 1): (lambda: hop_step(1, 1, 2),),
+            (1, 1): (lambda: hop_step(0, 0, 2), lambda: hop_step(0, 1, 2)),
+            (2, 1): (lambda: hop_step(1, 0, 1), lambda: hop_step(1, 1, 1)),
         }
 
         empty = jnp.zeros((images, PAD - SENT, D), BF16)
@@ -735,21 +739,22 @@
             return total[:SENT]
 
         def stage(k):
-            return pltpu.make_async_copy(d_stage.at[k], y_stage.at[k], own_sem.at[3])
+            return pltpu.make_async_copy(d_stage.at[1], y_stage.at[k], own_sem.at[3])
+
+        to_mate_sum().wait_send()
 
         for k, (s, partner) in enumerate(zip((mate_s, over_s, corner_s), partners)):
-            (to_corner, to_mate_sum, to_over)[k]().wait_send()
             for i in range(images):
-                d_stage[k, i * SENT : (i + 1) * SENT] = one_sum(s, i).astype(BF16)
+                d_stage[1, i * SENT : (i + 1) * SENT] = one_sum(s, i).astype(BF16)
             stage(k).start()
             stage(k).wait()
             remote(y_stage.at[k], y_got.at[k], y_send.at[k], y_recv.at[k], partner).start()
         for i in range(images):
-            d_stage[0, i * SENT : (i + 1) * SENT] = one_sum(me, i).astype(BF16)
-        last_stage = pltpu.make_async_copy(d_stage.at[0], y_stage.at[3], own_sem.at[3])
-        last_stage.start()
-        last_stage.wait()
+            d_stage[1, i * SENT : (i + 1) * SENT] = one_sum(me, i).astype(BF16)
+        stage(3).start()
+        stage(3).wait()
         own_sum.wait()
+        to_over().wait_send()
 
     count_rows = images * SENT
     pl.run_scoped(
@@ -761,10 +766,8 @@
         pltpu.VMEM((D, group * slots), BF16),
         pltpu.VMEM((group, count_rows, D), F32),
         pltpu.VMEM((group, local * slots, D), BF16),
-        pltpu.VMEM((3, count_rows, D), BF16),
-    )
-    remote(d_mate, d_mate, back_send.at[1], back_recv.at[1], mate).wait_recv()
-    remote(d_over, d_over, back_send.at[2], back_recv.at[2], over).wait_recv()
+        pltpu.VMEM((2, count_rows, D), BF16),
+    )
 
     def rows_of(start, size):
         return pl.ds(pl.multiple_of(start, quarter), size)
@@ -772,7 +775,15 @@
     kept_y, given_y = rows_of(y * quarter, quarter), rows_of((1 - y) * quarter, quarter)
     final_rows = rows_of(core * half + y * quarter, quarter)
 
-    def backward(g_low, g_mid, d_att):
+    def backward(g_low, g_mid, d_att, attnw):
+        fetch_attn = pltpu.make_async_copy(attn_full, attnw, own_sem.at[0])
+        fetch_attn.start()
+        for k in range(2):
+            finish(1, k)
+            hop_step(2, k, 0)
+        fetch_attn.wait()
+        remote(d_mate, d_mate, back_send.at[1], back_recv.at[1], mate).wait_recv()
+        remote(d_over, d_over, back_send.at[2], back_recv.at[2], over).wait_recv()
         v_sum[...] = jnp.zeros_like(v_sum)
 
         def before_attention(cot_v, mid_v, own_v, mate_v, over_v):
@@ -814,7 +825,7 @@
         )
 
         def through_attention(
-            tok_v, qkv_v, att_tv, low_tv, dqkv, part_own, sum_a, sum_b, sum_c, sum_d, gt_v, old_v, got_v,
+            tok_v, qkv_v, att_tv, low_tv, part_own, sum_a, sum_b, sum_c, sum_d, got_v,
         ):
             def move_a(p):
                 return remote(part_own.at[p, :, theirs], part_a.at[p], a_sem.at[p, 0], a_sem.at[p, 1], mate)
@@ -904,23 +915,20 @@
                 pltpu.make_async_copy(source, target, in_sem.at[n])
                 for n, (source, target) in enumerate((
                     (tok, tok_v), (qkv, qkv_v), (att_t, att_tv), (low_t, low_tv),
-                    (attn_old, old_v.at[0]), (first_old, old_v.at[1]), (second_old, old_v.at[2]),
                 ))
             ]
             for fetch in fetches:
                 fetch.start()
             for fetch in fetches:
                 fetch.wait()
-            finish(1, 0)
-            finish(1, 1)
-            hop_step(2, 0, 0)
-            hop_step(2, 1, 0)
+            hop_step(2, 0, 1)
+            hop_step(2, 1, 1)
             scatter_part(3, att_tv, lambda i: g_low[i])
 
             key_index = lax.broadcasted_iota(jnp.int32, (PAD, PAD), 0)
 
             def result(i):
-                return pltpu.make_async_copy(gt_v.at[i], grad_tok.at[i], out_sem.at[i, 0])
+                return pltpu.make_async_copy(tok_v.at[i], grad_tok.at[i], out_sem.at[i, 0])
 
             def one_image(i, carry):
                 for pair in range(HEADS // 2):
@@ -950,23 +958,22 @@
                         ))
                     for part in range(3):
                         joined = jnp.where(pair_lane < HEAD_DIM, results[0][part], results[1][part])
-                        dqkv[i, :, part * D + offset : part * D + offset + 128] = joined.astype(BF16)
+                        qkv_v[i, :, part * D + offset : part * D + offset + 128] = joined.astype(BF16)
                 grad = jnp.zeros((PAD, D), F32)
                 for part in range(3):
                     columns = pl.ds(part * D, D)
-                    grad += contract_last(dqkv[i, :, columns], attnw[:, :, columns].reshape(D, D))
+                    grad += contract_last(qkv_v[i, :, columns], attnw[:, :, columns].reshape(D, D))
                 normed, inverse = normalize(tok_v[i].astype(F32))
                 v_sum[0:1] += jnp.sum(grad * normed, axis=0, keepdims=True)
                 v_sum[1:2] += jnp.sum(grad, axis=0, keepdims=True)
-                gt_v[i] = (g_mid[i] + norm_back(grad * gain_one, normed, inverse)).astype(BF16)
+                tok_v[i] = (g_mid[i] + norm_back(grad * gain_one, normed, inverse)).astype(BF16)
                 result(i).start()
                 for turn, actions in enumerate((
-                    (lambda: stage_b(3), lambda: hop_step(2, 0, 1), lambda: hop_step(2, 1, 1)),
-                    (lambda: stage_c(3), lambda: collect(1, 0), lambda: collect(1, 1),
-                     lambda: hop_step(2, 0, 2), lambda: hop_step(2, 1, 2)),
-                    (lambda: stage_d(3), lambda: finish(2, 0), lambda: finish(2, 1), lambda: hop_step(3, 0, 0)),
-                    (lambda: stage_e(3), lambda: hop_step(3, 1, 0), lambda: hop_step(3, 0, 1)),
-                    (lambda: hop_step(3, 1, 1), lambda: hop_step(3, 0, 2)),
+                    (lambda: stage_b(3), lambda: collect(1, 0), lambda: collect(1, 1)),
+                    (lambda: stage_c(3), lambda: hop_step(2, 0, 2), lambda: hop_step(2, 1, 2)),
+                    (lambda: stage_d(3),),
+                    (lambda: stage_e(3), lambda: finish(2, 0), lambda: finish(2, 1),
+                     lambda: hop_step(3, 0, 0), lambda: hop_step(3, 1, 0)),
                 )):
                     @pl.when(i == turn)
                     def _():
@@ -985,12 +992,14 @@
             v_stage[0] = v_sum[...]
             v_move(0, mate).start()
             for p in range(3):
-                scatter_part(p, low_tv, lambda i: dqkv[i, :, p * D : (p + 1) * D])
+                scatter_part(p, low_tv, lambda i: qkv_v[i, :, p * D : (p + 1) * D])
             tail = {
-                0: (lambda: hop_step(3, 1, 2), block_output),
-                1: (lambda: finish(3, 0),),
-                2: (lambda: finish(3, 1),),
+                0: (lambda: hop_step(3, 0, 2), lambda: hop_step(3, 1, 2)),
+                1: (block_output,),
+                2: (lambda: finish(3, 0), lambda: finish(3, 1)),
             }
+            hop_step(3, 0, 1)
+            hop_step(3, 1, 1)
             for n, stage in enumerate((stage_b, stage_c, stage_d)):
                 for p in range(3):
                     stage(p)
@@ -1028,25 +1037,14 @@
 
             for p in (3, 0, 1, 2):
                 settle(p)
-            for p in range(4):
-                columns = pl.ds(p * D, D)
-                new = adam_update(
-                    old_v[0, :, columns], old_v[1, :, columns], old_v[2, :, columns], whole[:, columns],
-                    0.03, 0.1,
-                )
-                for n in range(3):
-                    old_v[n, :, columns] = new[n]
-            results = [
-                pltpu.make_async_copy(old_v.at[n], target, in_sem.at[n])
-                for n, target in enumerate((attn_new, first_new, second_new))
-            ]
-            for copy in results:
-                copy.start()
-            for copy in results:
-                copy.wait()
+            copy = pltpu.make_async_copy(whole, attn_grad, in_sem.at[0])
+            copy.start()
+            copy.wait()
             for i in range(images):
                 result(i).wait()
             pltpu.make_async_copy(g_low, mixed, in_sem.at[5]).wait()
+            for k in range(2):
+                to_result(local - 1, k).wait()
 
         pl.run_scoped(
             through_attention,
@@ -1054,14 +1052,11 @@
             pltpu.VMEM((images, PAD, 3 * D), BF16),
             pltpu.VMEM((images, D, PAD), BF16),
             pltpu.VMEM((images, D, PAD), BF16),
-            pltpu.VMEM((images, PAD, 3 * D), BF16),
             pltpu.VMEM((4, shards, rows, D), BF16),
             pltpu.VMEM((4, shards, half, D), BF16),
             pltpu.VMEM((4, lines, COLUMNS, quarter, D), BF16),
             pltpu.VMEM((4, lines, quarter, D), BF16),
             pltpu.VMEM((4, lines, quarter, D), F32),
-            pltpu.VMEM((images, PAD, D), BF16),
-            pltpu.VMEM((3, rows, 4 * D), F32),
             pltpu.VMEM((count_rows, D), BF16),
         )
 
@@ -1070,19 +1065,17 @@
         pltpu.VMEM((images, PAD, D), BF16),
         pltpu.VMEM((images, PAD, D), F32),
         pltpu.VMEM((images, PAD, D), BF16),
-    )
-
-    to_mate.wait_send()
+        pltpu.VMEM((shards, rows, 4 * D), BF16),
+    )
+
     for e in range(local):
         settle_weights(e)
         if e not in SUM_FIRST:
             for k in range(2):
                 cross_sum(e, k).wait_send()
-    for k in range(2):
-        to_result(3, k).wait()
-
-
-def block(shards, capacity, route, comb, attn, tok, cot, expw, attn_state, vec_state, group):
+
+
+def block(shards, capacity, route, comb, attn, tok, cot, expw, vec_state, group):
     lines = shards // COLUMNS
     images = tok.shape[0]
     local, _, rows, ff = expw.shape
@@ -1096,7 +1089,6 @@
     hbm = pl.BlockSpec(memory_space=pl.ANY)
     shape = jax.ShapeDtypeStruct
     states = [shape(a.shape, F32) for a in vec_state]
-    attn_states = [shape(a.shape, F32) for a in attn_state]
     last = lines - 1
     outs = pl.pallas_call(
         functools.partial(block_kernel, shards, lines, slots),
@@ -1108,22 +1100,23 @@
             shape((images, PAD, 3 * D), BF16),
             shape((images, D, PAD), BF16),
             shape((images, D, PAD), BF16),
+            shape((shards,) + attn.shape, BF16),
             shape((count_rows, D), F32),
             shape((count_rows, D), BF16),
             shape((count_rows, D), BF16),
             shape((count_rows, D), BF16),
             shape((4, count_rows, D), BF16),
             shape((3, count_rows, D), BF16),
-            shape((local, 2, rows, ff), F32),
+            shape((rows, 2, local, ff), F32),
             shape((images, PAD, D), BF16),
             shape((images, PAD, D), BF16),
-        ] + attn_states,
-        in_specs=[vm] * 6 + [hbm] * 6,
-        out_specs=[vm] * 3 + [hbm] * 19,
+            shape(attn.shape, F32),
+        ],
+        in_specs=[vm] * 5 + [hbm] * 4,
+        out_specs=[vm] * 3 + [hbm] * 18,
         scratch_shapes=[
             pltpu.VMEM(attn.shape, BF16),
             pltpu.VMEM((8, 128), F32),
-            pltpu.VMEM((shards,) + attn.shape, BF16),
             pltpu.VMEM((group, 8, wide), jnp.int32),
             pltpu.VMEM((group, 8, wide), F32),
             pltpu.VMEM((shards, 8, 128), F32),
@@ -1162,9 +1155,9 @@
         compiler_params=pltpu.CompilerParams(
             collective_id=0, has_side_effects=True, vmem_limit_bytes=VMEM_LIMIT
         ),
-    )(route, comb, attn, *vec_state, tok, cot, expw, *attn_state)
-    vec_new, grads, mixed, grad_tok, attn_new = outs[:3], outs[16], outs[17], outs[18], outs[19:]
-    return mixed, grad_tok, grads, attn_new, vec_new
+    )(route, comb, *vec_state, tok, cot, expw, attn)
+    grads, mixed, grad_tok, attn_grad = outs[17:]
+    return mixed, grad_tok, grads, attn_grad, outs[:3]
 
 
 def by_image(rows):
@@ -1192,13 +1185,13 @@
         experts = expert_master.shape[2] * group
         capacity = max(2, 4 * count // experts)
         shard = jnp.transpose(expert_master.astype(BF16), (2, 1, 0, 3))
-        mixed, grad_tokens, grads, attn_new, vec_new = block(
+        mixed, grad_tokens, grads, attn_grad, vec_new = block(
             shards, capacity, as_lanes(routes, -1), as_lanes(combine, 0.0), attn_master,
             by_image(tokens), by_image(cotangent), shard,
-            [attn_master, attn_first, attn_second], [vector_master, vector_first, vector_second], group,
+            [vector_master, vector_first, vector_second], group,
         )
-        gradient = with_layout_constraint(jnp.transpose(grads, (2, 1, 0, 3)), Layout((0, 1, 2, 3)))
-        expert_new = adam_update(expert_master, expert_first, expert_second, gradient, 0.02, 0.1)
+        attn_new = adam_update(attn_master, attn_first, attn_second, attn_grad, 0.03, 0.1)
+        expert_new = adam_update(expert_master, expert_first, expert_second, grads, 0.02, 0.1)
         return (to_tokens(mixed, count), to_tokens(grad_tokens, count), *attn_new, *vec_new, *expert_new)
 
     return run

time: 421 us -> 421 us (level)
    unnamed x27 -> x22, local copies, waits for them, and re-layouts: 11.2 us -> 8.83 us
    sub x1 -> x2, other arithmetic: 16.3 us -> 16.7 us  [adam_update(): master - step_rate * (first_hat / (jnp.sqrt(second_hat) + ADAM_EPS) + dec...]
where the time goes in v4:
time: 421 us; the launch traced here: 413 us
  Pallas kernels  377 us (90%)
  local copies, waits for them, and re-layouts  18.6 us (4%)
  other arithmetic  16.7 us (4%)
    pallas_call x1, Pallas kernels, block(): pl.pallas_call(functools.partial(block_kernel, shards, lines, slots), out...  377 us
    sub x2, other arithmetic, adam_update(): master - step_rate * (first_hat / (jnp.sqrt(second_hat) + ADAM_EPS) + dec...  16.7 us
    unnamed x22, local copies, waits for them, and re-layouts  8.83 us

profile of v4, /device:TPU:0, one launch (start us, length us, event | category | flops | bytes accessed | tf_op | source)
XLA Modules:
  0.0 413.3 jit_solution(17397289393516714774)
XLA Ops:
  0.6 0.0 copy-start.1
  0.7 0.9 reshape.46
  1.5 0.8 reshape.48
  2.3 0.6 copy.30
  2.9 0.6 copy.29
  3.6 1.5 reshape.50
  5.1 1.2 pad.17.tok
  6.3 0.0 copy-done.1
  6.3 0.3 reshape.51
  6.5 1.2 pad.18.cot
  7.7 5.7 %copy.34 = bf16[64,2,4,2048]{3,0,1,2:T(8,128)(2,1)} copy(f32[64,2,4,2048]{3,2,1,0:T(4,128)} %param.23) | data formatting | bytes 6291456 | tf_op args[10]
  13.5 376.8 %shard_map.212 = (f32[5,64]{1,0:T(8,128)}, f32[5,64]{1,0:T(8,128)}, f32[5,64]{1,0:T(8,128)}, bf16[4,5,208,512]{3,2,1,0:T(8,128)(2,1)}, bf16[4,5,208,512]{3,2,1,0...) custom-call(s32[8,1280]{1,0:T(8,128)} %bitcast.13, ...), custom_call_target="tpu_custom_call" | custom-call | tf_op jit(solution)/shard_map/pallas_call | solution.py:1093
  390.3 0.0 copy-start.2
  390.3 0.0 copy-start
  390.3 0.0 copy-start.3
  390.3 1.4 slice.6
  391.7 1.2 reshape.52
  393.0 0.1 slice.7
  393.1 1.2 reshape.53
  394.3 2.6 multiply_subtract_fusion.1
  396.9 14.1 %multiply_subtract_fusion = (f32[64,2,4,2048]{3,2,1,0:T(4,128)}, f32[64,2,4,2048]{3,2,1,0:T(4,128)}, f32[64,2,4,2048]{3,2,1,0:T(4,128)}) fusion(f32[64,2,4,2048]{3,2,1,0:T(4,128)} %param.23, f32[64,2,4,2048]{3,2,1,0:T(4,128)} %get-tuple-element.24, f32[64,2,4,2048]{3,2,1,0:T(4,128)} %param.24, f32[64,2,4,2048]{3,2,1,0:T(4,128)} %param.25), kind=kLoop, calls=%fused_computation.3 | loop fusion | flops 15728640 | bytes 29360128 | tf_op jit(solution)/shard_map/sub | solution.py:106
  411.1 0.6 copy.38
  411.7 0.6 copy.39
  412.3 0.6 copy.40
  (11 shorter events, 0.0 us)
Async XLA Ops:
  0.6 5.6 %copy-start.1 = (bf16[985,512]{1,0:T(8,128)(2,1)S(1)}, bf16[985,512]{1,0:T(8,128)(2,1)}, u32[]{:S(2)}) copy-start(bf16[985,512]{1,0:T(8,128)(2,1)} %param.14) | copy-start | bytes 3025924
  390.3 2.7 copy-start.2
  390.3 4.0 copy-start
  390.3 4.0 copy-start.3
  396.9 14.1 %copy-start.6 = (f32[5,64]{1,0:T(8,128)S(1)}, f32[5,64]{1,0:T(8,128)}, u32[]{:S(2)}) copy-start(f32[5,64]{1,0:T(8,128)} %get-tuple-element.47) | copy-start | bytes 3844
  396.9 14.7 %copy-start.5 = (f32[5,64]{1,0:T(8,128)S(1)}, f32[5,64]{1,0:T(8,128)}, u32[]{:S(2)}) copy-start(f32[5,64]{1,0:T(8,128)} %get-tuple-element.48) | copy-start | bytes 3844
  396.9 15.3 %copy-start.4 = (f32[5,64]{1,0:T(8,128)S(1)}, f32[5,64]{1,0:T(8,128)}, u32[]{:S(2)}) copy-start(f32[5,64]{1,0:T(8,128)} %get-tuple-element.49) | copy-start | bytes 3844
